TPU v7x, 256 devices: a whole 4x4x8 slice. The times are simulated.
256 devices in a mesh: row: 8 (over y, z_lo), col: 32 (over z_hi, x, core).
Axes of the slice: x: 4, y: 4, z: 8 (z_hi: 4, z_lo: 2; z = z_hi * 2 + z_lo), core: 2. Of those that a mesh axis runs over, the one named last changes fastest.
Arguments:
- object_field: float32 [2, 2048, 8192], P(None, 'row', 'col'), may hold values from -6 to 6
- probe_field: float32 [2, 256, 256], replicated, may hold values from -4.2 to 4.2
- amplitudes: bfloat16 [8, 32, 6, 256, 256], P('row', 'col'), may hold values from 0 to 2
- offsets: int32 [8, 32, 6, 2], P('row', 'col'), may hold values from 0 to 256
- counts: int32 [8, 32], P('row', 'col'), may hold values from 2 to 6
Outputs:
- updated_object: float32 [2, 2048, 8192], P(None, 'row', 'col')
Inputs may be any that keep to these rules, and one draw needn't show every extreme that they name: Tile (r, c) uses slots 0 to counts[r, c] - 1; offsets and amplitudes of the other slots are ignored.
All inputs are finite; a program needn't handle non-finite values.
Results may differ from a plain program's by a relative error of at most 0.0021.
Values sent between devices are 32-bit elements; how exact they have to be, the bound alone decides.
No kernel may reach another device: no remote copies, remote signals or barrier semaphores. Data moves between devices by JAX's collectives and lax.ppermute only.
A program may use at most 64 MiB of HBM per device.

v0:
```python
import math

import jax
import jax.numpy as jnp
from jax import lax
from jax.sharding import PartitionSpec as P

TILE = 256
RIM = 128
MAXPOS = 6
TROW = 1
TCOL = 1
ITERS = 2


smooth_term = 0.25
step_size = 0.5
regular_term = 1.0


def passed_along(value, axis, steps):
    count = lax.axis_size(axis)
    leading, last = (max(0, -steps), min(count, count - steps))
    return lax.ppermute(value, axis, [(source, source + steps) for source in range(leading, last)])


def extended_2(cells, sides, width):
    for axis, dim in sides:
        count = lax.axis_size(axis)
        ends = count - 1
        head = lax.slice_in_dim(cells, 0, width, axis=dim)
        tail = lax.slice_in_dim(cells, cells.shape[dim] - width, cells.shape[dim], axis=dim)
        cells = jnp.concatenate(
            [
                lax.ppermute(tail, axis, [(i, (i + 1) % count) for i in range(ends)]),
                cells,
                lax.ppermute(head, axis, [((i + 1) % count, i) for i in range(ends)]),
            ],
            axis=dim,
        )
    return cells


def dft_table(length):
    positions = jnp.arange(length, dtype=jnp.int32)
    phase_step = positions[:, None] * positions[None, :] % length
    phase_angle = phase_step.astype(jnp.float32) * (2.0 * math.pi / length)
    norm_scale = 1.0 / math.sqrt(length)
    cosine = jnp.cos(phase_angle) * norm_scale
    sine_part = jnp.sin(phase_angle) * norm_scale
    return jnp.stack([jnp.stack([cosine, sine_part]), jnp.stack([-sine_part, cosine])]).astype(
        jnp.bfloat16
    )


def transform(field, matrices, inverse):
    if inverse:
        first_form = "pqab,spbc->sqac"
        second_form = "spab,pqbc->sqac"
    else:
        first_form = "qpab,spbc->sqac"
        second_form = "spab,qpbc->sqac"
    half_done = jnp.einsum(first_form, matrices, field, preferred_element_type=jnp.float32).astype(
        jnp.bfloat16
    )
    return jnp.einsum(second_form, half_done, matrices, preferred_element_type=jnp.float32)


def patch_gradients(patches, probe_field, amplitudes, in_use, matrices):
    probe_real = probe_field[0]
    probe_imag = probe_field[1]
    object_real = patches[:, 0]
    object_imag = patches[:, 1]
    exit_wave = jnp.stack(
        [
            probe_real * object_real - probe_imag * object_imag,
            probe_real * object_imag + probe_imag * object_real,
        ],
        axis=1,
    ).astype(jnp.bfloat16)
    spectrum = transform(exit_wave, matrices, False)
    modulus = jnp.sqrt(
        spectrum[:, 0] * spectrum[:, 0] + spectrum[:, 1] * spectrum[:, 1] + smooth_term
    )
    factor = (1.0 - amplitudes.astype(jnp.float32) / modulus) * in_use[:, None, None]
    residual = (spectrum * factor[:, None]).astype(jnp.bfloat16)
    back_wave = transform(residual, matrices, True)
    return jnp.stack(
        [
            probe_real * back_wave[:, 0] + probe_imag * back_wave[:, 1],
            probe_real * back_wave[:, 1] - probe_imag * back_wave[:, 0],
        ],
        axis=1,
    )


def place_slots(pieces, row_starts, col_starts):
    lead_shape = pieces.shape[1:-2]
    canvas = jnp.zeros(lead_shape + (2 * TILE, 2 * TILE), jnp.float32)
    lead_zeros = tuple((jnp.zeros((), jnp.int32) for dim_size in lead_shape))

    def add_one(slot, inner):
        where_to = lead_zeros + (row_starts[slot], col_starts[slot])
        window = lax.dynamic_slice(inner, where_to, lead_shape + (TILE, TILE))
        return lax.dynamic_update_slice(inner, window + pieces[slot], where_to)

    return lax.fori_loop(0, MAXPOS, add_one, canvas)


def fold_cols(field):
    inner = field[:, :, RIM:-RIM]
    from_right = passed_along(field[:, :, :RIM], "col", -1)
    from_left = passed_along(field[:, :, -RIM:], "col", 1)
    inner = inner.at[:, :, -RIM:].add(from_right)
    return inner.at[:, :, :RIM].add(from_left)


def fold_rows(field):
    inner = field[:, RIM:-RIM, :]
    from_below = passed_along(field[:, :RIM, :], "row", -1)
    from_above = passed_along(field[:, -RIM:, :], "row", 1)
    inner = inner.at[:, -RIM:, :].add(from_below)
    return inner.at[:, :RIM, :].add(from_above)


def per_device(object_field, probe_field, amplitudes, offsets, counts):
    matrices = dft_table(TILE)
    slot_total = TROW * TCOL * MAXPOS
    zero_index = jnp.zeros((), jnp.int32)
    probe_power = probe_field[0] * probe_field[0] + probe_field[1] * probe_field[1]
    slot_index = jnp.arange(MAXPOS, dtype=jnp.int32)
    meta_block = jnp.concatenate(
        [offsets.reshape(TROW, TCOL, 2 * MAXPOS), counts.reshape(TROW, TCOL, 1)], axis=2
    )
    near_meta = extended_2(meta_block, (("row", 0), ("col", 1)), 1)
    light_grid = jnp.zeros(((TROW + 3) * TILE, (TCOL + 3) * TILE), jnp.float32)
    for near_row in range(TROW + 2):
        for near_col in range(TCOL + 2):
            entry = near_meta[near_row, near_col]
            slot_offsets = entry[: 2 * MAXPOS].reshape(MAXPOS, 2)
            weight = (slot_index < entry[2 * MAXPOS]).astype(jnp.float32)
            light_pieces = probe_power[None] * weight[:, None, None]
            canvas = place_slots(light_pieces, slot_offsets[:, 0], slot_offsets[:, 1])
            light_grid = light_grid.at[
                near_row * TILE : near_row * TILE + 2 * TILE,
                near_col * TILE : near_col * TILE + 2 * TILE,
            ].add(canvas)
    illumination = light_grid[
        TILE + RIM : TILE + RIM + TROW * TILE, TILE + RIM : TILE + RIM + TCOL * TILE
    ]
    flat_offsets = offsets.reshape(slot_total, 2)
    in_use = (
        (slot_index[None, None, :] < counts[:, :, None]).reshape(slot_total).astype(jnp.float32)
    )
    slot_ids = jnp.arange(slot_total, dtype=jnp.int32)
    own_row = slot_ids // (TCOL * MAXPOS)
    own_col = slot_ids // MAXPOS % TCOL
    top_rows = own_row * TILE + flat_offsets[:, 0]
    left_cols = own_col * TILE + flat_offsets[:, 1]
    flat_amps = amplitudes.reshape(slot_total, TILE, TILE)
    for iteration in range(ITERS):
        extended = extended_2(object_field, (("row", 1), ("col", 2)), RIM)

        def cut_patch(top_row, left_col):
            return lax.dynamic_slice(extended, (zero_index, top_row, left_col), (2, TILE, TILE))

        patches = jax.vmap(cut_patch)(top_rows, left_cols)
        pieces = patch_gradients(patches, probe_field, flat_amps, in_use, matrices)
        tile_pieces = pieces.reshape(TROW, TCOL, MAXPOS, 2, TILE, TILE)
        grad_grid = jnp.zeros((2, TROW * TILE + 2 * RIM, TCOL * TILE + 2 * RIM), jnp.float32)
        canvas = place_slots(tile_pieces[0, 0], offsets[0, 0, :, 0], offsets[0, 0, :, 1])
        grad_grid = grad_grid.at[:, 0 : 2 * TILE, 0 : 2 * TILE].add(canvas)
        gradient = fold_rows(fold_cols(grad_grid))
        object_field = object_field - step_size * gradient / (illumination + regular_term)
    return object_field


def solution(mesh):
    in_specs = (
        P(None, "row", "col"),
        P(),
        P("row", "col", None, None, None),
        P("row", "col", None, None),
        P("row", "col"),
    )
    out_specs = P(None, "row", "col")
    return jax.shard_map(
        per_device, mesh=mesh, in_specs=in_specs, out_specs=out_specs, check_vma=False
    )
```

profile of v0, /device:TPU:87, one launch (start us, length us, event | category | flops | bytes accessed | tf_op | source)
XLA Modules:
  0.0 1053.1 jit_solution(11833854883907700129)
XLA Ops:
  48.2 56.4 %while.167 = (s32[]{:T(128)}, f32[512,512]{1,0:T(8,128)S(1)}, s32[6]{0:T(128)S(1)}, s32[6]{0:T(128)S(1)}, f32[6,256,256]{2,1,0:T(8,128)S(1)}, /*index=5*/s32[]{:T(128)}, s32[]{:T(128)}, s32[]{:T(128)}) while((s32[]{:T(128)}, f32[512,512]{1,0:T(8,128)S(1)}, s32[6]{0:T(128)S(1)}, s32[6]{0:T(128)S(1)}, f32[6,256,256]{2,1,0:T(8,128)S(1)}, ...), condition=%wide.region_3.4_spmd, body=%wide.region_2.3_spmd.sunk | while | flops 65544 | bytes 1310913 | solution.py:107
  104.7 65.7 %while.168 = (s32[]{:T(128)}, f32[512,512]{1,0:T(8,128)S(1)}, s32[6]{0:T(128)S(1)}, s32[6]{0:T(128)S(1)}, f32[6,256,256]{2,1,0:T(8,128)}, /*index=5*/s32[]{:T(128)}, s32[]{:T(128)}, s32[]{:T(128)}) while((s32[]{:T(128)}, f32[512,512]{1,0:T(8,128)S(1)}, s32[6]{0:T(128)S(1)}, s32[6]{0:T(128)S(1)}, f32[6,256,256]{2,1,0:T(8,128)}, ...), condition=%wide.region_6.7_spmd, body=%wide.region_5.6_spmd.sunk | while | flops 65544 | bytes 1310913 | solution.py:107
  170.8 62.0 %while.169 = (s32[]{:T(128)}, f32[512,512]{1,0:T(8,128)S(1)}, s32[6]{0:T(128)S(1)}, s32[6]{0:T(128)S(1)}, f32[6,256,256]{2,1,0:T(8,128)}, /*index=5*/s32[]{:T(128)}, s32[]{:T(128)}, s32[]{:T(128)}) while((s32[]{:T(128)}, f32[512,512]{1,0:T(8,128)S(1)}, s32[6]{0:T(128)S(1)}, s32[6]{0:T(128)S(1)}, f32[6,256,256]{2,1,0:T(8,128)}, ...), condition=%wide.region_9.10_spmd, body=%wide.region_8.9_spmd.sunk | while | flops 65544 | bytes 1310913 | solution.py:107
  238.5 8.4 scatter-add.65
  250.5 7.7 scatter-add.66
  258.5 64.4 %while.170 = (s32[]{:T(128)}, f32[512,512]{1,0:T(8,128)S(1)}, s32[6]{0:T(128)S(1)}, s32[6]{0:T(128)S(1)}, f32[6,256,256]{2,1,0:T(8,128)}, /*index=5*/s32[]{:T(128)}, s32[]{:T(128)}, s32[]{:T(128)}) while((s32[]{:T(128)}, f32[512,512]{1,0:T(8,128)S(1)}, s32[6]{0:T(128)S(1)}, s32[6]{0:T(128)S(1)}, f32[6,256,256]{2,1,0:T(8,128)}, ...), condition=%wide.region_11.12_spmd, body=%wide.region_10.11_spmd.sunk | while | flops 65544 | bytes 1310913 | solution.py:107
  323.0 62.5 %while.171 = (s32[]{:T(128)}, f32[512,512]{1,0:T(8,128)S(1)}, s32[6]{0:T(128)S(1)}, s32[6]{0:T(128)S(1)}, f32[6,256,256]{2,1,0:T(8,128)}, /*index=5*/s32[]{:T(128)}, s32[]{:T(128)}, s32[]{:T(128)}) while((s32[]{:T(128)}, f32[512,512]{1,0:T(8,128)S(1)}, s32[6]{0:T(128)S(1)}, s32[6]{0:T(128)S(1)}, f32[6,256,256]{2,1,0:T(8,128)}, ...), condition=%wide.region_13.14_spmd, body=%wide.region_12.13_spmd.sunk | while | flops 65544 | bytes 1310913 | solution.py:107
  385.9 63.1 %while.172 = (s32[]{:T(128)}, f32[512,512]{1,0:T(8,128)S(1)}, s32[6]{0:T(128)S(1)}, s32[6]{0:T(128)S(1)}, f32[6,256,256]{2,1,0:T(8,128)}, /*index=5*/s32[]{:T(128)}, s32[]{:T(128)}, s32[]{:T(128)}) while((s32[]{:T(128)}, f32[512,512]{1,0:T(8,128)S(1)}, s32[6]{0:T(128)S(1)}, s32[6]{0:T(128)S(1)}, f32[6,256,256]{2,1,0:T(8,128)}, ...), condition=%wide.region_15.16_spmd, body=%wide.region_14.15_spmd.sunk | while | flops 65544 | bytes 1310913 | solution.py:107
  450.4 59.7 %while.173 = (s32[]{:T(128)}, f32[512,512]{1,0:T(8,128)}, s32[6]{0:T(128)S(1)}, s32[6]{0:T(128)S(1)}, f32[6,256,256]{2,1,0:T(8,128)}, /*index=5*/s32[]{:T(128)}, s32[]{:T(128)}, s32[]{:T(128)}) while((s32[]{:T(128)}, f32[512,512]{1,0:T(8,128)}, s32[6]{0:T(128)S(1)}, s32[6]{0:T(128)S(1)}, f32[6,256,256]{2,1,0:T(8,128)}, ...), condition=%wide.region_17.18_spmd, body=%wide.region_16.17_spmd.sunk | while | flops 65544 | bytes 1310913 | solution.py:107
  511.3 62.1 %while.174 = (s32[]{:T(128)}, f32[512,512]{1,0:T(8,128)}, s32[6]{0:T(128)S(1)}, s32[6]{0:T(128)S(1)}, f32[6,256,256]{2,1,0:T(8,128)}, /*index=5*/s32[]{:T(128)}, s32[]{:T(128)}, s32[]{:T(128)}) while((s32[]{:T(128)}, f32[512,512]{1,0:T(8,128)}, s32[6]{0:T(128)S(1)}, s32[6]{0:T(128)S(1)}, f32[6,256,256]{2,1,0:T(8,128)}, ...), condition=%wide.region_19.20_spmd, body=%wide.region_18.19_spmd.sunk | while | flops 65544 | bytes 1310913 | solution.py:107
  583.9 8.6 collective-permute-start.2
  594.8 64.8 %while.175 = (s32[]{:T(128)}, f32[512,512]{1,0:T(8,128)S(1)}, s32[6]{0:T(128)S(1)}, s32[6]{0:T(128)S(1)}, f32[6,256,256]{2,1,0:T(8,128)}, /*index=5*/s32[]{:T(128)}, s32[]{:T(128)}, s32[]{:T(128)}) while((s32[]{:T(128)}, f32[512,512]{1,0:T(8,128)S(1)}, s32[6]{0:T(128)S(1)}, s32[6]{0:T(128)S(1)}, f32[6,256,256]{2,1,0:T(8,128)}, ...), condition=%wide.region_21.22_spmd, body=%wide.region_20.21_spmd.sunk | while | flops 65544 | bytes 1310913 | solution.py:107
  664.8 26.0 %while.177 = (s32[]{:T(128)}, f32[2,512,512]{2,1,0:T(8,128)}, s32[6,3]{0,1:T(4,128)S(1)}, f32[6,2,256,256]{2,3,0,1:T(8,128)}, s32[]{:T(128)}) while((s32[]{:T(128)}, f32[2,512,512]{2,1,0:T(8,128)}, s32[6,3]{0,1:T(4,128)S(1)}, f32[6,2,256,256]{2,3,0,1:T(8,128)}, s32[]{:T(128)}) %tuple.423), condition=%wide.while_cond.19, body=%wide.while_body.19.sunk | while | flops 2 | bytes 3146353 | solution.py:165
  709.0 92.2 %while.166 = (s32[]{:T(128)}, f32[2,512,512]{2,1,0:T(8,128)S(1)}, s32[6]{0:T(128)S(1)}, s32[6]{0:T(128)S(1)}, f32[6,2,256,256]{2,3,0,1:T(8,128)}, /*index=5*/s32[]{:T(128)}, s32[]{:T(128)}, s32[]{:T(128)}) while((s32[]{:T(128)}, f32[2,512,512]{2,1,0:T(8,128)S(1)}, s32[6]{0:T(128)S(1)}, s32[6]{0:T(128)S(1)}, f32[6,2,256,256]{2,3,0,1:T(8,128)}, ...), condition=%wide.region_1.2_spmd, body=%wide.region_0.1_spmd.sunk | while | flops 131080 | bytes 4718785 | solution.py:107
  715.6 7.3 dynamic_update_slice.88
  729.5 8.4 dynamic_update_slice.88
  744.5 9.8 dynamic_update_slice.88
  760.9 9.8 dynamic_update_slice.88
  777.4 10.4 dynamic_update_slice.88
  806.0 7.9 collective-permute-start.5
  833.0 10.6 %collective-permute-done.7 = f32[2,128,256]{2,1,0:T(8,128)S(1)} collective-permute-done((f32[2,128,256]{2,1,0:T(8,128)S(1)}, f32[2,128,256]{2,1,0:T(8,128)S(1)}, u32[]{:S(2)}, u32[]{:S(2)}) %collective-permute-start.7) | collective-permute-done | bytes 262176 | tf_op jit(solution)/shard_map/ppermute | solution.py:24
  853.6 9.3 collective-permute-start.14
  869.8 13.5 %collective-permute-done.15 = f32[2,512,128]{2,1,0:T(8,128)} collective-permute-done((f32[2,512,128]{2,1,0:T(8,128)S(1)}, f32[2,512,128]{2,1,0:T(8,128)}, u32[]{:S(2)}, u32[]{:S(2)}) %collective-permute-start.15) | collective-permute-done | bytes 524320 | tf_op jit(solution)/shard_map/ppermute | solution.py:37
  886.7 19.1 %while.178 = (s32[]{:T(128)}, f32[2,512,512]{2,1,0:T(8,128)S(1)}, s32[6,3]{0,1:T(4,128)S(1)}, f32[6,2,256,256]{2,3,0,1:T(8,128)}, s32[]{:T(128)}) while((s32[]{:T(128)}, f32[2,512,512]{2,1,0:T(8,128)S(1)}, s32[6,3]{0,1:T(4,128)S(1)}, f32[6,2,256,256]{2,3,0,1:T(8,128)}, s32[]{:T(128)}) %tuple.462), condition=%wide.while_cond.20, body=%wide.while_body.20.sunk | while | flops 2 | bytes 3146353 | solution.py:165
  924.0 92.6 %while.176 = (s32[]{:T(128)}, f32[2,512,512]{2,1,0:T(8,128)S(1)}, s32[6]{0:T(128)S(1)}, s32[6]{0:T(128)S(1)}, f32[6,2,256,256]{2,3,0,1:T(8,128)}, /*index=5*/s32[]{:T(128)}, s32[]{:T(128)}, s32[]{:T(128)}) while((s32[]{:T(128)}, f32[2,512,512]{2,1,0:T(8,128)S(1)}, s32[6]{0:T(128)S(1)}, s32[6]{0:T(128)S(1)}, f32[6,2,256,256]{2,3,0,1:T(8,128)}, ...), condition=%wide.region_23.24_spmd, body=%wide.region_22.23_spmd.sunk | while | flops 131080 | bytes 4718785 | solution.py:107
  930.6 7.3 dynamic_update_slice.98
  944.6 8.4 dynamic_update_slice.98
  959.6 9.8 dynamic_update_slice.98
  976.1 9.8 dynamic_update_slice.98
  992.6 10.4 dynamic_update_slice.98
  1018.6 7.9 collective-permute-start.17
  1044.6 7.6 collective-permute-done.19
  (532 shorter events, 623.0 us)
Async XLA Ops:
  0.0 20.8 %copy-start.23 = (s32[1,1,6,2]{2,3,1,0:T(2,128)S(1)}, s32[1,1,6,2]{2,3,1,0:T(2,128)}, u32[]{:S(2)}) copy-start(s32[1,1,6,2]{2,3,1,0:T(2,128)} %param.72) | copy-start | bytes 148
  0.0 19.5 %copy-start.17 = (f32[2,256,256]{2,1,0:T(8,128)S(1)}, f32[2,256,256]{2,1,0:T(8,128)}, u32[]{:S(2)}) copy-start(f32[2,256,256]{2,1,0:T(8,128)} %param.70) | copy-start | bytes 1572868
  1.6 22.9 %collective-permute-start.8 = (s32[1,1,13]{2,1,0:T(1,128)S(1)}, s32[1,1,13]{2,1,0:T(1,128)S(1)}, u32[]{:S(2)}, u32[]{:S(2)}) collective-permute-start(s32[1,1,13]{2,1,0:T(1,128)S(1)} %pad_add_fusion.2), channel_id=1, source_target_pairs={{0,32},{32,64},{64,96},{96,128},{128,160},{160,192},{192,224},{1,3... | collective-permute-start | bytes 164 | tf_op jit(solution)/shard_map/ppermute | solution.py:35
  5.2 19.4 %collective-permute-start.9 = (s32[1,1,13]{2,1,0:T(1,128)S(1)}, s32[1,1,13]{2,1,0:T(1,128)S(1)}, u32[]{:S(2)}, u32[]{:S(2)}) collective-permute-start(s32[1,1,13]{2,1,0:T(1,128)S(1)} %pad_add_fusion.2), channel_id=1, source_target_pairs={{32,0},{64,32},{96,64},{128,96},{160,128},{192,160},{224,192},{33,... | collective-permute-start | bytes 164 | tf_op jit(solution)/shard_map/ppermute | solution.py:37
  9.7 571.3 %collective-permute-start = (f32[2,128,256]{2,1,0:T(8,128)}, f32[2,128,256]{2,1,0:T(8,128)}, u32[]{:S(2)}, u32[]{:S(2)}) collective-permute-start(f32[2,128,256]{2,1,0:T(8,128)} %get-tuple-element.1508), channel_id=1, source_target_pairs={{0,32},{32,64},{64,96},{96,128},{128,160},{160,192},{192,224},{1,3... | collective-permute-start | bytes 786440 | tf_op jit(solution)/shard_map/ppermute | solution.py:35
  12.3 569.7 %collective-permute-start.1 = (f32[2,128,256]{2,1,0:T(8,128)}, f32[2,128,256]{2,1,0:T(8,128)}, u32[]{:S(2)}, u32[]{:S(2)}) collective-permute-start(f32[2,128,256]{2,1,0:T(8,128)} %get-tuple-element.1507), channel_id=1, source_target_pairs={{32,0},{64,32},{96,64},{128,96},{160,128},{192,160},{224,192},{33,... | collective-permute-start | bytes 786440 | tf_op jit(solution)/shard_map/ppermute | solution.py:37
  24.7 12.8 %collective-permute-start.11 = (s32[3,1,13]{2,1,0:T(1,128)S(1)}, s32[3,1,13]{2,1,0:T(1,128)S(1)}, u32[]{:S(2)}, u32[]{:S(2)}) collective-permute-start(s32[3,1,13]{2,1,0:T(1,128)S(1)} %pad_add_fusion.1), channel_id=1, source_target_pairs={{1,0},{2,1},{3,2},{4,3},{5,4},{6,5},{7,6},{8,7},{9,8},{10,9},{11,1... | collective-permute-start | bytes 476 | tf_op jit(solution)/shard_map/ppermute | solution.py:37
  28.4 8.2 collective-permute-start.10
  583.9 75.7 %collective-permute-start.2 = (f32[2,512,128]{2,1,0:T(8,128)}, f32[2,512,128]{2,1,0:T(8,128)}, u32[]{:S(2)}, u32[]{:S(2)}) collective-permute-start(f32[2,512,128]{2,1,0:T(8,128)} %get-tuple-element.1500), channel_id=1, source_target_pairs={{0,1},{1,2},{2,3},{3,4},{4,5},{5,6},{6,7},{7,8},{8,9},{9,10},{10,1... | collective-permute-start | bytes 1572872 | tf_op jit(solution)/shard_map/ppermute | solution.py:35
  592.5 67.1 %collective-permute-start.3 = (f32[2,512,128]{2,1,0:T(8,128)S(1)}, f32[2,512,128]{2,1,0:T(8,128)}, u32[]{:S(2)}, u32[]{:S(2)}) collective-permute-start(f32[2,512,128]{2,1,0:T(8,128)S(1)} %get-tuple-element.1501), channel_id=1, source_target_pairs={{1,0},{2,1},{3,2},{4,3},{5,4},{6,5},{7,6},{8,7},{9,8},{10,9},{11,1... | collective-permute-start | bytes 1572872 | tf_op jit(solution)/shard_map/ppermute | solution.py:37
  664.8 26.0 %copy-start.9 = (f32[256,256]{0,1:T(8,128)S(1)}, f32[256,256]{0,1:T(8,128)}, u32[]{:S(2)}) copy-start(f32[256,256]{0,1:T(8,128)} %copy.18) | copy-start | bytes 786436
  664.8 26.0 %copy-start.10 = (f32[256,256]{0,1:T(8,128)S(1)}, f32[256,256]{0,1:T(8,128)}, u32[]{:S(2)}) copy-start(f32[256,256]{0,1:T(8,128)} %copy.20) | copy-start | bytes 786436
  801.4 19.8 %collective-permute-start.4 = (f32[2,512,128]{2,1,0:T(8,128)S(1)}, f32[2,512,128]{2,1,0:T(8,128)S(1)}, u32[]{:S(2)}, u32[]{:S(2)}) collective-permute-start(f32[2,512,128]{2,1,0:T(8,128)S(1)} %get-tuple-element.1493), channel_id=1, source_target_pairs={{1,0},{2,1},{3,2},{4,3},{5,4},{6,5},{7,6},{8,7},{9,8},{10,9},{11,1... | collective-permute-start | bytes 1572872 | tf_op jit(solution)/shard_map/ppermute | solution.py:24
  803.4 10.4 copy-start.4
  806.0 19.0 %collective-permute-start.5 = (f32[2,512,128]{2,1,0:T(8,128)S(1)}, f32[2,512,128]{2,1,0:T(8,128)S(1)}, u32[]{:S(2)}, u32[]{:S(2)}) collective-permute-start(f32[2,512,128]{2,1,0:T(8,128)S(1)} %get-tuple-element.1492), channel_id=1, source_target_pairs={{0,1},{1,2},{2,3},{3,4},{4,5},{5,6},{6,7},{7,8},{8,9},{9,10},{10,1... | collective-permute-start | bytes 1572872 | tf_op jit(solution)/shard_map/ppermute | solution.py:24
  816.4 10.7 %copy-start.6 = (f32[512,512]{1,0:T(8,128)S(1)}, f32[512,512]{1,0:T(8,128)}, u32[]{:S(2)}) copy-start(f32[512,512]{1,0:T(8,128)} %copy-done.5) | copy-start | bytes 3145732
  821.2 5.9 copy-start
  825.1 7.8 collective-permute-start.6
  827.4 16.3 %copy-start.13 = (f32[2,256,256]{2,1,0:T(8,128)S(1)}, f32[2,256,256]{2,1,0:T(8,128)}, u32[]{:S(2)}) copy-start(f32[2,256,256]{2,1,0:T(8,128)} %param.69) | copy-start | bytes 1572868
  827.4 16.2 %collective-permute-start.7 = (f32[2,128,256]{2,1,0:T(8,128)S(1)}, f32[2,128,256]{2,1,0:T(8,128)S(1)}, u32[]{:S(2)}, u32[]{:S(2)}) collective-permute-start(f32[2,128,256]{2,1,0:T(8,128)S(1)} %get-tuple-element.1498), channel_id=1, source_target_pairs={{0,32},{32,64},{64,96},{96,128},{128,160},{160,192},{192,224},{1,3... | collective-permute-start | bytes 786440 | tf_op jit(solution)/shard_map/ppermute | solution.py:24
  830.9 12.8 %copy-start.14 = (f32[256,256]{1,0:T(8,128)}, f32[256,256]{1,0:T(8,128)S(1)}, u32[]{:S(2)}) copy-start(f32[256,256]{1,0:T(8,128)S(1)} %slice_add_fusion.10) | copy-start | bytes 786436
  843.8 39.5 %copy-start.1 = (f32[2,256,256]{2,1,0:T(8,128)}, f32[2,256,256]{2,1,0:T(8,128)S(1)}, u32[]{:S(2)}) copy-start(f32[2,256,256]{2,1,0:T(8,128)S(1)} %divide_subtract_fusion.1) | copy-start | bytes 1572868
  843.8 8.0 collective-permute-start.12
  845.8 7.7 collective-permute-start.13
  853.6 15.5 %collective-permute-start.14 = (f32[2,512,128]{2,1,0:T(8,128)S(1)}, f32[2,512,128]{2,1,0:T(8,128)S(1)}, u32[]{:S(2)}, u32[]{:S(2)}) collective-permute-start(f32[2,512,128]{2,1,0:T(8,128)S(1)} %get-tuple-element.1496), channel_id=1, source_target_pairs={{0,1},{1,2},{2,3},{3,4},{4,5},{5,6},{6,7},{7,8},{8,9},{9,10},{10,1... | collective-permute-start | bytes 1572872 | tf_op jit(solution)/shard_map/ppermute | solution.py:35
  862.9 20.4 %collective-permute-start.15 = (f32[2,512,128]{2,1,0:T(8,128)S(1)}, f32[2,512,128]{2,1,0:T(8,128)}, u32[]{:S(2)}, u32[]{:S(2)}) collective-permute-start(f32[2,512,128]{2,1,0:T(8,128)S(1)} %get-tuple-element.1497), channel_id=1, source_target_pairs={{1,0},{2,1},{3,2},{4,3},{5,4},{6,5},{7,6},{8,7},{9,8},{10,9},{11,1... | collective-permute-start | bytes 1572872 | tf_op jit(solution)/shard_map/ppermute | solution.py:37
  1016.7 16.3 %collective-permute-start.16 = (f32[2,512,128]{2,1,0:T(8,128)S(1)}, f32[2,512,128]{2,1,0:T(8,128)S(1)}, u32[]{:S(2)}, u32[]{:S(2)}) collective-permute-start(f32[2,512,128]{2,1,0:T(8,128)S(1)} %get-tuple-element.1491), channel_id=1, source_target_pairs={{1,0},{2,1},{3,2},{4,3},{5,4},{6,5},{7,6},{8,7},{9,8},{10,9},{11,1... | collective-permute-start | bytes 1572872 | tf_op jit(solution)/shard_map/ppermute | solution.py:24
  1018.6 18.6 %collective-permute-start.17 = (f32[2,512,128]{2,1,0:T(8,128)S(1)}, f32[2,512,128]{2,1,0:T(8,128)S(1)}, u32[]{:S(2)}, u32[]{:S(2)}) collective-permute-start(f32[2,512,128]{2,1,0:T(8,128)S(1)} %get-tuple-element.1490), channel_id=1, source_target_pairs={{0,1},{1,2},{2,3},{3,4},{4,5},{5,6},{6,7},{7,8},{8,9},{9,10},{10,1... | collective-permute-start | bytes 1572872 | tf_op jit(solution)/shard_map/ppermute | solution.py:24
  1037.3 14.9 %copy-start.2 = (f32[2,256,256]{2,1,0:T(8,128)S(1)}, f32[2,256,256]{2,1,0:T(8,128)}, u32[]{:S(2)}) copy-start(f32[2,256,256]{2,1,0:T(8,128)} %copy-done.1) | copy-start | bytes 1572868
  1037.3 14.9 %copy-start.15 = (f32[256,256]{1,0:T(8,128)S(1)}, f32[256,256]{1,0:T(8,128)}, u32[]{:S(2)}) copy-start(f32[256,256]{1,0:T(8,128)} %copy-done.14) | copy-start | bytes 786436
  1037.3 7.2 collective-permute-start.18
  1039.4 12.8 %collective-permute-start.19 = (f32[2,128,256]{2,1,0:T(8,128)S(1)}, f32[2,128,256]{2,1,0:T(8,128)S(1)}, u32[]{:S(2)}, u32[]{:S(2)}) collective-permute-start(f32[2,128,256]{2,1,0:T(8,128)S(1)} %get-tuple-element.1494), channel_id=1, source_target_pairs={{0,32},{32,64},{64,96},{96,128},{128,160},{160,192},{192,224},{1,3... | collective-permute-start | bytes 786440 | tf_op jit(solution)/shard_map/ppermute | solution.py:24
  (12 other events, 35.9 us)
where the time goes:
time: 1060 us; the launch traced here: 1050 us
  local copies, waits for them, and re-layouts  520 us (49%)
  loops' own time  256 us (24%)
  other arithmetic  115 us (11%)
  starting transfers between devices  81.3 us (8%)
  waiting for transfers between devices  61.7 us (6%)
  matrix products  18 us (2%)
    dynamic_update_slice x66, local copies, waits for them, and re-layouts, add_one(): return lax.dynamic_update_slice(inner, window + pieces[slot], where_to)  333 us
    another operation x11, loops' own time, place_slots(): return lax.fori_loop(0, MAXPOS, add_one, canvas)  256 us
    dynamic_slice x132, local copies, waits for them, and re-layouts, add_one(): where_to = lead_zeros + (row_starts[slot], col_starts[slot])  83.6 us
    add x66, other arithmetic, add_one(): return lax.dynamic_update_slice(inner, window + pieces[slot], where_to)  57.7 us
    gather x60, local copies, waits for them, and re-layouts  45 us
    ppermute x8, waiting for transfers between devices, passed_along(): lax.ppermute(value, axis, [(source, source + steps) for source in range(l...  40.8 us
    ppermute x6, starting transfers between devices, extended_2(): lax.ppermute(tail, axis, [(i, (i + 1) % count) for i in range(ends)])  32.3 us
    ppermute x8, starting transfers between devices, passed_along(): lax.ppermute(value, axis, [(source, source + steps) for source in range(l...  30.5 us
  transfers between devices with their start and end apart: 20, of which 12 were waited for; matrix products, arithmetic and copies ran while one was open for 40% of the time, Pallas kernels for 0%

commit v1 on v0

v1 whole, which is shorter than its diff:
```python
import functools
import math

import jax
import jax.numpy as jnp
import numpy as np
from jax import lax
from jax.experimental import pallas as pl
from jax.experimental.pallas import tpu as pltpu
from jax.sharding import PartitionSpec as P

TILE = 256
RIM = 128
MAXPOS = 6
EXT = TILE + 2 * RIM
LANES = 128
META = 16

smooth_term = 0.25
step_size = 0.5
regular_term = 1.0

VMEM = pl.BlockSpec(memory_space=pltpu.VMEM)
SMEM = pl.BlockSpec(memory_space=pltpu.SMEM)
PARAMS = pltpu.CompilerParams(vmem_limit_bytes=40 * 1024 * 1024)


def dft_tables():
    index = np.arange(TILE)
    angle = (index[:, None] * index[None, :] % TILE) * (2.0 * math.pi / TILE)
    cosine = np.cos(angle) / math.sqrt(TILE)
    sine = -np.sin(angle) / math.sqrt(TILE)
    ahead = np.block([[cosine, -sine], [sine, cosine]]).astype(np.float32)
    return jnp.asarray(ahead, jnp.bfloat16), jnp.asarray(ahead.T, jnp.bfloat16)


def swap(value, axis, first):
    count = lax.axis_size(axis)
    pairs = []
    for low in range(first, count - 1, 2):
        pairs += [(low, low + 1), (low + 1, low)]
    return lax.ppermute(value, axis, pairs)


def call(body, out_shapes, in_specs, scratch=(), flops=0, bytes_accessed=1 << 20, out_specs=None):
    return pl.pallas_call(
        body,
        out_shape=out_shapes,
        in_specs=in_specs,
        out_specs=out_specs if out_specs is not None else jax.tree.map(lambda _: VMEM, out_shapes),
        scratch_shapes=scratch,
        compiler_params=PARAMS,
        cost_estimate=pl.CostEstimate(flops=flops, bytes_accessed=bytes_accessed, transcendentals=0),
    )


def f32(*shape):
    return jax.ShapeDtypeStruct(shape, jnp.float32)


def aligned(value, unit):
    return pl.multiple_of(value, unit)


def pack_rows_kernel(place, obj, offs, cnt, a_out, b_out):
    parity = place[0] & 1
    a_row = aligned((1 - parity) * RIM, RIM)
    b_row = aligned(parity * RIM, RIM)
    for p in range(2):
        a_out[p * RIM : (p + 1) * RIM, :] = obj[p, pl.ds(a_row, RIM), :]
        b_out[p * RIM : (p + 1) * RIM, :] = obj[p, pl.ds(b_row, RIM), :]
    for out in (a_out, b_out):
        out[2 * RIM :, :] = jnp.zeros((8, TILE), jnp.float32)
        out[2 * RIM : 2 * RIM + 1, 0:12] = offs[...].astype(jnp.float32)
        out[2 * RIM : 2 * RIM + 1, 12:13] = cnt[...].astype(jnp.float32)


def pack_cols_kernel(place, obj, row_a, row_b, offs, cnt, center, a_out, b_out):
    row_parity = place[0] & 1
    a_at = aligned((1 - row_parity) * (RIM + TILE), RIM)
    b_at = aligned(row_parity * (RIM + TILE), RIM)
    for p in range(2):
        center[p, RIM : RIM + TILE, :] = obj[p]
        center[p, pl.ds(a_at, RIM), :] = row_a[p * RIM : (p + 1) * RIM, :]
        center[p, pl.ds(b_at, RIM), :] = row_b[p * RIM : (p + 1) * RIM, :]
    even = (place[1] & 1) == 0
    for p in range(2):
        low = center[p, :, 0:LANES]
        high = center[p, :, LANES:TILE]
        a_out[p * EXT : (p + 1) * EXT, :] = jnp.where(even, high, low)
        b_out[p * EXT : (p + 1) * EXT, :] = jnp.where(even, low, high)
    meta_a = row_a[2 * RIM : 2 * RIM + 1, 0:LANES]
    meta_b = row_b[2 * RIM : 2 * RIM + 1, 0:LANES]
    odd_row = row_parity == 1
    for out in (a_out, b_out):
        out[2 * EXT :, :] = jnp.zeros((8, LANES), jnp.float32)
        out[2 * EXT : 2 * EXT + 1, :] = jnp.where(odd_row, meta_a, meta_b)
        out[2 * EXT + 1 : 2 * EXT + 2, 0:12] = offs[...].astype(jnp.float32)
        out[2 * EXT + 1 : 2 * EXT + 2, 12:13] = cnt[...].astype(jnp.float32)
        out[2 * EXT + 2 : 2 * EXT + 3, :] = jnp.where(odd_row, meta_b, meta_a)


def light_kernel(metas, probe, out, canvas, padded):
    power = probe[0] * probe[0] + probe[1] * probe[1]
    padded[...] = jnp.zeros_like(padded)
    for b in range(2):
        padded[b + 1] = power[:, b * LANES : (b + 1) * LANES]
    canvas[...] = jnp.zeros_like(canvas)
    lane = lax.broadcasted_iota(jnp.int32, (TILE, LANES), 1)

    def add(index, carry):
        near = index // MAXPOS
        slot = index - near * MAXPOS
        used = slot < metas[near, 2 * MAXPOS]
        row = (near // 3) * TILE + metas[near, 2 * slot]
        col = (near % 3 - 1) * TILE - RIM + metas[near, 2 * slot + 1]
        for b in range(2):
            start = b * LANES - col

            @pl.when(used & (start > -LANES) & (start < TILE))
            def _():
                spot = start + LANES
                block = spot // LANES
                shift = spot - block * LANES
                back = (LANES - shift) & (LANES - 1)
                first = pltpu.roll(padded[block], back, 1)
                second = pltpu.roll(padded[block + 1], back, 1)
                part = jnp.where(lane < LANES - shift, first, second)
                canvas[b, pl.ds(row, TILE), :] += part

        return carry

    lax.fori_loop(0, 9 * MAXPOS, add, 0)
    for b in range(2):
        out[:, b * LANES : (b + 1) * LANES] = step_size / (
            canvas[b, TILE : TILE + EXT, :] + regular_term
        )


def iterate_kernel(
    place, offs, cnt, center, col_a, col_b, probe, amps, ahead, back, own, a_out, b_out, ext, grad, wave
):
    parity = place[1] & 1
    a_block = 3 * (1 - parity)
    b_block = 3 * parity
    for p in range(2):
        ext[p, a_block, 0:EXT, :] = col_a[p * EXT : (p + 1) * EXT, :]
        ext[p, b_block, 0:EXT, :] = col_b[p * EXT : (p + 1) * EXT, :]
        for b in range(2):
            ext[p, 1 + b, 0:EXT, :] = center[p, :, b * LANES : (b + 1) * LANES]
    grad[...] = jnp.zeros_like(grad)
    lane = lax.broadcasted_iota(jnp.int32, (TILE, LANES), 1)

    def one(slot, carry):
        row = offs[2 * slot]
        col = offs[2 * slot + 1]
        block = col // LANES
        shift = col - block * LANES
        unshift = (LANES - shift) & (LANES - 1)
        blocks = [block, block + 1, jnp.minimum(block + 2, 3)]
        keep = lane < LANES - shift
        window = []
        for p in range(2):
            turned = [pltpu.roll(ext[p, b, pl.ds(row, TILE), :], unshift, 1) for b in blocks]
            window.append([jnp.where(keep, turned[h], turned[h + 1]) for h in range(2)])
        for h in range(2):
            at = slice(h * LANES, (h + 1) * LANES)
            pr = probe[0, :, at]
            pi = probe[1, :, at]
            re = window[0][h]
            im = window[1][h]
            wave[0:TILE, at] = (pr * re - pi * im).astype(jnp.bfloat16)
            wave[TILE : 2 * TILE, at] = (pr * im + pi * re).astype(jnp.bfloat16)
        half = jnp.dot(ahead[...], wave[...], preferred_element_type=jnp.float32).astype(jnp.bfloat16)
        spectrum = jnp.dot(half[:TILE], back[0:TILE, :], preferred_element_type=jnp.float32) + jnp.dot(
            half[TILE:], back[TILE:, :], preferred_element_type=jnp.float32
        )
        sr = spectrum[:, :TILE]
        si = spectrum[:, TILE:]
        factor = 1.0 - amps[slot].astype(jnp.float32) * lax.rsqrt(sr * sr + si * si + smooth_term)
        wave[0:TILE, :] = (sr * factor).astype(jnp.bfloat16)
        wave[TILE : 2 * TILE, :] = (si * factor).astype(jnp.bfloat16)
        back_half = jnp.dot(back[...], wave[...], preferred_element_type=jnp.float32).astype(jnp.bfloat16)
        back_wave = jnp.dot(back_half[:TILE], ahead[0:TILE, :], preferred_element_type=jnp.float32) + jnp.dot(
            back_half[TILE:], ahead[TILE:, :], preferred_element_type=jnp.float32
        )
        pieces = [[], []]
        for h in range(2):
            at = slice(h * LANES, (h + 1) * LANES)
            pr = probe[0, :, at]
            pi = probe[1, :, at]
            br = back_wave[:, h * LANES : (h + 1) * LANES]
            bi = back_wave[:, TILE + h * LANES : TILE + (h + 1) * LANES]
            pieces[0].append(pltpu.roll(pr * br + pi * bi, shift, 1))
            pieces[1].append(pltpu.roll(pr * bi - pi * br, shift, 1))
        right = lane >= shift
        for p in range(2):
            h0, h1 = pieces[p]
            grad[p, blocks[0], pl.ds(row, TILE), :] += jnp.where(right, h0, 0.0)
            grad[p, blocks[1], pl.ds(row, TILE), :] += jnp.where(right, h1, h0)
            grad[p, blocks[2], pl.ds(row, TILE), :] += jnp.where(right, 0.0, h1)
        return carry

    lax.fori_loop(0, cnt[0], one, 0)
    for p in range(2):
        a_out[p * EXT : (p + 1) * EXT, :] = grad[p, a_block, 0:EXT, :]
        b_out[p * EXT : (p + 1) * EXT, :] = grad[p, b_block, 0:EXT, :]
        for b in range(2):
            own[p, :, b * LANES : (b + 1) * LANES] = grad[p, 1 + b, 0:EXT, :]


def add_cols(place, own, col_a, col_b, p):
    even = (place[1] & 1) == 0
    from_a = col_a[p * EXT : (p + 1) * EXT, :]
    from_b = col_b[p * EXT : (p + 1) * EXT, :]
    low = own[p, :, 0:LANES] + jnp.where(even, from_b, from_a)
    high = own[p, :, LANES:TILE] + jnp.where(even, from_a, from_b)
    return low, high


def fold_cols_kernel(depth, place, own, col_a, col_b, total, a_out, b_out):
    row_parity = place[0] & 1
    a_at = aligned((1 - row_parity) * (EXT - depth), RIM)
    b_at = aligned(row_parity * (EXT - depth), RIM)
    for p in range(2):
        low, high = add_cols(place, own, col_a, col_b, p)
        total[p, :, 0:LANES] = low
        total[p, :, LANES:TILE] = high
        a_out[p] = total[p, pl.ds(a_at, depth), :]
        b_out[p] = total[p, pl.ds(b_at, depth), :]


def update_wide_kernel(place, center, total, row_a, row_b, scale, fresh, a_out, b_out):
    row_parity = place[0] & 1
    a_at = aligned((1 - row_parity) * TILE, RIM)
    b_at = aligned(row_parity * TILE, RIM)
    even = (place[1] & 1) == 0
    for p in range(2):
        fresh[p, pl.ds(a_at, TILE), :] = center[p, pl.ds(a_at, TILE), :] - scale[pl.ds(a_at, TILE), :] * (
            total[p, pl.ds(a_at, TILE), :] + row_a[p]
        )
        fresh[p, pl.ds(b_at, TILE), :] = center[p, pl.ds(b_at, TILE), :] - scale[pl.ds(b_at, TILE), :] * (
            total[p, pl.ds(b_at, TILE), :] + row_b[p]
        )

    @pl.when(place[0] == 0)
    def _():
        fresh[:, 0:RIM, :] = jnp.zeros((2, RIM, TILE), jnp.float32)

    @pl.when(place[0] == place[2] - 1)
    def _():
        fresh[:, EXT - RIM :, :] = jnp.zeros((2, RIM, TILE), jnp.float32)

    for p in range(2):
        low = fresh[p, :, 0:LANES]
        high = fresh[p, :, LANES:TILE]
        a_out[p * EXT : (p + 1) * EXT, :] = jnp.where(even, high, low)
        b_out[p * EXT : (p + 1) * EXT, :] = jnp.where(even, low, high)


def update_own_kernel(place, center, total, row_a, row_b, scale, out):
    odd = (place[0] & 1) == 1
    for p in range(2):
        top = jnp.where(odd, row_a[p], row_b[p])
        bottom = jnp.where(odd, row_b[p], row_a[p])
        for half, came in ((0, top), (1, bottom)):
            at = slice(RIM + half * RIM, RIM + (half + 1) * RIM)
            out[p, half * RIM : (half + 1) * RIM, :] = center[p, at, :] - scale[at, :] * (
                total[p, at, :] + came
            )


def swaps(values, axis):
    return tuple(swap(value, axis, first) for first, value in enumerate(values))


def per_device(object_field, probe_field, amplitudes, offsets, counts):
    ahead, back = dft_tables()
    place = jnp.stack(
        [lax.axis_index("row"), lax.axis_index("col"), lax.axis_size("row"), lax.axis_size("col")]
    ).astype(jnp.int32)
    offs = offsets.reshape(1, 2 * MAXPOS)
    cnt = counts.reshape(1, 1)
    flat_offs = offsets.reshape(2 * MAXPOS)
    flat_cnt = counts.reshape(1)
    amps = amplitudes.reshape(MAXPOS, TILE, TILE)

    row_strip = f32(2 * RIM + 8, TILE)
    strips = call(pack_rows_kernel, (row_strip, row_strip), [SMEM, VMEM, VMEM, VMEM])(
        place, object_field, offs, cnt
    )
    row_a, row_b = swaps(strips, "row")
    col_strip = f32(2 * EXT + 8, LANES)
    center, a, b = call(
        pack_cols_kernel, (f32(2, EXT, TILE), col_strip, col_strip), [SMEM] + [VMEM] * 5
    )(place, object_field, row_a, row_b, offs, cnt)
    col_a, col_b = swaps((a, b), "col")

    odd = lax.axis_index("col") % 2 == 1
    near = [s[2 * EXT : 2 * EXT + 3, :META] for s in (col_a, col_b, a)]
    metas = jnp.stack(
        [jnp.where(odd, near[0], near[1]), near[2], jnp.where(odd, near[1], near[0])], axis=1
    ).reshape(9, META).astype(jnp.int32)
    scale = call(
        light_kernel,
        f32(EXT, TILE),
        [SMEM, VMEM],
        [pltpu.VMEM((2, 4 * TILE + 8, LANES), jnp.float32), pltpu.VMEM((5, TILE, LANES), jnp.float32)],
        bytes_accessed=12 << 20,
    )(metas, probe_field)

    fold_strip = f32(2 * EXT, LANES)
    iterate = call(
        iterate_kernel,
        (f32(2, EXT, TILE), fold_strip, fold_strip),
        [SMEM, SMEM, SMEM] + [VMEM] * 7,
        [
            pltpu.VMEM((2, 4, EXT + 8, LANES), jnp.float32),
            pltpu.VMEM((2, 4, EXT + 8, LANES), jnp.float32),
            pltpu.VMEM((2 * TILE, TILE), jnp.bfloat16),
        ],
        flops=3 << 30,
        bytes_accessed=6 << 20,
    )

    def fold(own, a, b, depth):
        a, b = swaps((a, b), "col")
        total, a, b = call(
            functools.partial(fold_cols_kernel, depth),
            (f32(2, EXT, TILE), f32(2, depth, TILE), f32(2, depth, TILE)),
            [SMEM] + [VMEM] * 3,
        )(place, own, a, b)
        return (total,) + swaps((a, b), "row")

    own, a, b = iterate(place, flat_offs, flat_cnt, center, col_a, col_b, probe_field, amps, ahead, back)
    total, row_a, row_b = fold(own, a, b, TILE)
    center, a, b = call(
        update_wide_kernel, (f32(2, EXT, TILE), fold_strip, fold_strip), [SMEM] + [VMEM] * 5
    )(place, center, total, row_a, row_b, scale)
    col_a, col_b = swaps((a, b), "col")
    own, a, b = iterate(place, flat_offs, flat_cnt, center, col_a, col_b, probe_field, amps, ahead, back)
    total, row_a, row_b = fold(own, a, b, RIM)
    return call(update_own_kernel, f32(2, TILE, TILE), [SMEM] + [VMEM] * 5)(
        place, center, total, row_a, row_b, scale
    )


def solution(mesh):
    in_specs = (
        P(None, "row", "col"),
        P(),
        P("row", "col", None, None, None),
        P("row", "col", None, None),
        P("row", "col"),
    )
    return jax.shard_map(
        per_device, mesh=mesh, in_specs=in_specs, out_specs=P(None, "row", "col"), check_vma=False
    )
```

time: 1060 us -> 163 us (0.15)
  local copies, waits for them, and re-layouts: 520 us -> 11.8 us
  loops' own time: 256 us -> 0 us
  other arithmetic: 115 us -> 0.77 us
  Pallas kernels: 0 us -> 24.2 us
  starting transfers between devices: 81.3 us -> 58.9 us
  matrix products: 18 us -> 0 us
    dynamic_update_slice x66 -> x0, local copies, waits for them, and re-layouts: 333 us -> none  [add_one(): return lax.dynamic_update_slice(inner, window + pieces[slot], where_to)]
    another operation x13 -> x0, loops' own time: 256 us -> none  [the longest x11 256 us: place_slots(): return lax.fori_loop(0, MAXPOS, add_one, canvas)]
    dynamic_slice x156 -> x0, local copies, waits for them, and re-layouts: 99 us -> none  [the longest x132 83.6 us: add_one(): where_to = lead_zeros + (row_starts[slot], col_starts[slot])]
    add x69 -> x0, other arithmetic: 62.3 us -> none  [the longest x66 57.7 us: add_one(): return lax.dynamic_update_slice(inner, window + pieces[slot], where_to)]
    gather x60 -> x0, local copies, waits for them, and re-layouts: 45 us -> none
    pallas_call x0 -> x9, Pallas kernels: none -> 24.2 us  [the longest x2 10.7 us: per_device(): iterate(place, flat_offs, flat_cnt, center, col_a, col_b, probe_field, am...]
    ppermute x20 -> x14, starting transfers between devices: 81.3 us -> 58.9 us  [swap(): return lax.ppermute(value, axis, pairs)]
    scatter-add x3 -> x0, local copies, waits for them, and re-layouts: 18.6 us -> none  [per_device(): light_grid = light_grid.at[near_row * TILE:near_row * TILE + 2 * TILE, ne...]
  transfers between devices with their start and end apart: 20 -> 14, of which waited for: 12 -> 9; matrix products, arithmetic and copies ran while one was open for 40% -> 1% of each run, Pallas kernels for 0% -> 4%
where the time goes in v1:
time: 163 us; the launch traced here: 161 us
  waiting for transfers between devices  64.6 us (40%)
  starting transfers between devices  58.9 us (36%)
  Pallas kernels  24.2 us (15%)
  local copies, waits for them, and re-layouts  11.8 us (7%)
    ppermute x14, waiting for transfers between devices, swap(): return lax.ppermute(value, axis, pairs)  64.6 us
    ppermute x14, starting transfers between devices, swap(): return lax.ppermute(value, axis, pairs)  58.9 us
    unnamed x37, local copies, waits for them, and re-layouts  11 us
    pallas_call x2, Pallas kernels, per_device(): iterate(place, flat_offs, flat_cnt, center, col_a, col_b, probe_field, am...  10.7 us
    pallas_call x1, Pallas kernels, per_device(): call(light_kernel, f32(EXT, TILE), [SMEM, VMEM], [pltpu.VMEM((2, 4 * TILE...  6.33 us
  transfers between devices with their start and end apart: 14, of which 9 were waited for; matrix products, arithmetic and copies ran while one was open for 1% of the time, Pallas kernels for 4%

profile of v1, /device:TPU:87, one launch (start us, length us, event | category | flops | bytes accessed | tf_op | source)
XLA Modules:
  0.0 161.3 jit_solution(15474356785435410620)
XLA Ops:
  0.9 1.0 copy-done
  2.6 1.7 %collective-permute-start = (f32[264,256]{1,0:T(8,128)S(1)}, f32[264,256]{1,0:T(8,128)S(1)}, u32[]{:S(2)}, u32[]{:S(2)}) collective-permute-start(f32[264,256]{1,0:T(8,128)S(1)} %get-tuple-element.25), channel_id=1, source_target_pairs={{0,32},{32,0},{64,96},{96,64},{128,160},{160,128},{192,224},{224,1... | collective-permute-start | bytes 811016 | tf_op jit(solution)/shard_map/ppermute | solution.py:42
  4.3 2.0 %collective-permute-start.1 = (f32[264,256]{1,0:T(8,128)S(1)}, f32[264,256]{1,0:T(8,128)S(1)}, u32[]{:S(2)}, u32[]{:S(2)}) collective-permute-start(f32[264,256]{1,0:T(8,128)S(1)} %get-tuple-element.26), channel_id=1, source_target_pairs={{32,64},{64,32},{96,128},{128,96},{160,192},{192,160},{33,65},{65,... | collective-permute-start | bytes 811016 | tf_op jit(solution)/shard_map/ppermute | solution.py:42
  6.3 4.0 %collective-permute-done.row_a = f32[264,256]{1,0:T(8,128)S(1)} collective-permute-done((f32[264,256]{1,0:T(8,128)S(1)}, f32[264,256]{1,0:T(8,128)S(1)}, u32[]{:S(2)}, u32[]{:S(2)}) %collective-permute-start) | collective-permute-done | bytes 270368 | tf_op jit(solution)/shard_map/ppermute | solution.py:42
  10.4 5.7 %collective-permute-done.1.row_b = f32[264,256]{1,0:T(8,128)S(1)} collective-permute-done((f32[264,256]{1,0:T(8,128)S(1)}, f32[264,256]{1,0:T(8,128)S(1)}, u32[]{:S(2)}, u32[]{:S(2)}) %collective-permute-start.1) | collective-permute-done | bytes 270368 | tf_op jit(solution)/shard_map/ppermute | solution.py:42
  16.1 1.7 %shard_map.74 = (f32[2,512,256]{2,1,0:T(8,128)S(1)}, f32[1032,128]{1,0:T(8,128)}, f32[1032,128]{1,0:T(8,128)}) custom-call(s32[4]{0:T(128)S(1)} %pad_add_fusion.place, f32[2,256,256]{2,1,0:T(8,128)S(1)} %copy-done, f32[264,256]{1,0:T(8,128)S(1)} %collective-permute-done.row_a, f32[264,256]{1,0:T(8,128)S(1)} %collective-permute-done.1.row_b, ...), custom_call_target="tpu_custom_call" | custom-call | bytes 1048576 | tf_op jit(solution)/shard_map/pallas_call | solution.py:294
  17.7 7.1 %collective-permute-start.3 = (f32[1032,128]{1,0:T(8,128)}, f32[1032,128]{1,0:T(8,128)S(1)}, u32[]{:S(2)}, u32[]{:S(2)}) collective-permute-start(f32[1032,128]{1,0:T(8,128)} %get-tuple-element.29), channel_id=1, source_target_pairs={{1,2},{2,1},{3,4},{4,3},{5,6},{6,5},{7,8},{8,7},{9,10},{10,9},{11,... | collective-permute-start | bytes 1585160 | tf_op jit(solution)/shard_map/ppermute | solution.py:42
  25.0 13.4 %collective-permute-done.3.col_b = f32[1032,128]{1,0:T(8,128)S(1)} collective-permute-done((f32[1032,128]{1,0:T(8,128)}, f32[1032,128]{1,0:T(8,128)S(1)}, u32[]{:S(2)}, u32[]{:S(2)}) %collective-permute-start.3) | collective-permute-done | bytes 528416 | tf_op jit(solution)/shard_map/ppermute | solution.py:42
  39.2 1.0 copy-done.10
  40.3 1.1 copy-done.11
  41.4 1.0 copy-done.13
  42.4 1.0 copy-done.15
  43.5 5.8 %shard_map.75 = (f32[2,512,256]{2,1,0:T(8,128)S(1)}, f32[1024,128]{1,0:T(8,128)}, f32[1024,128]{1,0:T(8,128)}) custom-call(s32[4]{0:T(128)S(1)} %pad_add_fusion.place, s32[12]{0:T(128)S(1)} %reshape.15.offs, s32[1]{0:T(128)} %bitcast.10.cnt, f32[2,512,256]{2,1,0:T(8,128)S(1)} %get-tuple-element.27.center, f32[1032,128]{1,0:T(8,128)S(1)} %copy-done.10, ...), custom_call_target="tpu_custom_call" | custom-call | flops 3221225472 | bytes 6291456 | tf_op jit(solution)/shard_map/pallas_call | solution.py:335
  49.3 14.9 %collective-permute-start.5 = (f32[1024,128]{1,0:T(8,128)}, f32[1024,128]{1,0:T(8,128)S(1)}, u32[]{:S(2)}, u32[]{:S(2)}) collective-permute-start(f32[1024,128]{1,0:T(8,128)} %get-tuple-element.32), channel_id=1, source_target_pairs={{1,2},{2,1},{3,4},{4,3},{5,6},{6,5},{7,8},{8,7},{9,10},{10,9},{11,... | collective-permute-start | bytes 1572872 | tf_op jit(solution)/shard_map/ppermute | solution.py:42
  65.0 13.1 %collective-permute-done.5.col_b = f32[1024,128]{1,0:T(8,128)S(1)} collective-permute-done((f32[1024,128]{1,0:T(8,128)}, f32[1024,128]{1,0:T(8,128)S(1)}, u32[]{:S(2)}, u32[]{:S(2)}) %collective-permute-start.5) | collective-permute-done | bytes 524320 | tf_op jit(solution)/shard_map/ppermute | solution.py:42
  78.9 1.0 copy-done.2
  80.0 1.0 copy-done.4
  81.0 1.8 %shard_map.76 = (f32[2,512,256]{2,1,0:T(8,128)S(1)}, f32[2,256,256]{2,1,0:T(8,128)}, f32[2,256,256]{2,1,0:T(8,128)}) custom-call(s32[4]{0:T(128)S(1)} %pad_add_fusion.place, f32[2,512,256]{2,1,0:T(8,128)S(1)} %get-tuple-element.30.own, f32[1024,128]{1,0:T(8,128)S(1)} %copy-done.2, f32[1024,128]{1,0:T(8,128)S(1)} %copy-done.4), custom_call_target="tpu_custom_call" | custom-call | bytes 1048576 | tf_op jit(solution)/shard_map/pallas_call | solution.py:328
  82.8 1.9 %collective-permute-start.7 = (f32[2,256,256]{2,1,0:T(8,128)}, f32[2,256,256]{2,1,0:T(8,128)S(1)}, u32[]{:S(2)}, u32[]{:S(2)}) collective-permute-start(f32[2,256,256]{2,1,0:T(8,128)} %get-tuple-element.35), channel_id=1, source_target_pairs={{32,64},{64,32},{96,128},{128,96},{160,192},{192,160},{33,65},{65,... | collective-permute-start | bytes 1572872 | tf_op jit(solution)/shard_map/ppermute | solution.py:42
  86.1 1.0 copy-done.6
  87.2 6.3 %shard_map.77.scale = f32[512,256]{1,0:T(8,128)S(1)} custom-call(s32[9,16]{1,0:T(8,128)S(1)} %convert_element_type.6.metas, f32[2,256,256]{2,1,0:T(8,128)S(1)} %copy-done.6), custom_call_target="tpu_custom_call" | custom-call | bytes 12582912 | tf_op jit(solution)/shard_map/pallas_call | solution.py:304
  93.5 1.6 collective-permute-done.7.row_b
  96.0 9.6 %collective-permute-start.9 = (f32[1024,128]{1,0:T(8,128)S(1)}, f32[1024,128]{1,0:T(8,128)S(1)}, u32[]{:S(2)}, u32[]{:S(2)}) collective-permute-start(f32[1024,128]{1,0:T(8,128)S(1)} %get-tuple-element.38), channel_id=1, source_target_pairs={{1,2},{2,1},{3,4},{4,3},{5,6},{6,5},{7,8},{8,7},{9,10},{10,9},{11,... | collective-permute-start | bytes 1572872 | tf_op jit(solution)/shard_map/ppermute | solution.py:42
  105.7 11.1 %collective-permute-done.9.col_b = f32[1024,128]{1,0:T(8,128)S(1)} collective-permute-done((f32[1024,128]{1,0:T(8,128)S(1)}, f32[1024,128]{1,0:T(8,128)S(1)}, u32[]{:S(2)}, u32[]{:S(2)}) %collective-permute-start.9) | collective-permute-done | bytes 524320 | tf_op jit(solution)/shard_map/ppermute | solution.py:42
  116.8 4.9 %shard_map.79 = (f32[2,512,256]{2,1,0:T(8,128)S(1)}, f32[1024,128]{1,0:T(8,128)S(1)}, f32[1024,128]{1,0:T(8,128)S(1)}) custom-call(s32[4]{0:T(128)S(1)} %pad_add_fusion.place, s32[12]{0:T(128)S(1)} %reshape.15.offs, s32[1]{0:T(128)} %bitcast.11.cnt, f32[2,512,256]{2,1,0:T(8,128)S(1)} %get-tuple-element.36.center, ...), custom_call_target="tpu_custom_call" | custom-call | flops 3221225472 | bytes 6291456 | tf_op jit(solution)/shard_map/pallas_call | solution.py:341
  121.8 16.2 %collective-permute-start.11 = (f32[1024,128]{1,0:T(8,128)S(1)}, f32[1024,128]{1,0:T(8,128)S(1)}, u32[]{:S(2)}, u32[]{:S(2)}) collective-permute-start(f32[1024,128]{1,0:T(8,128)S(1)} %get-tuple-element.41), channel_id=1, source_target_pairs={{1,2},{2,1},{3,4},{4,3},{5,6},{6,5},{7,8},{8,7},{9,10},{10,9},{11,... | collective-permute-start | bytes 1572872 | tf_op jit(solution)/shard_map/ppermute | solution.py:42
  138.0 9.7 %collective-permute-done.11.col_b = f32[1024,128]{1,0:T(8,128)S(1)} collective-permute-done((f32[1024,128]{1,0:T(8,128)S(1)}, f32[1024,128]{1,0:T(8,128)S(1)}, u32[]{:S(2)}, u32[]{:S(2)}) %collective-permute-start.11) | collective-permute-done | bytes 524320 | tf_op jit(solution)/shard_map/ppermute | solution.py:42
  148.5 3.3 %collective-permute-start.12 = (f32[2,128,256]{2,1,0:T(8,128)S(1)}, f32[2,128,256]{2,1,0:T(8,128)S(1)}, u32[]{:S(2)}, u32[]{:S(2)}) collective-permute-start(f32[2,128,256]{2,1,0:T(8,128)S(1)} %get-tuple-element.43), channel_id=1, source_target_pairs={{0,32},{32,0},{64,96},{96,64},{128,160},{160,128},{192,224},{224,1... | collective-permute-start | bytes 786440 | tf_op jit(solution)/shard_map/ppermute | solution.py:42
  151.8 1.9 %collective-permute-start.13 = (f32[2,128,256]{2,1,0:T(8,128)S(1)}, f32[2,128,256]{2,1,0:T(8,128)S(1)}, u32[]{:S(2)}, u32[]{:S(2)}) collective-permute-start(f32[2,128,256]{2,1,0:T(8,128)S(1)} %get-tuple-element.44), channel_id=1, source_target_pairs={{32,64},{64,32},{96,128},{128,96},{160,192},{192,160},{33,65},{65,... | collective-permute-start | bytes 786440 | tf_op jit(solution)/shard_map/ppermute | solution.py:42
  153.7 1.8 %collective-permute-done.12.row_a = f32[2,128,256]{2,1,0:T(8,128)S(1)} collective-permute-done((f32[2,128,256]{2,1,0:T(8,128)S(1)}, f32[2,128,256]{2,1,0:T(8,128)S(1)}, u32[]{:S(2)}, u32[]{:S(2)}) %collective-permute-start.12) | collective-permute-done | bytes 262176 | tf_op jit(solution)/shard_map/ppermute | solution.py:42
  155.6 4.2 %collective-permute-done.13.row_b = f32[2,128,256]{2,1,0:T(8,128)S(1)} collective-permute-done((f32[2,128,256]{2,1,0:T(8,128)S(1)}, f32[2,128,256]{2,1,0:T(8,128)S(1)}, u32[]{:S(2)}, u32[]{:S(2)}) %collective-permute-start.13) | collective-permute-done | bytes 262176 | tf_op jit(solution)/shard_map/ppermute | solution.py:42
  159.8 1.5 shard_map.81
  (50 shorter events, 6.8 us)
Async XLA Ops:
  0.0 0.7 copy-start.17
  0.9 1.0 copy-start
  2.6 7.8 %collective-permute-start = (f32[264,256]{1,0:T(8,128)S(1)}, f32[264,256]{1,0:T(8,128)S(1)}, u32[]{:S(2)}, u32[]{:S(2)}) collective-permute-start(f32[264,256]{1,0:T(8,128)S(1)} %get-tuple-element.25), channel_id=1, source_target_pairs={{0,32},{32,0},{64,96},{96,64},{128,160},{160,128},{192,224},{224,1... | collective-permute-start | bytes 811016 | tf_op jit(solution)/shard_map/ppermute | solution.py:42
  4.3 34.9 %copy-start.5 = (f32[2,256,256]{2,1,0:T(8,128)S(1)}, f32[2,256,256]{2,1,0:T(8,128)}, u32[]{:S(2)}) copy-start(f32[2,256,256]{2,1,0:T(8,128)} %probe.5) | copy-start | bytes 1572868
  4.3 11.8 %collective-permute-start.1 = (f32[264,256]{1,0:T(8,128)S(1)}, f32[264,256]{1,0:T(8,128)S(1)}, u32[]{:S(2)}, u32[]{:S(2)}) collective-permute-start(f32[264,256]{1,0:T(8,128)S(1)} %get-tuple-element.26), channel_id=1, source_target_pairs={{32,64},{64,32},{96,128},{128,96},{160,192},{192,160},{33,65},{65,... | collective-permute-start | bytes 811016 | tf_op jit(solution)/shard_map/ppermute | solution.py:42
  17.7 20.6 %collective-permute-start.3 = (f32[1032,128]{1,0:T(8,128)}, f32[1032,128]{1,0:T(8,128)S(1)}, u32[]{:S(2)}, u32[]{:S(2)}) collective-permute-start(f32[1032,128]{1,0:T(8,128)} %get-tuple-element.29), channel_id=1, source_target_pairs={{1,2},{2,1},{3,4},{4,3},{5,6},{6,5},{7,8},{8,7},{9,10},{10,9},{11,... | collective-permute-start | bytes 1585160 | tf_op jit(solution)/shard_map/ppermute | solution.py:42
  24.8 13.5 %collective-permute-start.2 = (f32[1032,128]{1,0:T(8,128)}, f32[1032,128]{1,0:T(8,128)S(1)}, u32[]{:S(2)}, u32[]{:S(2)}) collective-permute-start(f32[1032,128]{1,0:T(8,128)} %get-tuple-element.28), channel_id=1, source_target_pairs={{0,1},{1,0},{2,3},{3,2},{4,5},{5,4},{6,7},{7,6},{8,9},{9,8},{10,11... | collective-permute-start | bytes 1585160 | tf_op jit(solution)/shard_map/ppermute | solution.py:42
  38.4 10.9 %copy-start.8 = (f32[1032,128]{1,0:T(8,128)}, f32[1032,128]{1,0:T(8,128)S(1)}, u32[]{:S(2)}) copy-start(f32[1032,128]{1,0:T(8,128)S(1)} %collective-permute-done.3.col_b) | copy-start | bytes 1585156
  38.4 0.8 copy-start.9
  39.2 1.0 copy-start.10
  40.3 1.1 copy-start.11
  41.4 1.0 copy-start.13
  42.4 1.0 copy-start.15
  49.3 14.9 %collective-permute-start.4 = (f32[1024,128]{1,0:T(8,128)}, f32[1024,128]{1,0:T(8,128)S(1)}, u32[]{:S(2)}, u32[]{:S(2)}) collective-permute-start(f32[1024,128]{1,0:T(8,128)} %get-tuple-element.31), channel_id=1, source_target_pairs={{0,1},{1,0},{2,3},{3,2},{4,5},{5,4},{6,7},{7,6},{8,9},{9,8},{10,11... | collective-permute-start | bytes 1572872 | tf_op jit(solution)/shard_map/ppermute | solution.py:42
  49.3 28.9 %collective-permute-start.5 = (f32[1024,128]{1,0:T(8,128)}, f32[1024,128]{1,0:T(8,128)S(1)}, u32[]{:S(2)}, u32[]{:S(2)}) collective-permute-start(f32[1024,128]{1,0:T(8,128)} %get-tuple-element.32), channel_id=1, source_target_pairs={{1,2},{2,1},{3,4},{4,3},{5,6},{6,5},{7,8},{8,7},{9,10},{10,9},{11,... | collective-permute-start | bytes 1572872 | tf_op jit(solution)/shard_map/ppermute | solution.py:42
  64.2 0.8 copy-start.1
  78.1 0.8 copy-start.3
  78.9 1.0 copy-start.2
  80.0 1.0 copy-start.4
  82.8 10.7 %collective-permute-start.6 = (f32[2,256,256]{2,1,0:T(8,128)}, f32[2,256,256]{2,1,0:T(8,128)S(1)}, u32[]{:S(2)}, u32[]{:S(2)}) collective-permute-start(f32[2,256,256]{2,1,0:T(8,128)} %get-tuple-element.34), channel_id=1, source_target_pairs={{0,32},{32,0},{64,96},{96,64},{128,160},{160,128},{192,224},{224,1... | collective-permute-start | bytes 1572872 | tf_op jit(solution)/shard_map/ppermute | solution.py:42
  82.8 12.3 %collective-permute-start.7 = (f32[2,256,256]{2,1,0:T(8,128)}, f32[2,256,256]{2,1,0:T(8,128)S(1)}, u32[]{:S(2)}, u32[]{:S(2)}) collective-permute-start(f32[2,256,256]{2,1,0:T(8,128)} %get-tuple-element.35), channel_id=1, source_target_pairs={{32,64},{64,32},{96,128},{128,96},{160,192},{192,160},{33,65},{65,... | collective-permute-start | bytes 1572872 | tf_op jit(solution)/shard_map/ppermute | solution.py:42
  86.1 1.0 copy-start.6
  95.1 21.7 %copy-start.7 = (f32[2,256,256]{2,1,0:T(8,128)S(1)}, f32[2,256,256]{2,1,0:T(8,128)}, u32[]{:S(2)}) copy-start(f32[2,256,256]{2,1,0:T(8,128)} %probe.5) | copy-start | bytes 1572868
  95.1 21.7 %copy-start.12 = (bf16[1,1,6,256,256]{4,3,2,1,0:T(8,128)(2,1)S(1)}, bf16[1,1,6,256,256]{4,3,2,1,0:T(8,128)(2,1)}, u32[]{:S(2)}) copy-start(bf16[1,1,6,256,256]{4,3,2,1,0:T(8,128)(2,1)} %param.9) | copy-start | bytes 2359300
  95.1 21.7 %copy-start.14 = (bf16[512,512]{1,0:T(8,128)(2,1)S(1)}, bf16[512,512]{1,0:T(8,128)(2,1)}, u32[]{:S(2)}) copy-start(bf16[512,512]{1,0:T(8,128)(2,1)} %constant.32.clone.back) | copy-start | bytes 1572868
  95.1 21.7 %copy-start.16 = (bf16[512,512]{1,0:T(8,128)(2,1)S(1)}, bf16[512,512]{1,0:T(8,128)(2,1)}, u32[]{:S(2)}) copy-start(bf16[512,512]{1,0:T(8,128)(2,1)} %constant.31.clone.ahead) | copy-start | bytes 1572868
  95.9 9.7 %collective-permute-start.8 = (f32[1024,128]{1,0:T(8,128)S(1)}, f32[1024,128]{1,0:T(8,128)S(1)}, u32[]{:S(2)}, u32[]{:S(2)}) collective-permute-start(f32[1024,128]{1,0:T(8,128)S(1)} %get-tuple-element.37), channel_id=1, source_target_pairs={{0,1},{1,0},{2,3},{3,2},{4,5},{5,4},{6,7},{7,6},{8,9},{9,8},{10,11... | collective-permute-start | bytes 1572872 | tf_op jit(solution)/shard_map/ppermute | solution.py:42
  96.0 20.7 %collective-permute-start.9 = (f32[1024,128]{1,0:T(8,128)S(1)}, f32[1024,128]{1,0:T(8,128)S(1)}, u32[]{:S(2)}, u32[]{:S(2)}) collective-permute-start(f32[1024,128]{1,0:T(8,128)S(1)} %get-tuple-element.38), channel_id=1, source_target_pairs={{1,2},{2,1},{3,4},{4,3},{5,6},{6,5},{7,8},{8,7},{9,10},{10,9},{11,... | collective-permute-start | bytes 1572872 | tf_op jit(solution)/shard_map/ppermute | solution.py:42
  121.7 16.3 %collective-permute-start.10 = (f32[1024,128]{1,0:T(8,128)S(1)}, f32[1024,128]{1,0:T(8,128)S(1)}, u32[]{:S(2)}, u32[]{:S(2)}) collective-permute-start(f32[1024,128]{1,0:T(8,128)S(1)} %get-tuple-element.40), channel_id=1, source_target_pairs={{0,1},{1,0},{2,3},{3,2},{4,5},{5,4},{6,7},{7,6},{8,9},{9,8},{10,11... | collective-permute-start | bytes 1572872 | tf_op jit(solution)/shard_map/ppermute | solution.py:42
  121.8 25.9 %collective-permute-start.11 = (f32[1024,128]{1,0:T(8,128)S(1)}, f32[1024,128]{1,0:T(8,128)S(1)}, u32[]{:S(2)}, u32[]{:S(2)}) collective-permute-start(f32[1024,128]{1,0:T(8,128)S(1)} %get-tuple-element.41), channel_id=1, source_target_pairs={{1,2},{2,1},{3,4},{4,3},{5,6},{6,5},{7,8},{8,7},{9,10},{10,9},{11,... | collective-permute-start | bytes 1572872 | tf_op jit(solution)/shard_map/ppermute | solution.py:42
  148.5 7.1 %collective-permute-start.12 = (f32[2,128,256]{2,1,0:T(8,128)S(1)}, f32[2,128,256]{2,1,0:T(8,128)S(1)}, u32[]{:S(2)}, u32[]{:S(2)}) collective-permute-start(f32[2,128,256]{2,1,0:T(8,128)S(1)} %get-tuple-element.43), channel_id=1, source_target_pairs={{0,32},{32,0},{64,96},{96,64},{128,160},{160,128},{192,224},{224,1... | collective-permute-start | bytes 786440 | tf_op jit(solution)/shard_map/ppermute | solution.py:42
  151.8 8.0 %collective-permute-start.13 = (f32[2,128,256]{2,1,0:T(8,128)S(1)}, f32[2,128,256]{2,1,0:T(8,128)S(1)}, u32[]{:S(2)}, u32[]{:S(2)}) collective-permute-start(f32[2,128,256]{2,1,0:T(8,128)S(1)} %get-tuple-element.44), channel_id=1, source_target_pairs={{32,64},{64,32},{96,128},{128,96},{160,192},{192,160},{33,65},{65,... | collective-permute-start | bytes 786440 | tf_op jit(solution)/shard_map/ppermute | solution.py:42

commit v2 on v1

v2 whole, which is shorter than its diff:
```python
import functools
import math

import jax
import jax.numpy as jnp
import numpy as np
from jax import lax
from jax.experimental import pallas as pl
from jax.experimental.pallas import tpu as pltpu
from jax.sharding import PartitionSpec as P

TILE = 256
RIM = 128
MAXPOS = 6
EXT = TILE + 2 * RIM
LANES = 128

smooth_term = 0.25
step_size = 0.5
regular_term = 1.0

VMEM = pl.BlockSpec(memory_space=pltpu.VMEM)
SMEM = pl.BlockSpec(memory_space=pltpu.SMEM)


def dft_tables():
    index = np.arange(TILE)
    angle = (index[:, None] * index[None, :] % TILE) * (2.0 * math.pi / TILE)
    cosine = np.cos(angle) / math.sqrt(TILE)
    sine = -np.sin(angle) / math.sqrt(TILE)
    ahead = np.block([[cosine, -sine], [sine, cosine]]).astype(np.float32)
    return jnp.asarray(np.concatenate([ahead, ahead.T]), jnp.bfloat16)


def swap(value, axis, first):
    count = lax.axis_size(axis)
    pairs = []
    for low in range(first, count - 1, 2):
        pairs += [(low, low + 1), (low + 1, low)]
    return lax.ppermute(value, axis, pairs)


def call(body, out_shapes, in_specs, scratch=(), flops=0, bytes_accessed=1 << 20, vmem=6):
    return pl.pallas_call(
        body,
        out_shape=out_shapes,
        in_specs=in_specs,
        out_specs=jax.tree.map(lambda _: VMEM, out_shapes),
        scratch_shapes=scratch,
        compiler_params=pltpu.CompilerParams(vmem_limit_bytes=vmem << 20),
        cost_estimate=pl.CostEstimate(flops=flops, bytes_accessed=bytes_accessed, transcendentals=0),
    )


def f32(*shape):
    return pltpu.VMEM(shape, jnp.float32)


def aligned(value, unit):
    return pl.multiple_of(value, unit)


def pack_rows_kernel(place, obj, offs, cnt, a_out, b_out):
    parity = place[0] & 1
    a_row = aligned((1 - parity) * RIM, RIM)
    b_row = aligned(parity * RIM, RIM)
    for p in range(2):
        a_out[p * RIM : (p + 1) * RIM, :] = obj[p, pl.ds(a_row, RIM), :]
        b_out[p * RIM : (p + 1) * RIM, :] = obj[p, pl.ds(b_row, RIM), :]
    for out in (a_out, b_out):
        out[2 * RIM :, :] = jnp.zeros((8, TILE), jnp.float32)
        out[2 * RIM : 2 * RIM + 1, 0:12] = offs[...].astype(jnp.float32)
        out[2 * RIM : 2 * RIM + 1, 12:13] = cnt[...].astype(jnp.float32)


def pack_cols_kernel(place, obj, row_a, row_b, offs, cnt, a_out, b_out, meta):
    row_odd = place[0] & 1
    a_at = (1 - row_odd) * (RIM + TILE)
    b_at = row_odd * (RIM + TILE)
    even = (place[1] & 1) == 0
    for p in range(2):
        mine = obj[p]
        pieces = [(mine, p * EXT + RIM, TILE)]
        for row, at in ((row_a, a_at), (row_b, b_at)):
            pieces.append((row[p * RIM : (p + 1) * RIM, :], aligned(p * EXT + at, RIM), RIM))
        for piece, at, size in pieces:
            low = piece[:, 0:LANES]
            high = piece[:, LANES:TILE]
            a_out[pl.ds(at, size), :] = jnp.where(even, high, low)
            b_out[pl.ds(at, size), :] = jnp.where(even, low, high)
    meta_a = row_a[2 * RIM : 2 * RIM + 1, 0:LANES]
    meta_b = row_b[2 * RIM : 2 * RIM + 1, 0:LANES]
    odd = row_odd == 1
    meta[...] = jnp.zeros_like(meta)
    meta[0:1, :] = jnp.where(odd, meta_a, meta_b)
    meta[1:2, 0:12] = offs[...].astype(jnp.float32)
    meta[1:2, 12:13] = cnt[...].astype(jnp.float32)
    meta[2:3, :] = jnp.where(odd, meta_b, meta_a)
    a_out[2 * EXT :, :] = meta[...]
    b_out[2 * EXT :, :] = meta[...]


def center_kernel(place, obj, row_a, row_b, center):
    row_odd = place[0] & 1
    a_at = aligned((1 - row_odd) * (RIM + TILE), RIM)
    b_at = aligned(row_odd * (RIM + TILE), RIM)
    for p in range(2):
        center[p, RIM : RIM + TILE, :] = obj[p]
        center[p, pl.ds(a_at, RIM), :] = row_a[p * RIM : (p + 1) * RIM, :]
        center[p, pl.ds(b_at, RIM), :] = row_b[p * RIM : (p + 1) * RIM, :]


def light_kernel(metas, probe, out, canvas, padded):
    power = probe[0] * probe[0] + probe[1] * probe[1]
    padded[...] = jnp.zeros_like(padded)
    for b in range(2):
        padded[b + 1] = power[:, b * LANES : (b + 1) * LANES]
    canvas[...] = jnp.zeros_like(canvas)
    lane = lax.broadcasted_iota(jnp.int32, (TILE, LANES), 1)

    def add(index, carry):
        near = index // MAXPOS
        slot = index - near * MAXPOS
        where = (near % 3) * 8 + near // 3
        used = slot < metas[where, 2 * MAXPOS]
        row = (near // 3) * TILE + metas[where, 2 * slot]
        col = (near % 3 - 1) * TILE - RIM + metas[where, 2 * slot + 1]
        for b in range(2):
            start = b * LANES - col

            @pl.when(used & (start > -LANES) & (start < TILE))
            def _():
                spot = start + LANES
                block = spot // LANES
                shift = spot - block * LANES
                back = (LANES - shift) & (LANES - 1)
                first = pltpu.roll(padded[block], back, 1)
                second = pltpu.roll(padded[block + 1], back, 1)
                part = jnp.where(lane < LANES - shift, first, second)
                canvas[b, pl.ds(row, TILE), :] += part

        return carry

    lax.fori_loop(0, 9 * MAXPOS, add, 0)
    for b in range(2):
        out[:, b * LANES : (b + 1) * LANES] = step_size / (
            canvas[b, TILE : TILE + EXT, :] + regular_term
        )


def product(left, right):
    return jnp.dot(left, right, preferred_element_type=jnp.float32)


def transform(table, other, wave):
    half = product(table[...], wave).astype(jnp.bfloat16)
    return product(half[:TILE], other[0:TILE, :]) + product(half[TILE:], other[TILE:, :])


def iterate_kernel(
    first, place, offs, cnt, meta, center, col_a, col_b, probe, amps, tables, own, a_out, b_out, *rest
):
    ext, grad, wave, residual = rest[-4:]
    ahead = tables.at[0 : 2 * TILE]
    back = tables.at[2 * TILE : 4 * TILE]
    if first:
        odd = (place[1] & 1) == 1
        from_a = col_a[2 * EXT :, :]
        from_b = col_b[2 * EXT :, :]
        for side, rows in enumerate((jnp.where(odd, from_a, from_b), meta[...], jnp.where(odd, from_b, from_a))):
            rest[0][8 * side : 8 * side + 8, :] = rows.astype(jnp.int32)
    parity = place[1] & 1
    a_block = 3 * (1 - parity)
    b_block = 3 * parity
    for p in range(2):
        ext[p, a_block, 0:EXT, :] = col_a[p * EXT : (p + 1) * EXT, :]
        ext[p, b_block, 0:EXT, :] = col_b[p * EXT : (p + 1) * EXT, :]
        for b in range(2):
            ext[p, 1 + b, 0:EXT, :] = center[p, :, b * LANES : (b + 1) * LANES]
    grad[...] = jnp.zeros_like(grad)
    lane = lax.broadcasted_iota(jnp.int32, (TILE, LANES), 1)
    slots = range(MAXPOS)
    rows, shifts, blocks = [], [], []
    for slot in slots:
        col = offs[2 * slot + 1]
        block = col // LANES
        rows.append(pl.ds(offs[2 * slot], TILE))
        shifts.append(col - block * LANES)
        blocks.append([block, block + 1, jnp.minimum(block + 2, 3)])
    for slot in slots:
        unshift = (LANES - shifts[slot]) & (LANES - 1)
        keep = lane < LANES - shifts[slot]
        window = []
        for p in range(2):
            turned = [pltpu.roll(ext[p, b, rows[slot], :], unshift, 1) for b in blocks[slot]]
            window.append([jnp.where(keep, turned[h], turned[h + 1]) for h in range(2)])
        for h in range(2):
            at = slice(h * LANES, (h + 1) * LANES)
            pr = probe[0, :, at]
            pi = probe[1, :, at]
            re = window[0][h]
            im = window[1][h]
            wave[slot, 0:TILE, at] = (pr * re - pi * im).astype(jnp.bfloat16)
            wave[slot, TILE : 2 * TILE, at] = (pr * im + pi * re).astype(jnp.bfloat16)
    spectra = [transform(ahead, back, wave[slot]) for slot in slots]
    for slot in slots:
        used = jnp.where(slot < cnt[0], 1.0, 0.0)
        sr = spectra[slot][:, :TILE]
        si = spectra[slot][:, TILE:]
        root = lax.rsqrt(sr * sr + si * si + smooth_term)
        factor = (1.0 - amps[slot].astype(jnp.float32) * root) * used
        residual[slot, 0:TILE, :] = (sr * factor).astype(jnp.bfloat16)
        residual[slot, TILE : 2 * TILE, :] = (si * factor).astype(jnp.bfloat16)
    waves = [transform(back, ahead, residual[slot]) for slot in slots]
    for slot in slots:
        pieces = [[], []]
        for h in range(2):
            at = slice(h * LANES, (h + 1) * LANES)
            pr = probe[0, :, at]
            pi = probe[1, :, at]
            br = waves[slot][:, h * LANES : (h + 1) * LANES]
            bi = waves[slot][:, TILE + h * LANES : TILE + (h + 1) * LANES]
            pieces[0].append(pltpu.roll(pr * br + pi * bi, shifts[slot], 1))
            pieces[1].append(pltpu.roll(pr * bi - pi * br, shifts[slot], 1))
        right = lane >= shifts[slot]
        for p in range(2):
            h0, h1 = pieces[p]
            grad[p, blocks[slot][0], rows[slot], :] += jnp.where(right, h0, 0.0)
            grad[p, blocks[slot][1], rows[slot], :] += jnp.where(right, h1, h0)
            grad[p, blocks[slot][2], rows[slot], :] += jnp.where(right, 0.0, h1)
    for p in range(2):
        a_out[p * EXT : (p + 1) * EXT, :] = grad[p, a_block, 0:EXT, :]
        b_out[p * EXT : (p + 1) * EXT, :] = grad[p, b_block, 0:EXT, :]
        for b in range(2):
            own[p, :, b * LANES : (b + 1) * LANES] = grad[p, 1 + b, 0:EXT, :]


def add_cols(place, own, col_a, col_b, p):
    even = (place[1] & 1) == 0
    from_a = col_a[p * EXT : (p + 1) * EXT, :]
    from_b = col_b[p * EXT : (p + 1) * EXT, :]
    low = own[p, :, 0:LANES] + jnp.where(even, from_b, from_a)
    high = own[p, :, LANES:TILE] + jnp.where(even, from_a, from_b)
    return low, high


def fold_cols_kernel(depth, place, own, col_a, col_b, total, a_out, b_out):
    row_parity = place[0] & 1
    a_at = aligned((1 - row_parity) * (EXT - depth), RIM)
    b_at = aligned(row_parity * (EXT - depth), RIM)
    for p in range(2):
        low, high = add_cols(place, own, col_a, col_b, p)
        total[p, :, 0:LANES] = low
        total[p, :, LANES:TILE] = high
        a_out[p] = total[p, pl.ds(a_at, depth), :]
        b_out[p] = total[p, pl.ds(b_at, depth), :]


def update_wide_kernel(place, center, total, row_a, row_b, scale, fresh, a_out, b_out):
    row_parity = place[0] & 1
    a_at = aligned((1 - row_parity) * TILE, RIM)
    b_at = aligned(row_parity * TILE, RIM)
    even = (place[1] & 1) == 0
    for p in range(2):
        fresh[p, pl.ds(a_at, TILE), :] = center[p, pl.ds(a_at, TILE), :] - scale[pl.ds(a_at, TILE), :] * (
            total[p, pl.ds(a_at, TILE), :] + row_a[p]
        )
        fresh[p, pl.ds(b_at, TILE), :] = center[p, pl.ds(b_at, TILE), :] - scale[pl.ds(b_at, TILE), :] * (
            total[p, pl.ds(b_at, TILE), :] + row_b[p]
        )

    @pl.when(place[0] == 0)
    def _():
        fresh[:, 0:RIM, :] = jnp.zeros((2, RIM, TILE), jnp.float32)

    @pl.when(place[0] == place[2] - 1)
    def _():
        fresh[:, EXT - RIM :, :] = jnp.zeros((2, RIM, TILE), jnp.float32)

    for p in range(2):
        low = fresh[p, :, 0:LANES]
        high = fresh[p, :, LANES:TILE]
        a_out[p * EXT : (p + 1) * EXT, :] = jnp.where(even, high, low)
        b_out[p * EXT : (p + 1) * EXT, :] = jnp.where(even, low, high)


def update_own_kernel(place, center, total, row_a, row_b, scale, out):
    odd = (place[0] & 1) == 1
    for p in range(2):
        top = jnp.where(odd, row_a[p], row_b[p])
        bottom = jnp.where(odd, row_b[p], row_a[p])
        for half, came in ((0, top), (1, bottom)):
            at = slice(RIM + half * RIM, RIM + (half + 1) * RIM)
            out[p, half * RIM : (half + 1) * RIM, :] = center[p, at, :] - scale[at, :] * (
                total[p, at, :] + came
            )


def swaps(values, axis):
    far = swap(values[1], axis, 1)
    return swap(values[0], axis, 0), far


def per_device(object_field, probe_field, amplitudes, offsets, counts):
    tables = dft_tables()
    place = jnp.stack(
        [lax.axis_index("row"), lax.axis_index("col"), lax.axis_size("row"), lax.axis_size("col")]
    ).astype(jnp.int32)
    offs = offsets.reshape(1, 2 * MAXPOS)
    cnt = counts.reshape(1, 1)
    flat_offs = offsets.reshape(2 * MAXPOS)
    flat_cnt = counts.reshape(1)
    amps = amplitudes.reshape(MAXPOS, TILE, TILE)

    row_strip = f32(2 * RIM + 8, TILE)
    strips = call(pack_rows_kernel, (row_strip, row_strip), [SMEM, VMEM, VMEM, VMEM])(
        place, object_field, offs, cnt
    )
    row_a, row_b = swaps(strips, "row")
    col_strip = f32(2 * EXT + 8, LANES)
    a, b, meta = call(pack_cols_kernel, (col_strip, col_strip, f32(8, LANES)), [SMEM] + [VMEM] * 5)(
        place, object_field, row_a, row_b, offs, cnt
    )
    center = call(center_kernel, f32(2, EXT, TILE), [SMEM] + [VMEM] * 3, bytes_accessed=4 << 20)(
        place, object_field, row_a, row_b
    )
    col_a, col_b = swaps((a, b), "col")

    fold_strip = f32(2 * EXT, LANES)
    grid = pltpu.VMEM((2, 4, EXT + 8, LANES), jnp.float32)
    stack = pltpu.VMEM((MAXPOS, 2 * TILE, TILE), jnp.bfloat16)

    def iterate(first, center, cols):
        outs = (f32(2, EXT, TILE), fold_strip, fold_strip)
        if first:
            outs += (jax.ShapeDtypeStruct((24, LANES), jnp.int32),)
        return call(
            functools.partial(iterate_kernel, first),
            outs,
            [SMEM] * 3 + [VMEM] * 7,
            [grid, grid, stack, stack],
            flops=3 << 30,
            bytes_accessed=6 << 20,
            vmem=14,
        )(place, flat_offs, flat_cnt, meta, center, *cols, probe_field, amps, tables)

    def fold(first, center, cols, depth):
        own, a, b, *metas = iterate(first, center, cols)
        a, b = swaps((a, b), "col")
        total, a, b = call(
            functools.partial(fold_cols_kernel, depth),
            (f32(2, EXT, TILE), f32(2, depth, TILE), f32(2, depth, TILE)),
            [SMEM] + [VMEM] * 3,
        )(place, own, a, b)
        return (total, metas) + swaps((a, b), "row")

    total, metas, row_a, row_b = fold(True, center, (col_a, col_b), TILE)
    scale = call(
        light_kernel,
        f32(EXT, TILE),
        [SMEM, VMEM],
        [pltpu.VMEM((2, 4 * TILE + 8, LANES), jnp.float32), pltpu.VMEM((5, TILE, LANES), jnp.float32)],
        bytes_accessed=12 << 20,
    )(metas[0], probe_field)
    center, a, b = call(
        update_wide_kernel, (f32(2, EXT, TILE), fold_strip, fold_strip), [SMEM] + [VMEM] * 5
    )(place, center, total, row_a, row_b, scale)
    total, _, row_a, row_b = fold(False, center, swaps((a, b), "col"), RIM)
    return call(
        update_own_kernel, jax.ShapeDtypeStruct((2, TILE, TILE), jnp.float32), [SMEM] + [VMEM] * 5
    )(place, center, total, row_a, row_b, scale)


def solution(mesh):
    in_specs = (
        P(None, "row", "col"),
        P(),
        P("row", "col", None, None, None),
        P("row", "col", None, None),
        P("row", "col"),
    )
    return jax.shard_map(
        per_device, mesh=mesh, in_specs=in_specs, out_specs=P(None, "row", "col"), check_vma=False
    )
```

time: 163 us -> 146 us (0.90)
  starting transfers between devices: 58.9 us -> 41 us
  waiting for transfers between devices: 64.6 us -> 74.3 us
  local copies, waits for them, and re-layouts: 11.8 us -> 2.55 us
  Pallas kernels: 24.2 us -> 26.1 us
    ppermute x14, starting transfers between devices: 58.9 us -> 41 us  [swap(): return lax.ppermute(value, axis, pairs)]
    ppermute x14, waiting for transfers between devices: 64.6 us -> 74.3 us  [swap(): return lax.ppermute(value, axis, pairs)]
    unnamed x37 -> x15, local copies, waits for them, and re-layouts: 11 us -> 2.39 us
    pallas_call x1, Pallas kernels: 6.33 us -> 8.08 us  [per_device(): call(light_kernel, f32(EXT, TILE), [SMEM, VMEM], [pltpu.VMEM((2, 4 * TILE...]
    pallas_call x4 -> x5, Pallas kernels: 13.9 us -> 14.9 us  [the longest x2 12.1 us: iterate(): call(functools.partial(iterate_kernel, first), outs, [SMEM] * 3 + [VMEM]...]
  transfers between devices with their start and end apart: 14 -> 14, of which waited for: 9 -> 10; matrix products, arithmetic and copies ran while one was open for 1% -> 0% of each run, Pallas kernels for 4% -> 6%
where the time goes in v2:
time: 146 us; the launch traced here: 145 us
  waiting for transfers between devices  74.3 us (51%)
  starting transfers between devices  41 us (28%)
  Pallas kernels  26.1 us (18%)
  local copies, waits for them, and re-layouts  2.55 us (2%)
    ppermute x14, waiting for transfers between devices, swap(): return lax.ppermute(value, axis, pairs)  74.3 us
    ppermute x14, starting transfers between devices, swap(): return lax.ppermute(value, axis, pairs)  41 us
    pallas_call x2, Pallas kernels, iterate(): call(functools.partial(iterate_kernel, first), outs, [SMEM] * 3 + [VMEM]...  12.1 us
    pallas_call x1, Pallas kernels, per_device(): call(light_kernel, f32(EXT, TILE), [SMEM, VMEM], [pltpu.VMEM((2, 4 * TILE...  8.08 us
  transfers between devices with their start and end apart: 14, of which 10 were waited for; matrix products, arithmetic and copies ran while one was open for 0% of the time, Pallas kernels for 6%

profile of v2, /device:TPU:87, one launch (start us, length us, event | category | flops | bytes accessed | tf_op | source)
XLA Modules:
  0.0 144.9 jit_solution(13664116371075859026)
XLA Ops:
  0.9 1.0 copy-done
  2.0 0.6 shard_map.64
  2.6 1.7 %collective-permute-start = (f32[264,256]{1,0:T(8,128)S(1)}, f32[264,256]{1,0:T(8,128)S(1)}, u32[]{:S(2)}, u32[]{:S(2)}) collective-permute-start(f32[264,256]{1,0:T(8,128)S(1)} %get-tuple-element.26), channel_id=1, source_target_pairs={{0,32},{32,0},{64,96},{96,64},{128,160},{160,128},{192,224},{224,1... | collective-permute-start | bytes 811016 | tf_op jit(solution)/shard_map/ppermute | solution.py:40
  4.3 2.0 %collective-permute-start.1 = (f32[264,256]{1,0:T(8,128)S(1)}, f32[264,256]{1,0:T(8,128)S(1)}, u32[]{:S(2)}, u32[]{:S(2)}) collective-permute-start(f32[264,256]{1,0:T(8,128)S(1)} %get-tuple-element.27), channel_id=1, source_target_pairs={{32,64},{64,32},{96,128},{128,96},{160,192},{192,160},{33,65},{65,... | collective-permute-start | bytes 811016 | tf_op jit(solution)/shard_map/ppermute | solution.py:40
  6.3 4.0 %collective-permute-done.row_a = f32[264,256]{1,0:T(8,128)S(1)} collective-permute-done((f32[264,256]{1,0:T(8,128)S(1)}, f32[264,256]{1,0:T(8,128)S(1)}, u32[]{:S(2)}, u32[]{:S(2)}) %collective-permute-start) | collective-permute-done | bytes 270368 | tf_op jit(solution)/shard_map/ppermute | solution.py:40
  10.4 5.7 %collective-permute-done.1.row_b = f32[264,256]{1,0:T(8,128)S(1)} collective-permute-done((f32[264,256]{1,0:T(8,128)S(1)}, f32[264,256]{1,0:T(8,128)S(1)}, u32[]{:S(2)}, u32[]{:S(2)}) %collective-permute-start.1) | collective-permute-done | bytes 270368 | tf_op jit(solution)/shard_map/ppermute | solution.py:40
  16.1 0.7 shard_map.66
  16.7 1.4 collective-permute-start.2
  18.1 5.7 %collective-permute-start.3 = (f32[1032,128]{1,0:T(8,128)S(1)}, f32[1032,128]{1,0:T(8,128)S(1)}, u32[]{:S(2)}, u32[]{:S(2)}) collective-permute-start(f32[1032,128]{1,0:T(8,128)S(1)} %get-tuple-element.30), channel_id=1, source_target_pairs={{1,2},{2,1},{3,4},{4,3},{5,6},{6,5},{7,8},{8,7},{9,10},{10,9},{11,... | collective-permute-start | bytes 1585160 | tf_op jit(solution)/shard_map/ppermute | solution.py:40
  24.0 0.6 shard_map.65.center
  24.6 13.9 %collective-permute-done.3.col_b = f32[1032,128]{1,0:T(8,128)S(1)} collective-permute-done((f32[1032,128]{1,0:T(8,128)S(1)}, f32[1032,128]{1,0:T(8,128)S(1)}, u32[]{:S(2)}, u32[]{:S(2)}) %collective-permute-start.3) | collective-permute-done | bytes 528416 | tf_op jit(solution)/shard_map/ppermute | solution.py:40
  38.5 1.2 copy-done.4
  39.8 6.1 %shard_map.67 = (f32[2,512,256]{2,1,0:T(8,128)S(1)}, f32[1024,128]{1,0:T(8,128)S(1)}, f32[1024,128]{1,0:T(8,128)S(1)}, s32[24,128]{1,0:T(8,128)S(1)}) custom-call(s32[4]{0:T(128)S(1)} %pad_add_fusion.place, s32[12]{0:T(128)S(1)} %reshape.13.offs, s32[1]{0:T(128)} %bitcast.4.cnt, f32[8,128]{1,0:T(8,128)S(1)} %get-tuple-element.28.meta, ...), custom_call_target="tpu_custom_call" | custom-call | flops 3221225472 | bytes 6291456 | tf_op jit(solution)/shard_map/pallas_call | solution.py:337
  46.0 5.8 %collective-permute-start.5 = (f32[1024,128]{1,0:T(8,128)S(1)}, f32[1024,128]{1,0:T(8,128)S(1)}, u32[]{:S(2)}, u32[]{:S(2)}) collective-permute-start(f32[1024,128]{1,0:T(8,128)S(1)} %get-tuple-element.33), channel_id=1, source_target_pairs={{1,2},{2,1},{3,4},{4,3},{5,6},{6,5},{7,8},{8,7},{9,10},{10,9},{11,... | collective-permute-start | bytes 1572872 | tf_op jit(solution)/shard_map/ppermute | solution.py:40
  51.8 15.9 %collective-permute-done.5.col_b = f32[1024,128]{1,0:T(8,128)S(1)} collective-permute-done((f32[1024,128]{1,0:T(8,128)S(1)}, f32[1024,128]{1,0:T(8,128)S(1)}, u32[]{:S(2)}, u32[]{:S(2)}) %collective-permute-start.5) | collective-permute-done | bytes 524320 | tf_op jit(solution)/shard_map/ppermute | solution.py:40
  67.7 0.8 shard_map.68
  68.6 1.9 %collective-permute-start.7 = (f32[2,256,256]{2,1,0:T(8,128)S(1)}, f32[2,256,256]{2,1,0:T(8,128)S(1)}, u32[]{:S(2)}, u32[]{:S(2)}) collective-permute-start(f32[2,256,256]{2,1,0:T(8,128)S(1)} %get-tuple-element.36), channel_id=1, source_target_pairs={{32,64},{64,32},{96,128},{128,96},{160,192},{192,160},{33,65},{65,... | collective-permute-start | bytes 1572872 | tf_op jit(solution)/shard_map/ppermute | solution.py:40
  70.6 8.1 %shard_map.69.scale = f32[512,256]{1,0:T(8,128)S(1)} custom-call(s32[24,128]{1,0:T(8,128)S(1)} %get-tuple-element.37.metas, f32[2,256,256]{2,1,0:T(8,128)S(1)} %copy-done.2), custom_call_target="tpu_custom_call" | custom-call | bytes 12582912 | tf_op jit(solution)/shard_map/pallas_call | solution.py:358
  78.6 1.4 collective-permute-done.6.row_a
  80.0 5.6 %collective-permute-done.7.row_b = f32[2,256,256]{2,1,0:T(8,128)S(1)} collective-permute-done((f32[2,256,256]{2,1,0:T(8,128)S(1)}, f32[2,256,256]{2,1,0:T(8,128)S(1)}, u32[]{:S(2)}, u32[]{:S(2)}) %collective-permute-start.7) | collective-permute-done | bytes 524320 | tf_op jit(solution)/shard_map/ppermute | solution.py:40
  85.6 0.9 shard_map.70
  86.7 4.5 %collective-permute-start.9 = (f32[1024,128]{1,0:T(8,128)S(1)}, f32[1024,128]{1,0:T(8,128)S(1)}, u32[]{:S(2)}, u32[]{:S(2)}) collective-permute-start(f32[1024,128]{1,0:T(8,128)S(1)} %get-tuple-element.40), channel_id=1, source_target_pairs={{1,2},{2,1},{3,4},{4,3},{5,6},{6,5},{7,8},{8,7},{9,10},{10,9},{11,... | collective-permute-start | bytes 1572872 | tf_op jit(solution)/shard_map/ppermute | solution.py:40
  91.2 10.4 %collective-permute-done.9.col_b = f32[1024,128]{1,0:T(8,128)S(1)} collective-permute-done((f32[1024,128]{1,0:T(8,128)S(1)}, f32[1024,128]{1,0:T(8,128)S(1)}, u32[]{:S(2)}, u32[]{:S(2)}) %collective-permute-start.9) | collective-permute-done | bytes 524320 | tf_op jit(solution)/shard_map/ppermute | solution.py:40
  101.6 6.0 %shard_map.71 = (f32[2,512,256]{2,1,0:T(8,128)S(1)}, f32[1024,128]{1,0:T(8,128)S(1)}, f32[1024,128]{1,0:T(8,128)S(1)}) custom-call(s32[4]{0:T(128)S(1)} %pad_add_fusion.place, s32[12]{0:T(128)S(1)} %reshape.13.offs, s32[1]{0:T(128)} %bitcast.5.cnt, f32[8,128]{1,0:T(8,128)S(1)} %get-tuple-element.28.meta, f32[2,512,256]{2,1,0:T(8,128)S(1)} %get-tuple-element.38.center, ...), custom_call_target="tpu_custom_call" | custom-call | flops 3221225472 | bytes 6291456 | tf_op jit(solution)/shard_map/pallas_call | solution.py:337
  107.6 5.5 %collective-permute-start.11 = (f32[1024,128]{1,0:T(8,128)S(1)}, f32[1024,128]{1,0:T(8,128)S(1)}, u32[]{:S(2)}, u32[]{:S(2)}) collective-permute-start(f32[1024,128]{1,0:T(8,128)S(1)} %get-tuple-element.43), channel_id=1, source_target_pairs={{1,2},{2,1},{3,4},{4,3},{5,6},{6,5},{7,8},{8,7},{9,10},{10,9},{11,... | collective-permute-start | bytes 1572872 | tf_op jit(solution)/shard_map/ppermute | solution.py:40
  113.1 11.8 %collective-permute-done.11.col_b = f32[1024,128]{1,0:T(8,128)S(1)} collective-permute-done((f32[1024,128]{1,0:T(8,128)S(1)}, f32[1024,128]{1,0:T(8,128)S(1)}, u32[]{:S(2)}, u32[]{:S(2)}) %collective-permute-start.11) | collective-permute-done | bytes 524320 | tf_op jit(solution)/shard_map/ppermute | solution.py:40
  124.9 0.8 shard_map.72
  125.7 9.4 %collective-permute-start.12 = (f32[2,128,256]{2,1,0:T(8,128)S(1)}, f32[2,128,256]{2,1,0:T(8,128)S(1)}, u32[]{:S(2)}, u32[]{:S(2)}) collective-permute-start(f32[2,128,256]{2,1,0:T(8,128)S(1)} %get-tuple-element.45), channel_id=1, source_target_pairs={{0,32},{32,0},{64,96},{96,64},{128,160},{160,128},{192,224},{224,1... | collective-permute-start | bytes 786440 | tf_op jit(solution)/shard_map/ppermute | solution.py:40
  135.1 2.7 %collective-permute-start.13 = (f32[2,128,256]{2,1,0:T(8,128)S(1)}, f32[2,128,256]{2,1,0:T(8,128)S(1)}, u32[]{:S(2)}, u32[]{:S(2)}) collective-permute-start(f32[2,128,256]{2,1,0:T(8,128)S(1)} %get-tuple-element.46), channel_id=1, source_target_pairs={{32,64},{64,32},{96,128},{128,96},{160,192},{192,160},{33,65},{65,... | collective-permute-start | bytes 786440 | tf_op jit(solution)/shard_map/ppermute | solution.py:40
  137.8 1.3 collective-permute-done.12.row_a
  139.1 4.4 %collective-permute-done.13.row_b = f32[2,128,256]{2,1,0:T(8,128)S(1)} collective-permute-done((f32[2,128,256]{2,1,0:T(8,128)S(1)}, f32[2,128,256]{2,1,0:T(8,128)S(1)}, u32[]{:S(2)}, u32[]{:S(2)}) %collective-permute-start.13) | collective-permute-done | bytes 262176 | tf_op jit(solution)/shard_map/ppermute | solution.py:40
  143.4 1.5 %shard_map.73 = f32[2,256,256]{2,1,0:T(8,128)} custom-call(s32[4]{0:T(128)S(1)} %pad_add_fusion.place, f32[2,512,256]{2,1,0:T(8,128)S(1)} %get-tuple-element.38.center, f32[2,512,256]{2,1,0:T(8,128)S(1)} %get-tuple-element.44.total, f32[2,128,256]{2,1,0:T(8,128)S(1)} %collective-permute-done.12.row_a, f32[2,128,256]{2,1,0:T(8,128)S(1)} %collective-permute-done.13.row_b, ...), custom_call_target="tpu_custom_call" | custom-call | bytes 1048576 | tf_op jit(solution)/shard_map/pallas_call | solution.py:369
  (24 shorter events, 0.7 us)
Async XLA Ops:
  0.0 0.7 copy-start.6
  0.9 1.0 copy-start
  2.6 7.8 %collective-permute-start = (f32[264,256]{1,0:T(8,128)S(1)}, f32[264,256]{1,0:T(8,128)S(1)}, u32[]{:S(2)}, u32[]{:S(2)}) collective-permute-start(f32[264,256]{1,0:T(8,128)S(1)} %get-tuple-element.26), channel_id=1, source_target_pairs={{0,32},{32,0},{64,96},{96,64},{128,160},{160,128},{192,224},{224,1... | collective-permute-start | bytes 811016 | tf_op jit(solution)/shard_map/ppermute | solution.py:40
  4.3 19.7 %copy-start.1 = (f32[2,256,256]{2,1,0:T(8,128)S(1)}, f32[2,256,256]{2,1,0:T(8,128)}, u32[]{:S(2)}) copy-start(f32[2,256,256]{2,1,0:T(8,128)} %obj.5) | copy-start | bytes 1572868
  4.3 11.8 %collective-permute-start.1 = (f32[264,256]{1,0:T(8,128)S(1)}, f32[264,256]{1,0:T(8,128)S(1)}, u32[]{:S(2)}, u32[]{:S(2)}) collective-permute-start(f32[264,256]{1,0:T(8,128)S(1)} %get-tuple-element.27), channel_id=1, source_target_pairs={{32,64},{64,32},{96,128},{128,96},{160,192},{192,160},{33,65},{65,... | collective-permute-start | bytes 811016 | tf_op jit(solution)/shard_map/ppermute | solution.py:40
  16.7 7.9 %collective-permute-start.2 = (f32[1032,128]{1,0:T(8,128)S(1)}, f32[1032,128]{1,0:T(8,128)S(1)}, u32[]{:S(2)}, u32[]{:S(2)}) collective-permute-start(f32[1032,128]{1,0:T(8,128)S(1)} %get-tuple-element.29), channel_id=1, source_target_pairs={{0,1},{1,0},{2,3},{3,2},{4,5},{5,4},{6,7},{7,6},{8,9},{9,8},{10,11... | collective-permute-start | bytes 1585160 | tf_op jit(solution)/shard_map/ppermute | solution.py:40
  18.1 20.4 %collective-permute-start.3 = (f32[1032,128]{1,0:T(8,128)S(1)}, f32[1032,128]{1,0:T(8,128)S(1)}, u32[]{:S(2)}, u32[]{:S(2)}) collective-permute-start(f32[1032,128]{1,0:T(8,128)S(1)} %get-tuple-element.30), channel_id=1, source_target_pairs={{1,2},{2,1},{3,4},{4,3},{5,6},{6,5},{7,8},{8,7},{9,10},{10,9},{11,... | collective-permute-start | bytes 1585160 | tf_op jit(solution)/shard_map/ppermute | solution.py:40
  24.0 14.6 %copy-start.2 = (f32[2,256,256]{2,1,0:T(8,128)S(1)}, f32[2,256,256]{2,1,0:T(8,128)}, u32[]{:S(2)}) copy-start(f32[2,256,256]{2,1,0:T(8,128)} %probe.5) | copy-start | bytes 1572868
  24.0 14.6 %copy-start.3 = (bf16[1,1,6,256,256]{4,3,2,1,0:T(8,128)(2,1)S(1)}, bf16[1,1,6,256,256]{4,3,2,1,0:T(8,128)(2,1)}, u32[]{:S(2)}) copy-start(bf16[1,1,6,256,256]{4,3,2,1,0:T(8,128)(2,1)} %param.8) | copy-start | bytes 2359300
  38.5 1.2 copy-start.4
  45.9 5.9 %collective-permute-start.4 = (f32[1024,128]{1,0:T(8,128)S(1)}, f32[1024,128]{1,0:T(8,128)S(1)}, u32[]{:S(2)}, u32[]{:S(2)}) collective-permute-start(f32[1024,128]{1,0:T(8,128)S(1)} %get-tuple-element.32), channel_id=1, source_target_pairs={{0,1},{1,0},{2,3},{3,2},{4,5},{5,4},{6,7},{7,6},{8,9},{9,8},{10,11... | collective-permute-start | bytes 1572872 | tf_op jit(solution)/shard_map/ppermute | solution.py:40
  46.0 21.7 %collective-permute-start.5 = (f32[1024,128]{1,0:T(8,128)S(1)}, f32[1024,128]{1,0:T(8,128)S(1)}, u32[]{:S(2)}, u32[]{:S(2)}) collective-permute-start(f32[1024,128]{1,0:T(8,128)S(1)} %get-tuple-element.33), channel_id=1, source_target_pairs={{1,2},{2,1},{3,4},{4,3},{5,6},{6,5},{7,8},{8,7},{9,10},{10,9},{11,... | collective-permute-start | bytes 1572872 | tf_op jit(solution)/shard_map/ppermute | solution.py:40
  68.5 11.5 %collective-permute-start.6 = (f32[2,256,256]{2,1,0:T(8,128)S(1)}, f32[2,256,256]{2,1,0:T(8,128)S(1)}, u32[]{:S(2)}, u32[]{:S(2)}) collective-permute-start(f32[2,256,256]{2,1,0:T(8,128)S(1)} %get-tuple-element.35), channel_id=1, source_target_pairs={{0,32},{32,0},{64,96},{96,64},{128,160},{160,128},{192,224},{224,1... | collective-permute-start | bytes 1572872 | tf_op jit(solution)/shard_map/ppermute | solution.py:40
  68.6 17.0 %collective-permute-start.7 = (f32[2,256,256]{2,1,0:T(8,128)S(1)}, f32[2,256,256]{2,1,0:T(8,128)S(1)}, u32[]{:S(2)}, u32[]{:S(2)}) collective-permute-start(f32[2,256,256]{2,1,0:T(8,128)S(1)} %get-tuple-element.36), channel_id=1, source_target_pairs={{32,64},{64,32},{96,128},{128,96},{160,192},{192,160},{33,65},{65,... | collective-permute-start | bytes 1572872 | tf_op jit(solution)/shard_map/ppermute | solution.py:40
  85.6 15.9 %copy-start.5 = (bf16[1024,512]{1,0:T(8,128)(2,1)S(1)}, bf16[1024,512]{1,0:T(8,128)(2,1)}, u32[]{:S(2)}) copy-start(bf16[1024,512]{1,0:T(8,128)(2,1)} %constant.15.clone.tables) | copy-start | bytes 3145732
  86.6 4.6 %collective-permute-start.8 = (f32[1024,128]{1,0:T(8,128)S(1)}, f32[1024,128]{1,0:T(8,128)S(1)}, u32[]{:S(2)}, u32[]{:S(2)}) collective-permute-start(f32[1024,128]{1,0:T(8,128)S(1)} %get-tuple-element.39), channel_id=1, source_target_pairs={{0,1},{1,0},{2,3},{3,2},{4,5},{5,4},{6,7},{7,6},{8,9},{9,8},{10,11... | collective-permute-start | bytes 1572872 | tf_op jit(solution)/shard_map/ppermute | solution.py:40
  86.7 14.9 %collective-permute-start.9 = (f32[1024,128]{1,0:T(8,128)S(1)}, f32[1024,128]{1,0:T(8,128)S(1)}, u32[]{:S(2)}, u32[]{:S(2)}) collective-permute-start(f32[1024,128]{1,0:T(8,128)S(1)} %get-tuple-element.40), channel_id=1, source_target_pairs={{1,2},{2,1},{3,4},{4,3},{5,6},{6,5},{7,8},{8,7},{9,10},{10,9},{11,... | collective-permute-start | bytes 1572872 | tf_op jit(solution)/shard_map/ppermute | solution.py:40
  107.5 5.6 %collective-permute-start.10 = (f32[1024,128]{1,0:T(8,128)S(1)}, f32[1024,128]{1,0:T(8,128)S(1)}, u32[]{:S(2)}, u32[]{:S(2)}) collective-permute-start(f32[1024,128]{1,0:T(8,128)S(1)} %get-tuple-element.42), channel_id=1, source_target_pairs={{0,1},{1,0},{2,3},{3,2},{4,5},{5,4},{6,7},{7,6},{8,9},{9,8},{10,11... | collective-permute-start | bytes 1572872 | tf_op jit(solution)/shard_map/ppermute | solution.py:40
  107.6 17.3 %collective-permute-start.11 = (f32[1024,128]{1,0:T(8,128)S(1)}, f32[1024,128]{1,0:T(8,128)S(1)}, u32[]{:S(2)}, u32[]{:S(2)}) collective-permute-start(f32[1024,128]{1,0:T(8,128)S(1)} %get-tuple-element.43), channel_id=1, source_target_pairs={{1,2},{2,1},{3,4},{4,3},{5,6},{6,5},{7,8},{8,7},{9,10},{10,9},{11,... | collective-permute-start | bytes 1572872 | tf_op jit(solution)/shard_map/ppermute | solution.py:40
  125.7 13.4 %collective-permute-start.12 = (f32[2,128,256]{2,1,0:T(8,128)S(1)}, f32[2,128,256]{2,1,0:T(8,128)S(1)}, u32[]{:S(2)}, u32[]{:S(2)}) collective-permute-start(f32[2,128,256]{2,1,0:T(8,128)S(1)} %get-tuple-element.45), channel_id=1, source_target_pairs={{0,32},{32,0},{64,96},{96,64},{128,160},{160,128},{192,224},{224,1... | collective-permute-start | bytes 786440 | tf_op jit(solution)/shard_map/ppermute | solution.py:40
  135.1 8.3 %collective-permute-start.13 = (f32[2,128,256]{2,1,0:T(8,128)S(1)}, f32[2,128,256]{2,1,0:T(8,128)S(1)}, u32[]{:S(2)}, u32[]{:S(2)}) collective-permute-start(f32[2,128,256]{2,1,0:T(8,128)S(1)} %get-tuple-element.46), channel_id=1, source_target_pairs={{32,64},{64,32},{96,128},{128,96},{160,192},{192,160},{33,65},{65,... | collective-permute-start | bytes 786440 | tf_op jit(solution)/shard_map/ppermute | solution.py:40

commit v3 on v2

--- a/solution.py
+++ b/solution.py
@@ -60,47 +60,58 @@
     return pl.multiple_of(value, unit)
 
 
-def pack_rows_kernel(place, obj, offs, cnt, a_out, b_out):
+def own_meta(offs, cnt, width):
+    lane = lax.broadcasted_iota(jnp.int32, (1, width), 1)
+    row = jnp.where(lane == 2 * MAXPOS, cnt[0, 0], 0)
+    for slot in range(MAXPOS):
+        row = jnp.where(lane == 2 * slot, offs[0, slot], row)
+        row = jnp.where(lane == 2 * slot + 1, offs[1, slot], row)
+    return row.astype(jnp.float32)
+
+
+def pack_rows_kernel(place, obj, offs, cnt, a_out, b_out, arrived):
     parity = place[0] & 1
-    a_row = aligned((1 - parity) * RIM, RIM)
-    b_row = aligned(parity * RIM, RIM)
-    for p in range(2):
-        a_out[p * RIM : (p + 1) * RIM, :] = obj[p, pl.ds(a_row, RIM), :]
-        b_out[p * RIM : (p + 1) * RIM, :] = obj[p, pl.ds(b_row, RIM), :]
+    copies = []
+    for p in range(2):
+        for out, at in ((a_out, 1 - parity), (b_out, parity)):
+            copies.append(
+                pltpu.make_async_copy(
+                    obj.at[p, pl.ds(aligned(at * RIM, RIM), RIM), :],
+                    out.at[pl.ds(p * RIM, RIM), :],
+                    arrived.at[len(copies)],
+                )
+            )
+            copies[-1].start()
+    meta = own_meta(offs, cnt, TILE)
     for out in (a_out, b_out):
         out[2 * RIM :, :] = jnp.zeros((8, TILE), jnp.float32)
-        out[2 * RIM : 2 * RIM + 1, 0:12] = offs[...].astype(jnp.float32)
-        out[2 * RIM : 2 * RIM + 1, 12:13] = cnt[...].astype(jnp.float32)
-
-
-def pack_cols_kernel(place, obj, row_a, row_b, offs, cnt, a_out, b_out, meta):
+        out[2 * RIM : 2 * RIM + 1, :] = meta
+    for copy in copies:
+        copy.wait()
+
+
+def pack_cols_kernel(near, place, obj, row_a, row_b, offs, cnt, out, meta):
     row_odd = place[0] & 1
     a_at = (1 - row_odd) * (RIM + TILE)
     b_at = row_odd * (RIM + TILE)
-    even = (place[1] & 1) == 0
-    for p in range(2):
-        mine = obj[p]
-        pieces = [(mine, p * EXT + RIM, TILE)]
+    high_side = (place[1] & 1) == (0 if near else 1)
+    for p in range(2):
+        pieces = [(obj[p], p * EXT + RIM, TILE)]
         for row, at in ((row_a, a_at), (row_b, b_at)):
             pieces.append((row[p * RIM : (p + 1) * RIM, :], aligned(p * EXT + at, RIM), RIM))
         for piece, at, size in pieces:
-            low = piece[:, 0:LANES]
-            high = piece[:, LANES:TILE]
-            a_out[pl.ds(at, size), :] = jnp.where(even, high, low)
-            b_out[pl.ds(at, size), :] = jnp.where(even, low, high)
+            out[pl.ds(at, size), :] = jnp.where(high_side, piece[:, LANES:TILE], piece[:, 0:LANES])
     meta_a = row_a[2 * RIM : 2 * RIM + 1, 0:LANES]
     meta_b = row_b[2 * RIM : 2 * RIM + 1, 0:LANES]
     odd = row_odd == 1
     meta[...] = jnp.zeros_like(meta)
     meta[0:1, :] = jnp.where(odd, meta_a, meta_b)
-    meta[1:2, 0:12] = offs[...].astype(jnp.float32)
-    meta[1:2, 12:13] = cnt[...].astype(jnp.float32)
+    meta[1:2, :] = own_meta(offs, cnt, LANES)
     meta[2:3, :] = jnp.where(odd, meta_b, meta_a)
-    a_out[2 * EXT :, :] = meta[...]
-    b_out[2 * EXT :, :] = meta[...]
-
-
-def center_kernel(place, obj, row_a, row_b, center):
+    out[2 * EXT :, :] = meta[...]
+
+
+def center_kernel(place, obj, row_a, row_b, tables, center):
     row_odd = place[0] & 1
     a_at = aligned((1 - row_odd) * (RIM + TILE), RIM)
     b_at = aligned(row_odd * (RIM + TILE), RIM)
@@ -158,9 +169,10 @@
 
 
 def iterate_kernel(
-    first, place, offs, cnt, meta, center, col_a, col_b, probe, amps, tables, own, a_out, b_out, *rest
+    first, place, offs, cnt, meta, center, col_1, col_2, probe, amps, tables, own, a_out, b_out, *rest
 ):
     ext, grad, wave, residual = rest[-4:]
+    col_a, col_b = (col_1, col_2) if first else (col_2, col_1)
     ahead = tables.at[0 : 2 * TILE]
     back = tables.at[2 * TILE : 4 * TILE]
     if first:
@@ -182,9 +194,9 @@
     slots = range(MAXPOS)
     rows, shifts, blocks = [], [], []
     for slot in slots:
-        col = offs[2 * slot + 1]
+        col = offs[1, slot]
         block = col // LANES
-        rows.append(pl.ds(offs[2 * slot], TILE))
+        rows.append(pl.ds(offs[0, slot], TILE))
         shifts.append(col - block * LANES)
         blocks.append([block, block + 1, jnp.minimum(block + 2, 3)])
     for slot in slots:
@@ -204,7 +216,7 @@
             wave[slot, TILE : 2 * TILE, at] = (pr * im + pi * re).astype(jnp.bfloat16)
     spectra = [transform(ahead, back, wave[slot]) for slot in slots]
     for slot in slots:
-        used = jnp.where(slot < cnt[0], 1.0, 0.0)
+        used = jnp.where(slot < cnt[0, 0], 1.0, 0.0)
         sr = spectra[slot][:, :TILE]
         si = spectra[slot][:, TILE:]
         root = lax.rsqrt(sr * sr + si * si + smooth_term)
@@ -244,7 +256,7 @@
     return low, high
 
 
-def fold_cols_kernel(depth, place, own, col_a, col_b, total, a_out, b_out):
+def fold_cols_kernel(depth, place, own, col_b, col_a, total, a_out, b_out):
     row_parity = place[0] & 1
     a_at = aligned((1 - row_parity) * (EXT - depth), RIM)
     b_at = aligned(row_parity * (EXT - depth), RIM)
@@ -284,16 +296,22 @@
         b_out[p * EXT : (p + 1) * EXT, :] = jnp.where(even, low, high)
 
 
-def update_own_kernel(place, center, total, row_a, row_b, scale, out):
+def update_own_kernel(place, center, total, row_a, row_b, scale, out, fresh, left):
     odd = (place[0] & 1) == 1
+    copies = []
     for p in range(2):
         top = jnp.where(odd, row_a[p], row_b[p])
         bottom = jnp.where(odd, row_b[p], row_a[p])
         for half, came in ((0, top), (1, bottom)):
             at = slice(RIM + half * RIM, RIM + (half + 1) * RIM)
-            out[p, half * RIM : (half + 1) * RIM, :] = center[p, at, :] - scale[at, :] * (
-                total[p, at, :] + came
+            rows = slice(half * RIM, (half + 1) * RIM)
+            fresh[p, rows, :] = center[p, at, :] - scale[at, :] * (total[p, at, :] + came)
+            copies.append(
+                pltpu.make_async_copy(fresh.at[p, rows, :], out.at[p, rows, :], left.at[len(copies)])
             )
+            copies[-1].start()
+    for copy in copies:
+        copy.wait()
 
 
 def swaps(values, axis):
@@ -306,23 +324,31 @@
     place = jnp.stack(
         [lax.axis_index("row"), lax.axis_index("col"), lax.axis_size("row"), lax.axis_size("col")]
     ).astype(jnp.int32)
-    offs = offsets.reshape(1, 2 * MAXPOS)
+    offs = jnp.transpose(offsets, (0, 1, 3, 2)).reshape(2, MAXPOS)
     cnt = counts.reshape(1, 1)
-    flat_offs = offsets.reshape(2 * MAXPOS)
-    flat_cnt = counts.reshape(1)
     amps = amplitudes.reshape(MAXPOS, TILE, TILE)
 
     row_strip = f32(2 * RIM + 8, TILE)
-    strips = call(pack_rows_kernel, (row_strip, row_strip), [SMEM, VMEM, VMEM, VMEM])(
-        place, object_field, offs, cnt
-    )
+    strips = call(
+        pack_rows_kernel,
+        (row_strip, row_strip),
+        [SMEM, pl.BlockSpec(memory_space=pl.ANY), SMEM, SMEM],
+        [pltpu.SemaphoreType.DMA((4,))],
+    )(place, object_field, offs, cnt)
     row_a, row_b = swaps(strips, "row")
-    col_strip = f32(2 * EXT + 8, LANES)
-    a, b, meta = call(pack_cols_kernel, (col_strip, col_strip, f32(8, LANES)), [SMEM] + [VMEM] * 5)(
-        place, object_field, row_a, row_b, offs, cnt
-    )
-    center = call(center_kernel, f32(2, EXT, TILE), [SMEM] + [VMEM] * 3, bytes_accessed=4 << 20)(
-        place, object_field, row_a, row_b
+
+    def pack_cols(near):
+        return call(
+            functools.partial(pack_cols_kernel, near),
+            (f32(2 * EXT + 8, LANES), f32(8, LANES)),
+            [SMEM] + [VMEM] * 3 + [SMEM] * 2,
+            bytes_accessed=(8 << 20) if near else (1 << 20),
+        )(place, object_field, row_a, row_b, offs, cnt)
+
+    b, meta = pack_cols(False)
+    a, _ = pack_cols(True)
+    center = call(center_kernel, f32(2, EXT, TILE), [SMEM] + [VMEM] * 4, bytes_accessed=4 << 20)(
+        place, object_field, row_a, row_b, tables
     )
     col_a, col_b = swaps((a, b), "col")
 
@@ -342,7 +368,7 @@
             flops=3 << 30,
             bytes_accessed=6 << 20,
             vmem=14,
-        )(place, flat_offs, flat_cnt, meta, center, *cols, probe_field, amps, tables)
+        )(place, offs, cnt, meta, center, *(cols if first else cols[::-1]), probe_field, amps, tables)
 
     def fold(first, center, cols, depth):
         own, a, b, *metas = iterate(first, center, cols)
@@ -351,7 +377,7 @@
             functools.partial(fold_cols_kernel, depth),
             (f32(2, EXT, TILE), f32(2, depth, TILE), f32(2, depth, TILE)),
             [SMEM] + [VMEM] * 3,
-        )(place, own, a, b)
+        )(place, own, b, a)
         return (total, metas) + swaps((a, b), "row")
 
     total, metas, row_a, row_b = fold(True, center, (col_a, col_b), TILE)
@@ -366,8 +392,13 @@
         update_wide_kernel, (f32(2, EXT, TILE), fold_strip, fold_strip), [SMEM] + [VMEM] * 5
     )(place, center, total, row_a, row_b, scale)
     total, _, row_a, row_b = fold(False, center, swaps((a, b), "col"), RIM)
-    return call(
-        update_own_kernel, jax.ShapeDtypeStruct((2, TILE, TILE), jnp.float32), [SMEM] + [VMEM] * 5
+    return pl.pallas_call(
+        update_own_kernel,
+        out_shape=jax.ShapeDtypeStruct((2, TILE, TILE), jnp.float32),
+        in_specs=[SMEM] + [VMEM] * 5,
+        out_specs=pl.BlockSpec(memory_space=pl.ANY),
+        scratch_shapes=[pltpu.VMEM((2, TILE, TILE), jnp.float32), pltpu.SemaphoreType.DMA((4,))],
+        compiler_params=pltpu.CompilerParams(vmem_limit_bytes=6 << 20),
     )(place, center, total, row_a, row_b, scale)
 
 

time: 146 us -> 150 us (1.027)
  Pallas kernels: 26.1 us -> 28.4 us
    pallas_call x4 -> x5, Pallas kernels: 3.4 us -> 5.12 us  [the longest x2 1.81 us: pack_cols(): call(functools.partial(pack_cols_kernel, near), (f32(2 * EXT + 8, LANES),...]
  transfers between devices with their start and end apart: 14 -> 14, of which waited for: 10 -> 8; matrix products, arithmetic and copies ran while one was open for 0% -> 0% of each run, Pallas kernels for 6% -> 7%
where the time goes in v3:
time: 150 us; the launch traced here: 149 us
  waiting for transfers between devices  75.7 us (50%)
  starting transfers between devices  41.6 us (28%)
  Pallas kernels  28.4 us (19%)
  local copies, waits for them, and re-layouts  1.74 us (1%)
    ppermute x14, waiting for transfers between devices, swap(): return lax.ppermute(value, axis, pairs)  75.7 us
    ppermute x14, starting transfers between devices, swap(): return lax.ppermute(value, axis, pairs)  41.6 us
    pallas_call x2, Pallas kernels, iterate(): call(functools.partial(iterate_kernel, first), outs, [SMEM] * 3 + [VMEM]...  12.3 us
    pallas_call x1, Pallas kernels, per_device(): call(light_kernel, f32(EXT, TILE), [SMEM, VMEM], [pltpu.VMEM((2, 4 * TILE...  8.47 us
  transfers between devices with their start and end apart: 14, of which 8 were waited for; matrix products, arithmetic and copies ran while one was open for 0% of the time, Pallas kernels for 7%

profile of v3, /device:TPU:87, one launch (start us, length us, event | category | flops | bytes accessed | tf_op | source)
XLA Modules:
  0.0 148.6 jit_solution(3240983736923373798)
XLA Ops:
  0.7 0.7 copy-done.3
  1.4 1.0 copy-done
  2.5 1.3 shard_map.64
  3.8 1.7 %collective-permute-start = (f32[264,256]{1,0:T(8,128)S(1)}, f32[264,256]{1,0:T(8,128)S(1)}, u32[]{:S(2)}, u32[]{:S(2)}) collective-permute-start(f32[264,256]{1,0:T(8,128)S(1)} %get-tuple-element.26), channel_id=1, source_target_pairs={{0,32},{32,0},{64,96},{96,64},{128,160},{160,128},{192,224},{224,1... | collective-permute-start | bytes 811016 | tf_op jit(solution)/shard_map/ppermute | solution.py:40
  5.5 2.0 %collective-permute-start.1 = (f32[264,256]{1,0:T(8,128)S(1)}, f32[264,256]{1,0:T(8,128)S(1)}, u32[]{:S(2)}, u32[]{:S(2)}) collective-permute-start(f32[264,256]{1,0:T(8,128)S(1)} %get-tuple-element.27), channel_id=1, source_target_pairs={{32,64},{64,32},{96,128},{128,96},{160,192},{192,160},{33,65},{65,... | collective-permute-start | bytes 811016 | tf_op jit(solution)/shard_map/ppermute | solution.py:40
  7.5 4.0 %collective-permute-done.row_a = f32[264,256]{1,0:T(8,128)S(1)} collective-permute-done((f32[264,256]{1,0:T(8,128)S(1)}, f32[264,256]{1,0:T(8,128)S(1)}, u32[]{:S(2)}, u32[]{:S(2)}) %collective-permute-start) | collective-permute-done | bytes 270368 | tf_op jit(solution)/shard_map/ppermute | solution.py:40
  11.6 5.7 %collective-permute-done.1.row_b = f32[264,256]{1,0:T(8,128)S(1)} collective-permute-done((f32[264,256]{1,0:T(8,128)S(1)}, f32[264,256]{1,0:T(8,128)S(1)}, u32[]{:S(2)}, u32[]{:S(2)}) %collective-permute-start.1) | collective-permute-done | bytes 270368 | tf_op jit(solution)/shard_map/ppermute | solution.py:40
  17.2 1.2 shard_map.67
  18.4 1.3 collective-permute-start.2
  19.8 0.6 shard_map.66
  20.4 5.9 %collective-permute-start.3 = (f32[1032,128]{1,0:T(8,128)S(1)}, f32[1032,128]{1,0:T(8,128)S(1)}, u32[]{:S(2)}, u32[]{:S(2)}) collective-permute-start(f32[1032,128]{1,0:T(8,128)S(1)} %get-tuple-element.30), channel_id=1, source_target_pairs={{1,2},{2,1},{3,4},{4,3},{5,6},{6,5},{7,8},{8,7},{9,10},{10,9},{11,... | collective-permute-start | bytes 1585160 | tf_op jit(solution)/shard_map/ppermute | solution.py:40
  26.3 0.6 shard_map.65.center
  26.9 14.0 %collective-permute-done.3.col_2 = f32[1032,128]{1,0:T(8,128)S(1)} collective-permute-done((f32[1032,128]{1,0:T(8,128)S(1)}, f32[1032,128]{1,0:T(8,128)S(1)}, u32[]{:S(2)}, u32[]{:S(2)}) %collective-permute-start.3) | collective-permute-done | bytes 528416 | tf_op jit(solution)/shard_map/ppermute | solution.py:40
  41.0 6.2 %shard_map.68 = (f32[2,512,256]{2,1,0:T(8,128)S(1)}, f32[1024,128]{1,0:T(8,128)S(1)}, f32[1024,128]{1,0:T(8,128)S(1)}, s32[24,128]{1,0:T(8,128)S(1)}) custom-call(s32[4]{0:T(128)S(1)} %pad_add_fusion.place, s32[2,6]{1,0:T(2,128)S(1)} %bitcast.9, s32[1,1]{1,0:T(1,128)S(6)} %copy.7.cnt, f32[8,128]{1,0:T(8,128)S(1)} %get-tuple-element.28.meta, ...), custom_call_target="tpu_custom_call" | custom-call | flops 3221225472 | bytes 6291456 | tf_op jit(solution)/shard_map/pallas_call | solution.py:363
  47.2 5.7 %collective-permute-start.4 = (f32[1024,128]{1,0:T(8,128)S(1)}, f32[1024,128]{1,0:T(8,128)S(1)}, u32[]{:S(2)}, u32[]{:S(2)}) collective-permute-start(f32[1024,128]{1,0:T(8,128)S(1)} %get-tuple-element.32), channel_id=1, source_target_pairs={{1,2},{2,1},{3,4},{4,3},{5,6},{6,5},{7,8},{8,7},{9,10},{10,9},{11,... | collective-permute-start | bytes 1572872 | tf_op jit(solution)/shard_map/ppermute | solution.py:40
  53.0 16.8 %collective-permute-done.4.col_b = f32[1024,128]{1,0:T(8,128)S(1)} collective-permute-done((f32[1024,128]{1,0:T(8,128)S(1)}, f32[1024,128]{1,0:T(8,128)S(1)}, u32[]{:S(2)}, u32[]{:S(2)}) %collective-permute-start.4) | collective-permute-done | bytes 524320 | tf_op jit(solution)/shard_map/ppermute | solution.py:40
  69.8 0.8 shard_map.69
  70.7 1.9 %collective-permute-start.7 = (f32[2,256,256]{2,1,0:T(8,128)S(1)}, f32[2,256,256]{2,1,0:T(8,128)S(1)}, u32[]{:S(2)}, u32[]{:S(2)}) collective-permute-start(f32[2,256,256]{2,1,0:T(8,128)S(1)} %get-tuple-element.36), channel_id=1, source_target_pairs={{32,64},{64,32},{96,128},{128,96},{160,192},{192,160},{33,65},{65,... | collective-permute-start | bytes 1572872 | tf_op jit(solution)/shard_map/ppermute | solution.py:40
  72.7 8.5 %shard_map.70.scale = f32[512,256]{1,0:T(8,128)S(1)} custom-call(s32[24,128]{1,0:T(8,128)S(1)} %get-tuple-element.37.metas, f32[2,256,256]{2,1,0:T(8,128)S(1)} %copy-done.2), custom_call_target="tpu_custom_call" | custom-call | bytes 12582912 | tf_op jit(solution)/shard_map/pallas_call | solution.py:384
  81.2 5.6 %collective-permute-done.7.row_b = f32[2,256,256]{2,1,0:T(8,128)S(1)} collective-permute-done((f32[2,256,256]{2,1,0:T(8,128)S(1)}, f32[2,256,256]{2,1,0:T(8,128)S(1)}, u32[]{:S(2)}, u32[]{:S(2)}) %collective-permute-start.7) | collective-permute-done | bytes 524320 | tf_op jit(solution)/shard_map/ppermute | solution.py:40
  86.7 0.9 shard_map.71
  87.6 4.9 %collective-permute-start.8 = (f32[1024,128]{1,0:T(8,128)S(1)}, f32[1024,128]{1,0:T(8,128)S(1)}, u32[]{:S(2)}, u32[]{:S(2)}) collective-permute-start(f32[1024,128]{1,0:T(8,128)S(1)} %get-tuple-element.39), channel_id=1, source_target_pairs={{1,2},{2,1},{3,4},{4,3},{5,6},{6,5},{7,8},{8,7},{9,10},{10,9},{11,... | collective-permute-start | bytes 1572872 | tf_op jit(solution)/shard_map/ppermute | solution.py:40
  92.5 0.3 collective-permute-start.9
  92.8 9.6 %collective-permute-done.8.col_1 = f32[1024,128]{1,0:T(8,128)S(1)} collective-permute-done((f32[1024,128]{1,0:T(8,128)S(1)}, f32[1024,128]{1,0:T(8,128)S(1)}, u32[]{:S(2)}, u32[]{:S(2)}) %collective-permute-start.8) | collective-permute-done | bytes 524320 | tf_op jit(solution)/shard_map/ppermute | solution.py:40
  102.4 6.2 %shard_map.72 = (f32[2,512,256]{2,1,0:T(8,128)S(1)}, f32[1024,128]{1,0:T(8,128)S(1)}, f32[1024,128]{1,0:T(8,128)S(1)}) custom-call(s32[4]{0:T(128)S(1)} %pad_add_fusion.place, s32[2,6]{1,0:T(2,128)S(1)} %bitcast.10, s32[1,1]{1,0:T(1,128)S(6)} %copy.7.cnt, f32[8,128]{1,0:T(8,128)S(1)} %get-tuple-element.28.meta, f32[2,512,256]{2,1,0:T(8,128)S(1)} %get-tuple-element.38.center, ...), custom_call_target="tpu_custom_call" | custom-call | flops 3221225472 | bytes 6291456 | tf_op jit(solution)/shard_map/pallas_call | solution.py:363
  108.6 7.8 %collective-permute-start.10 = (f32[1024,128]{1,0:T(8,128)S(1)}, f32[1024,128]{1,0:T(8,128)S(1)}, u32[]{:S(2)}, u32[]{:S(2)}) collective-permute-start(f32[1024,128]{1,0:T(8,128)S(1)} %get-tuple-element.42), channel_id=1, source_target_pairs={{1,2},{2,1},{3,4},{4,3},{5,6},{6,5},{7,8},{8,7},{9,10},{10,9},{11,... | collective-permute-start | bytes 1572872 | tf_op jit(solution)/shard_map/ppermute | solution.py:40
  116.6 15.3 %collective-permute-done.10.col_b = f32[1024,128]{1,0:T(8,128)S(1)} collective-permute-done((f32[1024,128]{1,0:T(8,128)S(1)}, f32[1024,128]{1,0:T(8,128)S(1)}, u32[]{:S(2)}, u32[]{:S(2)}) %collective-permute-start.10) | collective-permute-done | bytes 524320 | tf_op jit(solution)/shard_map/ppermute | solution.py:40
  131.9 0.8 shard_map.73
  132.7 4.8 %collective-permute-start.12 = (f32[2,128,256]{2,1,0:T(8,128)S(1)}, f32[2,128,256]{2,1,0:T(8,128)S(1)}, u32[]{:S(2)}, u32[]{:S(2)}) collective-permute-start(f32[2,128,256]{2,1,0:T(8,128)S(1)} %get-tuple-element.45), channel_id=1, source_target_pairs={{0,32},{32,0},{64,96},{96,64},{128,160},{160,128},{192,224},{224,1... | collective-permute-start | bytes 786440 | tf_op jit(solution)/shard_map/ppermute | solution.py:40
  137.5 4.9 %collective-permute-start.13 = (f32[2,128,256]{2,1,0:T(8,128)S(1)}, f32[2,128,256]{2,1,0:T(8,128)S(1)}, u32[]{:S(2)}, u32[]{:S(2)}) collective-permute-start(f32[2,128,256]{2,1,0:T(8,128)S(1)} %get-tuple-element.46), channel_id=1, source_target_pairs={{32,64},{64,32},{96,128},{128,96},{160,192},{192,160},{33,65},{65,... | collective-permute-start | bytes 786440 | tf_op jit(solution)/shard_map/ppermute | solution.py:40
  142.4 4.6 %collective-permute-done.13.row_b = f32[2,128,256]{2,1,0:T(8,128)S(1)} collective-permute-done((f32[2,128,256]{2,1,0:T(8,128)S(1)}, f32[2,128,256]{2,1,0:T(8,128)S(1)}, u32[]{:S(2)}, u32[]{:S(2)}) %collective-permute-start.13) | collective-permute-done | bytes 262176 | tf_op jit(solution)/shard_map/ppermute | solution.py:40
  147.0 1.4 shard_map.74
  (18 shorter events, 0.4 us)
Async XLA Ops:
  0.7 0.7 copy-start.3
  1.4 1.0 copy-start
  3.8 7.8 %collective-permute-start = (f32[264,256]{1,0:T(8,128)S(1)}, f32[264,256]{1,0:T(8,128)S(1)}, u32[]{:S(2)}, u32[]{:S(2)}) collective-permute-start(f32[264,256]{1,0:T(8,128)S(1)} %get-tuple-element.26), channel_id=1, source_target_pairs={{0,32},{32,0},{64,96},{96,64},{128,160},{160,128},{192,224},{224,1... | collective-permute-start | bytes 811016 | tf_op jit(solution)/shard_map/ppermute | solution.py:40
  5.5 20.8 %copy-start.1 = (bf16[1024,512]{1,0:T(8,128)(2,1)S(1)}, bf16[1024,512]{1,0:T(8,128)(2,1)}, u32[]{:S(2)}) copy-start(bf16[1024,512]{1,0:T(8,128)(2,1)} %constant.15.clone.tables) | copy-start | bytes 3145732
  5.5 11.8 %collective-permute-start.1 = (f32[264,256]{1,0:T(8,128)S(1)}, f32[264,256]{1,0:T(8,128)S(1)}, u32[]{:S(2)}, u32[]{:S(2)}) collective-permute-start(f32[264,256]{1,0:T(8,128)S(1)} %get-tuple-element.27), channel_id=1, source_target_pairs={{32,64},{64,32},{96,128},{128,96},{160,192},{192,160},{33,65},{65,... | collective-permute-start | bytes 811016 | tf_op jit(solution)/shard_map/ppermute | solution.py:40
  18.4 8.5 %collective-permute-start.2 = (f32[1032,128]{1,0:T(8,128)S(1)}, f32[1032,128]{1,0:T(8,128)S(1)}, u32[]{:S(2)}, u32[]{:S(2)}) collective-permute-start(f32[1032,128]{1,0:T(8,128)S(1)} %get-tuple-element.29), channel_id=1, source_target_pairs={{0,1},{1,0},{2,3},{3,2},{4,5},{5,4},{6,7},{7,6},{8,9},{9,8},{10,11... | collective-permute-start | bytes 1585160 | tf_op jit(solution)/shard_map/ppermute | solution.py:40
  20.4 20.6 %copy-start.2 = (f32[2,256,256]{2,1,0:T(8,128)S(1)}, f32[2,256,256]{2,1,0:T(8,128)}, u32[]{:S(2)}) copy-start(f32[2,256,256]{2,1,0:T(8,128)} %probe.5) | copy-start | bytes 1572868
  20.4 20.6 %copy-start.4 = (bf16[1,1,6,256,256]{4,3,2,1,0:T(8,128)(2,1)S(1)}, bf16[1,1,6,256,256]{4,3,2,1,0:T(8,128)(2,1)}, u32[]{:S(2)}) copy-start(bf16[1,1,6,256,256]{4,3,2,1,0:T(8,128)(2,1)} %param.8) | copy-start | bytes 2359300
  20.4 20.6 %collective-permute-start.3 = (f32[1032,128]{1,0:T(8,128)S(1)}, f32[1032,128]{1,0:T(8,128)S(1)}, u32[]{:S(2)}, u32[]{:S(2)}) collective-permute-start(f32[1032,128]{1,0:T(8,128)S(1)} %get-tuple-element.30), channel_id=1, source_target_pairs={{1,2},{2,1},{3,4},{4,3},{5,6},{6,5},{7,8},{8,7},{9,10},{10,9},{11,... | collective-permute-start | bytes 1585160 | tf_op jit(solution)/shard_map/ppermute | solution.py:40
  47.2 22.6 %collective-permute-start.4 = (f32[1024,128]{1,0:T(8,128)S(1)}, f32[1024,128]{1,0:T(8,128)S(1)}, u32[]{:S(2)}, u32[]{:S(2)}) collective-permute-start(f32[1024,128]{1,0:T(8,128)S(1)} %get-tuple-element.32), channel_id=1, source_target_pairs={{1,2},{2,1},{3,4},{4,3},{5,6},{6,5},{7,8},{8,7},{9,10},{10,9},{11,... | collective-permute-start | bytes 1572872 | tf_op jit(solution)/shard_map/ppermute | solution.py:40
  52.9 16.9 %collective-permute-start.5 = (f32[1024,128]{1,0:T(8,128)S(1)}, f32[1024,128]{1,0:T(8,128)S(1)}, u32[]{:S(2)}, u32[]{:S(2)}) collective-permute-start(f32[1024,128]{1,0:T(8,128)S(1)} %get-tuple-element.33), channel_id=1, source_target_pairs={{0,1},{1,0},{2,3},{3,2},{4,5},{5,4},{6,7},{7,6},{8,9},{9,8},{10,11... | collective-permute-start | bytes 1572872 | tf_op jit(solution)/shard_map/ppermute | solution.py:40
  70.6 10.5 %collective-permute-start.6 = (f32[2,256,256]{2,1,0:T(8,128)S(1)}, f32[2,256,256]{2,1,0:T(8,128)S(1)}, u32[]{:S(2)}, u32[]{:S(2)}) collective-permute-start(f32[2,256,256]{2,1,0:T(8,128)S(1)} %get-tuple-element.35), channel_id=1, source_target_pairs={{0,32},{32,0},{64,96},{96,64},{128,160},{160,128},{192,224},{224,1... | collective-permute-start | bytes 1572872 | tf_op jit(solution)/shard_map/ppermute | solution.py:40
  70.7 16.0 %collective-permute-start.7 = (f32[2,256,256]{2,1,0:T(8,128)S(1)}, f32[2,256,256]{2,1,0:T(8,128)S(1)}, u32[]{:S(2)}, u32[]{:S(2)}) collective-permute-start(f32[2,256,256]{2,1,0:T(8,128)S(1)} %get-tuple-element.36), channel_id=1, source_target_pairs={{32,64},{64,32},{96,128},{128,96},{160,192},{192,160},{33,65},{65,... | collective-permute-start | bytes 1572872 | tf_op jit(solution)/shard_map/ppermute | solution.py:40
  87.6 14.8 %collective-permute-start.8 = (f32[1024,128]{1,0:T(8,128)S(1)}, f32[1024,128]{1,0:T(8,128)S(1)}, u32[]{:S(2)}, u32[]{:S(2)}) collective-permute-start(f32[1024,128]{1,0:T(8,128)S(1)} %get-tuple-element.39), channel_id=1, source_target_pairs={{1,2},{2,1},{3,4},{4,3},{5,6},{6,5},{7,8},{8,7},{9,10},{10,9},{11,... | collective-permute-start | bytes 1572872 | tf_op jit(solution)/shard_map/ppermute | solution.py:40
  92.5 9.9 %collective-permute-start.9 = (f32[1024,128]{1,0:T(8,128)S(1)}, f32[1024,128]{1,0:T(8,128)S(1)}, u32[]{:S(2)}, u32[]{:S(2)}) collective-permute-start(f32[1024,128]{1,0:T(8,128)S(1)} %get-tuple-element.40), channel_id=1, source_target_pairs={{0,1},{1,0},{2,3},{3,2},{4,5},{5,4},{6,7},{7,6},{8,9},{9,8},{10,11... | collective-permute-start | bytes 1572872 | tf_op jit(solution)/shard_map/ppermute | solution.py:40
  108.6 23.2 %collective-permute-start.10 = (f32[1024,128]{1,0:T(8,128)S(1)}, f32[1024,128]{1,0:T(8,128)S(1)}, u32[]{:S(2)}, u32[]{:S(2)}) collective-permute-start(f32[1024,128]{1,0:T(8,128)S(1)} %get-tuple-element.42), channel_id=1, source_target_pairs={{1,2},{2,1},{3,4},{4,3},{5,6},{6,5},{7,8},{8,7},{9,10},{10,9},{11,... | collective-permute-start | bytes 1572872 | tf_op jit(solution)/shard_map/ppermute | solution.py:40
  116.5 15.4 %collective-permute-start.11 = (f32[1024,128]{1,0:T(8,128)S(1)}, f32[1024,128]{1,0:T(8,128)S(1)}, u32[]{:S(2)}, u32[]{:S(2)}) collective-permute-start(f32[1024,128]{1,0:T(8,128)S(1)} %get-tuple-element.43), channel_id=1, source_target_pairs={{0,1},{1,0},{2,3},{3,2},{4,5},{5,4},{6,7},{7,6},{8,9},{9,8},{10,11... | collective-permute-start | bytes 1572872 | tf_op jit(solution)/shard_map/ppermute | solution.py:40
  132.7 9.7 %collective-permute-start.12 = (f32[2,128,256]{2,1,0:T(8,128)S(1)}, f32[2,128,256]{2,1,0:T(8,128)S(1)}, u32[]{:S(2)}, u32[]{:S(2)}) collective-permute-start(f32[2,128,256]{2,1,0:T(8,128)S(1)} %get-tuple-element.45), channel_id=1, source_target_pairs={{0,32},{32,0},{64,96},{96,64},{128,160},{160,128},{192,224},{224,1... | collective-permute-start | bytes 786440 | tf_op jit(solution)/shard_map/ppermute | solution.py:40
  137.5 9.6 %collective-permute-start.13 = (f32[2,128,256]{2,1,0:T(8,128)S(1)}, f32[2,128,256]{2,1,0:T(8,128)S(1)}, u32[]{:S(2)}, u32[]{:S(2)}) collective-permute-start(f32[2,128,256]{2,1,0:T(8,128)S(1)} %get-tuple-element.46), channel_id=1, source_target_pairs={{32,64},{64,32},{96,128},{128,96},{160,192},{192,160},{33,65},{65,... | collective-permute-start | bytes 786440 | tf_op jit(solution)/shard_map/ppermute | solution.py:40

commit v4 on v2

--- a/solution.py
+++ b/solution.py
@@ -73,34 +73,31 @@
         out[2 * RIM : 2 * RIM + 1, 12:13] = cnt[...].astype(jnp.float32)
 
 
-def pack_cols_kernel(place, obj, row_a, row_b, offs, cnt, a_out, b_out, meta):
+def pack_cols_kernel(near, place, obj, row_a, row_b, offs, cnt, out, *meta_out):
     row_odd = place[0] & 1
     a_at = (1 - row_odd) * (RIM + TILE)
     b_at = row_odd * (RIM + TILE)
-    even = (place[1] & 1) == 0
-    for p in range(2):
-        mine = obj[p]
-        pieces = [(mine, p * EXT + RIM, TILE)]
+    high_side = (place[1] & 1) == (0 if near else 1)
+    for p in range(2):
+        pieces = [(obj[p], p * EXT + RIM, TILE)]
         for row, at in ((row_a, a_at), (row_b, b_at)):
             pieces.append((row[p * RIM : (p + 1) * RIM, :], aligned(p * EXT + at, RIM), RIM))
         for piece, at, size in pieces:
-            low = piece[:, 0:LANES]
-            high = piece[:, LANES:TILE]
-            a_out[pl.ds(at, size), :] = jnp.where(even, high, low)
-            b_out[pl.ds(at, size), :] = jnp.where(even, low, high)
+            out[pl.ds(at, size), :] = jnp.where(high_side, piece[:, LANES:TILE], piece[:, 0:LANES])
     meta_a = row_a[2 * RIM : 2 * RIM + 1, 0:LANES]
     meta_b = row_b[2 * RIM : 2 * RIM + 1, 0:LANES]
     odd = row_odd == 1
-    meta[...] = jnp.zeros_like(meta)
+    meta = out.at[2 * EXT :, :]
+    meta[...] = jnp.zeros((8, LANES), jnp.float32)
     meta[0:1, :] = jnp.where(odd, meta_a, meta_b)
     meta[1:2, 0:12] = offs[...].astype(jnp.float32)
     meta[1:2, 12:13] = cnt[...].astype(jnp.float32)
     meta[2:3, :] = jnp.where(odd, meta_b, meta_a)
-    a_out[2 * EXT :, :] = meta[...]
-    b_out[2 * EXT :, :] = meta[...]
-
-
-def center_kernel(place, obj, row_a, row_b, center):
+    for more in meta_out:
+        more[...] = meta[...]
+
+
+def center_kernel(place, obj, row_a, row_b, tables, center):
     row_odd = place[0] & 1
     a_at = aligned((1 - row_odd) * (RIM + TILE), RIM)
     b_at = aligned(row_odd * (RIM + TILE), RIM)
@@ -182,9 +179,10 @@
     slots = range(MAXPOS)
     rows, shifts, blocks = [], [], []
     for slot in slots:
-        col = offs[2 * slot + 1]
+        in_use = slot < cnt[0]
+        col = jnp.where(in_use, offs[2 * slot + 1], 0)
         block = col // LANES
-        rows.append(pl.ds(offs[2 * slot], TILE))
+        rows.append(pl.ds(jnp.where(in_use, offs[2 * slot], 0), TILE))
         shifts.append(col - block * LANES)
         blocks.append([block, block + 1, jnp.minimum(block + 2, 3)])
     for slot in slots:
@@ -318,11 +316,15 @@
     )
     row_a, row_b = swaps(strips, "row")
     col_strip = f32(2 * EXT + 8, LANES)
-    a, b, meta = call(pack_cols_kernel, (col_strip, col_strip, f32(8, LANES)), [SMEM] + [VMEM] * 5)(
-        place, object_field, row_a, row_b, offs, cnt
-    )
-    center = call(center_kernel, f32(2, EXT, TILE), [SMEM] + [VMEM] * 3, bytes_accessed=4 << 20)(
-        place, object_field, row_a, row_b
+    def pack_cols(near, *more):
+        return call(
+            functools.partial(pack_cols_kernel, near), (col_strip,) + more, [SMEM] + [VMEM] * 5
+        )(place, object_field, row_a, row_b, offs, cnt)
+
+    (a,) = pack_cols(True)
+    b, meta = pack_cols(False, f32(8, LANES))
+    center = call(center_kernel, f32(2, EXT, TILE), [SMEM] + [VMEM] * 4, bytes_accessed=4 << 20)(
+        place, object_field, row_a, row_b, tables
     )
     col_a, col_b = swaps((a, b), "col")
 

time: 146 us -> 145 us (level)
  waiting for transfers between devices: 74.3 us -> 69.3 us
  starting transfers between devices: 41 us -> 44.6 us
  Pallas kernels: 26.1 us -> 28.9 us
    ppermute x14, waiting for transfers between devices: 74.3 us -> 69.3 us  [swap(): return lax.ppermute(value, axis, pairs)]
    ppermute x14, starting transfers between devices: 41 us -> 44.6 us  [swap(): return lax.ppermute(value, axis, pairs)]
    pallas_call x2 -> x3, Pallas kernels: 1.31 us -> 2.77 us  [the longest x2 2.15 us: pack_cols(): call(functools.partial(pack_cols_kernel, near), (col_strip,) + more, [SME...]
  transfers between devices with their start and end apart: 14 -> 14, of which waited for: 10 -> 10; matrix products, arithmetic and copies ran while one was open for 0% -> 0% of each run, Pallas kernels for 6% -> 7%
where the time goes in v4:
time: 145 us
  waiting for transfers between devices  69.3 us (48%)
  starting transfers between devices  44.6 us (31%)
  Pallas kernels  28.9 us (20%)
    ppermute x14, waiting for transfers between devices, swap(): return lax.ppermute(value, axis, pairs)  69.3 us
    ppermute x14, starting transfers between devices, swap(): return lax.ppermute(value, axis, pairs)  44.6 us
    pallas_call x2, Pallas kernels, iterate(): call(functools.partial(iterate_kernel, first), outs, [SMEM] * 3 + [VMEM]...  12.5 us
    pallas_call x1, Pallas kernels, per_device(): call(light_kernel, f32(EXT, TILE), [SMEM, VMEM], [pltpu.VMEM((2, 4 * TILE...  9.13 us
  transfers between devices with their start and end apart: 14, of which 10 were waited for; matrix products, arithmetic and copies ran while one was open for 0% of the time, Pallas kernels for 7%

profile of v4, /device:TPU:87, one launch (start us, length us, event | category | flops | bytes accessed | tf_op | source)
XLA Modules:
  0.0 145.1 jit_solution(1713953854016428840)
XLA Ops:
  0.9 1.0 copy-done
  2.0 0.6 shard_map.64
  2.6 1.7 %collective-permute-start = (f32[264,256]{1,0:T(8,128)S(1)}, f32[264,256]{1,0:T(8,128)S(1)}, u32[]{:S(2)}, u32[]{:S(2)}) collective-permute-start(f32[264,256]{1,0:T(8,128)S(1)} %get-tuple-element.25), channel_id=1, source_target_pairs={{0,32},{32,0},{64,96},{96,64},{128,160},{160,128},{192,224},{224,1... | collective-permute-start | bytes 811016 | tf_op jit(solution)/shard_map/ppermute | solution.py:40
  4.3 1.9 %collective-permute-start.1 = (f32[264,256]{1,0:T(8,128)S(1)}, f32[264,256]{1,0:T(8,128)S(1)}, u32[]{:S(2)}, u32[]{:S(2)}) collective-permute-start(f32[264,256]{1,0:T(8,128)S(1)} %get-tuple-element.26), channel_id=1, source_target_pairs={{32,64},{64,32},{96,128},{128,96},{160,192},{192,160},{33,65},{65,... | collective-permute-start | bytes 811016 | tf_op jit(solution)/shard_map/ppermute | solution.py:40
  6.2 4.2 %collective-permute-done.row_a = f32[264,256]{1,0:T(8,128)S(1)} collective-permute-done((f32[264,256]{1,0:T(8,128)S(1)}, f32[264,256]{1,0:T(8,128)S(1)}, u32[]{:S(2)}, u32[]{:S(2)}) %collective-permute-start) | collective-permute-done | bytes 270368 | tf_op jit(solution)/shard_map/ppermute | solution.py:40
  10.4 5.7 %collective-permute-done.1.row_b = f32[264,256]{1,0:T(8,128)S(1)} collective-permute-done((f32[264,256]{1,0:T(8,128)S(1)}, f32[264,256]{1,0:T(8,128)S(1)}, u32[]{:S(2)}, u32[]{:S(2)}) %collective-permute-start.1) | collective-permute-done | bytes 270368 | tf_op jit(solution)/shard_map/ppermute | solution.py:40
  16.1 1.5 %shard_map.66 = (f32[1032,128]{1,0:T(8,128)}, f32[8,128]{1,0:T(8,128)S(1)}) custom-call(s32[4]{0:T(128)S(1)} %pad_add_fusion.place, f32[2,256,256]{2,1,0:T(8,128)S(1)} %copy-done, f32[264,256]{1,0:T(8,128)S(1)} %collective-permute-done.row_a, f32[264,256]{1,0:T(8,128)S(1)} %collective-permute-done.1.row_b, s32[1,12]{1,0:T(1,128)S(1)} %reshape.12.offs, ...), custom_call_target="tpu_custom_call" | custom-call | bytes 1048576 | tf_op jit(solution)/shard_map/pallas_call | solution.py:320
  17.5 7.2 %collective-permute-start.3 = (f32[1032,128]{1,0:T(8,128)}, f32[1032,128]{1,0:T(8,128)S(1)}, u32[]{:S(2)}, u32[]{:S(2)}) collective-permute-start(f32[1032,128]{1,0:T(8,128)} %get-tuple-element.28), channel_id=1, source_target_pairs={{1,2},{2,1},{3,4},{4,3},{5,6},{6,5},{7,8},{8,7},{9,10},{10,9},{11,... | collective-permute-start | bytes 1585160 | tf_op jit(solution)/shard_map/ppermute | solution.py:40
  24.8 0.7 shard_map.67
  25.6 0.6 shard_map.65.center
  26.2 12.1 %collective-permute-done.3.col_b = f32[1032,128]{1,0:T(8,128)S(1)} collective-permute-done((f32[1032,128]{1,0:T(8,128)}, f32[1032,128]{1,0:T(8,128)S(1)}, u32[]{:S(2)}, u32[]{:S(2)}) %collective-permute-start.3) | collective-permute-done | bytes 528416 | tf_op jit(solution)/shard_map/ppermute | solution.py:40
  38.3 6.5 %shard_map.68 = (f32[2,512,256]{2,1,0:T(8,128)S(1)}, f32[1024,128]{1,0:T(8,128)S(1)}, f32[1024,128]{1,0:T(8,128)S(1)}, s32[24,128]{1,0:T(8,128)S(1)}) custom-call(s32[4]{0:T(128)S(1)} %pad_add_fusion.place, s32[12]{0:T(128)S(1)} %reshape.13.offs, s32[1]{0:T(128)} %bitcast.4.cnt, f32[8,128]{1,0:T(8,128)S(1)} %get-tuple-element.27.meta, ...), custom_call_target="tpu_custom_call" | custom-call | flops 3221225472 | bytes 6291456 | tf_op jit(solution)/shard_map/pallas_call | solution.py:339
  44.9 7.0 %collective-permute-start.5 = (f32[1024,128]{1,0:T(8,128)S(1)}, f32[1024,128]{1,0:T(8,128)S(1)}, u32[]{:S(2)}, u32[]{:S(2)}) collective-permute-start(f32[1024,128]{1,0:T(8,128)S(1)} %get-tuple-element.31), channel_id=1, source_target_pairs={{1,2},{2,1},{3,4},{4,3},{5,6},{6,5},{7,8},{8,7},{9,10},{10,9},{11,... | collective-permute-start | bytes 1572872 | tf_op jit(solution)/shard_map/ppermute | solution.py:40
  51.9 14.5 %collective-permute-done.5.col_b = f32[1024,128]{1,0:T(8,128)S(1)} collective-permute-done((f32[1024,128]{1,0:T(8,128)S(1)}, f32[1024,128]{1,0:T(8,128)S(1)}, u32[]{:S(2)}, u32[]{:S(2)}) %collective-permute-start.5) | collective-permute-done | bytes 524320 | tf_op jit(solution)/shard_map/ppermute | solution.py:40
  66.4 0.8 shard_map.69
  67.3 0.1 collective-permute-start.6
  67.4 1.9 %collective-permute-start.7 = (f32[2,256,256]{2,1,0:T(8,128)S(1)}, f32[2,256,256]{2,1,0:T(8,128)S(1)}, u32[]{:S(2)}, u32[]{:S(2)}) collective-permute-start(f32[2,256,256]{2,1,0:T(8,128)S(1)} %get-tuple-element.34), channel_id=1, source_target_pairs={{32,64},{64,32},{96,128},{128,96},{160,192},{192,160},{33,65},{65,... | collective-permute-start | bytes 1572872 | tf_op jit(solution)/shard_map/ppermute | solution.py:40
  69.3 9.1 %shard_map.70.scale = f32[512,256]{1,0:T(8,128)S(1)} custom-call(s32[24,128]{1,0:T(8,128)S(1)} %get-tuple-element.35.metas, f32[2,256,256]{2,1,0:T(8,128)S(1)} %copy-done.3), custom_call_target="tpu_custom_call" | custom-call | bytes 12582912 | tf_op jit(solution)/shard_map/pallas_call | solution.py:360
  78.4 0.4 collective-permute-done.6.row_a
  78.9 5.6 %collective-permute-done.7.row_b = f32[2,256,256]{2,1,0:T(8,128)S(1)} collective-permute-done((f32[2,256,256]{2,1,0:T(8,128)S(1)}, f32[2,256,256]{2,1,0:T(8,128)S(1)}, u32[]{:S(2)}, u32[]{:S(2)}) %collective-permute-start.7) | collective-permute-done | bytes 524320 | tf_op jit(solution)/shard_map/ppermute | solution.py:40
  84.5 0.8 shard_map.71
  85.4 5.8 %collective-permute-start.9 = (f32[1024,128]{1,0:T(8,128)S(1)}, f32[1024,128]{1,0:T(8,128)S(1)}, u32[]{:S(2)}, u32[]{:S(2)}) collective-permute-start(f32[1024,128]{1,0:T(8,128)S(1)} %get-tuple-element.38), channel_id=1, source_target_pairs={{1,2},{2,1},{3,4},{4,3},{5,6},{6,5},{7,8},{8,7},{9,10},{10,9},{11,... | collective-permute-start | bytes 1572872 | tf_op jit(solution)/shard_map/ppermute | solution.py:40
  91.3 9.0 %collective-permute-done.9.col_b = f32[1024,128]{1,0:T(8,128)S(1)} collective-permute-done((f32[1024,128]{1,0:T(8,128)S(1)}, f32[1024,128]{1,0:T(8,128)S(1)}, u32[]{:S(2)}, u32[]{:S(2)}) %collective-permute-start.9) | collective-permute-done | bytes 524320 | tf_op jit(solution)/shard_map/ppermute | solution.py:40
  100.3 6.0 %shard_map.72 = (f32[2,512,256]{2,1,0:T(8,128)S(1)}, f32[1024,128]{1,0:T(8,128)S(1)}, f32[1024,128]{1,0:T(8,128)S(1)}) custom-call(s32[4]{0:T(128)S(1)} %pad_add_fusion.place, s32[12]{0:T(128)S(1)} %reshape.13.offs, s32[1]{0:T(128)} %bitcast.5.cnt, f32[8,128]{1,0:T(8,128)S(1)} %get-tuple-element.27.meta, f32[2,512,256]{2,1,0:T(8,128)S(1)} %get-tuple-element.36.center, ...), custom_call_target="tpu_custom_call" | custom-call | flops 3221225472 | bytes 6291456 | tf_op jit(solution)/shard_map/pallas_call | solution.py:339
  106.3 6.0 %collective-permute-start.11 = (f32[1024,128]{1,0:T(8,128)S(1)}, f32[1024,128]{1,0:T(8,128)S(1)}, u32[]{:S(2)}, u32[]{:S(2)}) collective-permute-start(f32[1024,128]{1,0:T(8,128)S(1)} %get-tuple-element.41), channel_id=1, source_target_pairs={{1,2},{2,1},{3,4},{4,3},{5,6},{6,5},{7,8},{8,7},{9,10},{10,9},{11,... | collective-permute-start | bytes 1572872 | tf_op jit(solution)/shard_map/ppermute | solution.py:40
  112.4 11.8 %collective-permute-done.11.col_b = f32[1024,128]{1,0:T(8,128)S(1)} collective-permute-done((f32[1024,128]{1,0:T(8,128)S(1)}, f32[1024,128]{1,0:T(8,128)S(1)}, u32[]{:S(2)}, u32[]{:S(2)}) %collective-permute-start.11) | collective-permute-done | bytes 524320 | tf_op jit(solution)/shard_map/ppermute | solution.py:40
  124.1 0.8 shard_map.73
  124.9 10.7 %collective-permute-start.12 = (f32[2,128,256]{2,1,0:T(8,128)S(1)}, f32[2,128,256]{2,1,0:T(8,128)S(1)}, u32[]{:S(2)}, u32[]{:S(2)}) collective-permute-start(f32[2,128,256]{2,1,0:T(8,128)S(1)} %get-tuple-element.43), channel_id=1, source_target_pairs={{0,32},{32,0},{64,96},{96,64},{128,160},{160,128},{192,224},{224,1... | collective-permute-start | bytes 786440 | tf_op jit(solution)/shard_map/ppermute | solution.py:40
  135.6 1.9 %collective-permute-start.13 = (f32[2,128,256]{2,1,0:T(8,128)S(1)}, f32[2,128,256]{2,1,0:T(8,128)S(1)}, u32[]{:S(2)}, u32[]{:S(2)}) collective-permute-start(f32[2,128,256]{2,1,0:T(8,128)S(1)} %get-tuple-element.44), channel_id=1, source_target_pairs={{32,64},{64,32},{96,128},{128,96},{160,192},{192,160},{33,65},{65,... | collective-permute-start | bytes 786440 | tf_op jit(solution)/shard_map/ppermute | solution.py:40
  137.5 1.8 %collective-permute-done.12.row_a = f32[2,128,256]{2,1,0:T(8,128)S(1)} collective-permute-done((f32[2,128,256]{2,1,0:T(8,128)S(1)}, f32[2,128,256]{2,1,0:T(8,128)S(1)}, u32[]{:S(2)}, u32[]{:S(2)}) %collective-permute-start.12) | collective-permute-done | bytes 262176 | tf_op jit(solution)/shard_map/ppermute | solution.py:40
  139.4 4.2 %collective-permute-done.13.row_b = f32[2,128,256]{2,1,0:T(8,128)S(1)} collective-permute-done((f32[2,128,256]{2,1,0:T(8,128)S(1)}, f32[2,128,256]{2,1,0:T(8,128)S(1)}, u32[]{:S(2)}, u32[]{:S(2)}) %collective-permute-start.13) | collective-permute-done | bytes 262176 | tf_op jit(solution)/shard_map/ppermute | solution.py:40
  143.6 1.5 %shard_map.74 = f32[2,256,256]{2,1,0:T(8,128)} custom-call(s32[4]{0:T(128)S(1)} %pad_add_fusion.place, f32[2,512,256]{2,1,0:T(8,128)S(1)} %get-tuple-element.36.center, f32[2,512,256]{2,1,0:T(8,128)S(1)} %get-tuple-element.42.total, f32[2,128,256]{2,1,0:T(8,128)S(1)} %collective-permute-done.12.row_a, f32[2,128,256]{2,1,0:T(8,128)S(1)} %collective-permute-done.13.row_b, ...), custom_call_target="tpu_custom_call" | custom-call | bytes 1048576 | tf_op jit(solution)/shard_map/pallas_call | solution.py:371
  (23 shorter events, 0.7 us)
Async XLA Ops:
  0.0 0.7 copy-start.5
  0.9 1.0 copy-start
  2.6 7.8 %collective-permute-start = (f32[264,256]{1,0:T(8,128)S(1)}, f32[264,256]{1,0:T(8,128)S(1)}, u32[]{:S(2)}, u32[]{:S(2)}) collective-permute-start(f32[264,256]{1,0:T(8,128)S(1)} %get-tuple-element.25), channel_id=1, source_target_pairs={{0,32},{32,0},{64,96},{96,64},{128,160},{160,128},{192,224},{224,1... | collective-permute-start | bytes 811016 | tf_op jit(solution)/shard_map/ppermute | solution.py:40
  4.3 11.8 %collective-permute-start.1 = (f32[264,256]{1,0:T(8,128)S(1)}, f32[264,256]{1,0:T(8,128)S(1)}, u32[]{:S(2)}, u32[]{:S(2)}) collective-permute-start(f32[264,256]{1,0:T(8,128)S(1)} %get-tuple-element.26), channel_id=1, source_target_pairs={{32,64},{64,32},{96,128},{128,96},{160,192},{192,160},{33,65},{65,... | collective-permute-start | bytes 811016 | tf_op jit(solution)/shard_map/ppermute | solution.py:40
  17.5 8.0 %copy-start.2 = (bf16[1024,512]{1,0:T(8,128)(2,1)S(1)}, bf16[1024,512]{1,0:T(8,128)(2,1)}, u32[]{:S(2)}) copy-start(bf16[1024,512]{1,0:T(8,128)(2,1)} %constant.15.clone.tables) | copy-start | bytes 3145732
  17.5 8.0 %copy-start.1 = (f32[2,256,256]{2,1,0:T(8,128)S(1)}, f32[2,256,256]{2,1,0:T(8,128)}, u32[]{:S(2)}) copy-start(f32[2,256,256]{2,1,0:T(8,128)} %obj.7) | copy-start | bytes 1572868
  17.5 20.8 %collective-permute-start.3 = (f32[1032,128]{1,0:T(8,128)}, f32[1032,128]{1,0:T(8,128)S(1)}, u32[]{:S(2)}, u32[]{:S(2)}) collective-permute-start(f32[1032,128]{1,0:T(8,128)} %get-tuple-element.28), channel_id=1, source_target_pairs={{1,2},{2,1},{3,4},{4,3},{5,6},{6,5},{7,8},{8,7},{9,10},{10,9},{11,... | collective-permute-start | bytes 1585160 | tf_op jit(solution)/shard_map/ppermute | solution.py:40
  25.4 12.9 %collective-permute-start.2 = (f32[1032,128]{1,0:T(8,128)S(1)}, f32[1032,128]{1,0:T(8,128)}, u32[]{:S(2)}, u32[]{:S(2)}) collective-permute-start(f32[1032,128]{1,0:T(8,128)S(1)} %shard_map.67), channel_id=1, source_target_pairs={{0,1},{1,0},{2,3},{3,2},{4,5},{5,4},{6,7},{7,6},{8,9},{9,8},{10,11... | collective-permute-start | bytes 1585160 | tf_op jit(solution)/shard_map/ppermute | solution.py:40
  25.6 12.8 %copy-start.3 = (f32[2,256,256]{2,1,0:T(8,128)S(1)}, f32[2,256,256]{2,1,0:T(8,128)}, u32[]{:S(2)}) copy-start(f32[2,256,256]{2,1,0:T(8,128)} %probe.5) | copy-start | bytes 1572868
  25.6 12.7 %copy-start.4 = (bf16[1,1,6,256,256]{4,3,2,1,0:T(8,128)(2,1)S(1)}, bf16[1,1,6,256,256]{4,3,2,1,0:T(8,128)(2,1)}, u32[]{:S(2)}) copy-start(bf16[1,1,6,256,256]{4,3,2,1,0:T(8,128)(2,1)} %param.8) | copy-start | bytes 2359300
  44.8 7.1 %collective-permute-start.4 = (f32[1024,128]{1,0:T(8,128)S(1)}, f32[1024,128]{1,0:T(8,128)S(1)}, u32[]{:S(2)}, u32[]{:S(2)}) collective-permute-start(f32[1024,128]{1,0:T(8,128)S(1)} %get-tuple-element.30), channel_id=1, source_target_pairs={{0,1},{1,0},{2,3},{3,2},{4,5},{5,4},{6,7},{7,6},{8,9},{9,8},{10,11... | collective-permute-start | bytes 1572872 | tf_op jit(solution)/shard_map/ppermute | solution.py:40
  44.9 21.5 %collective-permute-start.5 = (f32[1024,128]{1,0:T(8,128)S(1)}, f32[1024,128]{1,0:T(8,128)S(1)}, u32[]{:S(2)}, u32[]{:S(2)}) collective-permute-start(f32[1024,128]{1,0:T(8,128)S(1)} %get-tuple-element.31), channel_id=1, source_target_pairs={{1,2},{2,1},{3,4},{4,3},{5,6},{6,5},{7,8},{8,7},{9,10},{10,9},{11,... | collective-permute-start | bytes 1572872 | tf_op jit(solution)/shard_map/ppermute | solution.py:40
  67.3 11.6 %collective-permute-start.6 = (f32[2,256,256]{2,1,0:T(8,128)S(1)}, f32[2,256,256]{2,1,0:T(8,128)S(1)}, u32[]{:S(2)}, u32[]{:S(2)}) collective-permute-start(f32[2,256,256]{2,1,0:T(8,128)S(1)} %get-tuple-element.33), channel_id=1, source_target_pairs={{0,32},{32,0},{64,96},{96,64},{128,160},{160,128},{192,224},{224,1... | collective-permute-start | bytes 1572872 | tf_op jit(solution)/shard_map/ppermute | solution.py:40
  67.4 17.1 %collective-permute-start.7 = (f32[2,256,256]{2,1,0:T(8,128)S(1)}, f32[2,256,256]{2,1,0:T(8,128)S(1)}, u32[]{:S(2)}, u32[]{:S(2)}) collective-permute-start(f32[2,256,256]{2,1,0:T(8,128)S(1)} %get-tuple-element.34), channel_id=1, source_target_pairs={{32,64},{64,32},{96,128},{128,96},{160,192},{192,160},{33,65},{65,... | collective-permute-start | bytes 1572872 | tf_op jit(solution)/shard_map/ppermute | solution.py:40
  85.3 5.9 %collective-permute-start.8 = (f32[1024,128]{1,0:T(8,128)S(1)}, f32[1024,128]{1,0:T(8,128)S(1)}, u32[]{:S(2)}, u32[]{:S(2)}) collective-permute-start(f32[1024,128]{1,0:T(8,128)S(1)} %get-tuple-element.37), channel_id=1, source_target_pairs={{0,1},{1,0},{2,3},{3,2},{4,5},{5,4},{6,7},{7,6},{8,9},{9,8},{10,11... | collective-permute-start | bytes 1572872 | tf_op jit(solution)/shard_map/ppermute | solution.py:40
  85.4 14.8 %collective-permute-start.9 = (f32[1024,128]{1,0:T(8,128)S(1)}, f32[1024,128]{1,0:T(8,128)S(1)}, u32[]{:S(2)}, u32[]{:S(2)}) collective-permute-start(f32[1024,128]{1,0:T(8,128)S(1)} %get-tuple-element.38), channel_id=1, source_target_pairs={{1,2},{2,1},{3,4},{4,3},{5,6},{6,5},{7,8},{8,7},{9,10},{10,9},{11,... | collective-permute-start | bytes 1572872 | tf_op jit(solution)/shard_map/ppermute | solution.py:40
  106.2 6.1 %collective-permute-start.10 = (f32[1024,128]{1,0:T(8,128)S(1)}, f32[1024,128]{1,0:T(8,128)S(1)}, u32[]{:S(2)}, u32[]{:S(2)}) collective-permute-start(f32[1024,128]{1,0:T(8,128)S(1)} %get-tuple-element.40), channel_id=1, source_target_pairs={{0,1},{1,0},{2,3},{3,2},{4,5},{5,4},{6,7},{7,6},{8,9},{9,8},{10,11... | collective-permute-start | bytes 1572872 | tf_op jit(solution)/shard_map/ppermute | solution.py:40
  106.3 17.8 %collective-permute-start.11 = (f32[1024,128]{1,0:T(8,128)S(1)}, f32[1024,128]{1,0:T(8,128)S(1)}, u32[]{:S(2)}, u32[]{:S(2)}) collective-permute-start(f32[1024,128]{1,0:T(8,128)S(1)} %get-tuple-element.41), channel_id=1, source_target_pairs={{1,2},{2,1},{3,4},{4,3},{5,6},{6,5},{7,8},{8,7},{9,10},{10,9},{11,... | collective-permute-start | bytes 1572872 | tf_op jit(solution)/shard_map/ppermute | solution.py:40
  124.9 14.5 %collective-permute-start.12 = (f32[2,128,256]{2,1,0:T(8,128)S(1)}, f32[2,128,256]{2,1,0:T(8,128)S(1)}, u32[]{:S(2)}, u32[]{:S(2)}) collective-permute-start(f32[2,128,256]{2,1,0:T(8,128)S(1)} %get-tuple-element.43), channel_id=1, source_target_pairs={{0,32},{32,0},{64,96},{96,64},{128,160},{160,128},{192,224},{224,1... | collective-permute-start | bytes 786440 | tf_op jit(solution)/shard_map/ppermute | solution.py:40
  135.6 8.0 %collective-permute-start.13 = (f32[2,128,256]{2,1,0:T(8,128)S(1)}, f32[2,128,256]{2,1,0:T(8,128)S(1)}, u32[]{:S(2)}, u32[]{:S(2)}) collective-permute-start(f32[2,128,256]{2,1,0:T(8,128)S(1)} %get-tuple-element.44), channel_id=1, source_target_pairs={{32,64},{64,32},{96,128},{128,96},{160,192},{192,160},{33,65},{65,... | collective-permute-start | bytes 786440 | tf_op jit(solution)/shard_map/ppermute | solution.py:40

commit v5 on v4

--- a/solution.py
+++ b/solution.py
@@ -233,39 +233,39 @@
             own[p, :, b * LANES : (b + 1) * LANES] = grad[p, 1 + b, 0:EXT, :]
 
 
-def add_cols(place, own, col_a, col_b, p):
+def by_side(place, from_a, from_b):
     even = (place[1] & 1) == 0
-    from_a = col_a[p * EXT : (p + 1) * EXT, :]
-    from_b = col_b[p * EXT : (p + 1) * EXT, :]
-    low = own[p, :, 0:LANES] + jnp.where(even, from_b, from_a)
-    high = own[p, :, LANES:TILE] + jnp.where(even, from_a, from_b)
-    return low, high
-
-
-def fold_cols_kernel(depth, place, own, col_a, col_b, total, a_out, b_out):
+    return jnp.where(even, from_b, from_a), jnp.where(even, from_a, from_b)
+
+
+def fold_strips_kernel(depth, place, own, col_a, col_b, a_out, b_out):
     row_parity = place[0] & 1
-    a_at = aligned((1 - row_parity) * (EXT - depth), RIM)
-    b_at = aligned(row_parity * (EXT - depth), RIM)
-    for p in range(2):
-        low, high = add_cols(place, own, col_a, col_b, p)
-        total[p, :, 0:LANES] = low
-        total[p, :, LANES:TILE] = high
-        a_out[p] = total[p, pl.ds(a_at, depth), :]
-        b_out[p] = total[p, pl.ds(b_at, depth), :]
-
-
-def update_wide_kernel(place, center, total, row_a, row_b, scale, fresh, a_out, b_out):
+    for out, end in ((a_out, 1 - row_parity), (b_out, row_parity)):
+        at = end * (EXT - depth)
+        mine = pl.ds(aligned(at, RIM), depth)
+        for p in range(2):
+            theirs = pl.ds(aligned(p * EXT + at, RIM), depth)
+            left, right = by_side(place, col_a[theirs, :], col_b[theirs, :])
+            out[p, :, 0:LANES] = own[p, mine, 0:LANES] + left
+            out[p, :, LANES:TILE] = own[p, mine, LANES:TILE] + right
+
+
+def fold_inner_kernel(place, own, col_a, col_b, total):
+    mine = slice(RIM, RIM + TILE)
+    for p in range(2):
+        theirs = slice(p * EXT + RIM, p * EXT + RIM + TILE)
+        left, right = by_side(place, col_a[theirs, :], col_b[theirs, :])
+        total[p, :, 0:LANES] = own[p, mine, 0:LANES] + left
+        total[p, :, LANES:TILE] = own[p, mine, LANES:TILE] + right
+
+
+def update_wide_kernel(place, center, sent_a, sent_b, row_a, row_b, scale, fresh, a_out, b_out):
     row_parity = place[0] & 1
-    a_at = aligned((1 - row_parity) * TILE, RIM)
-    b_at = aligned(row_parity * TILE, RIM)
     even = (place[1] & 1) == 0
-    for p in range(2):
-        fresh[p, pl.ds(a_at, TILE), :] = center[p, pl.ds(a_at, TILE), :] - scale[pl.ds(a_at, TILE), :] * (
-            total[p, pl.ds(a_at, TILE), :] + row_a[p]
-        )
-        fresh[p, pl.ds(b_at, TILE), :] = center[p, pl.ds(b_at, TILE), :] - scale[pl.ds(b_at, TILE), :] * (
-            total[p, pl.ds(b_at, TILE), :] + row_b[p]
-        )
+    for sent, came, end in ((sent_a, row_a, 1 - row_parity), (sent_b, row_b, row_parity)):
+        rows = pl.ds(aligned(end * TILE, RIM), TILE)
+        for p in range(2):
+            fresh[p, rows, :] = center[p, rows, :] - scale[rows, :] * (sent[p] + came[p])
 
     @pl.when(place[0] == 0)
     def _():
@@ -290,7 +290,7 @@
         for half, came in ((0, top), (1, bottom)):
             at = slice(RIM + half * RIM, RIM + (half + 1) * RIM)
             out[p, half * RIM : (half + 1) * RIM, :] = center[p, at, :] - scale[at, :] * (
-                total[p, at, :] + came
+                total[p, half * RIM : (half + 1) * RIM, :] + came
             )
 
 
@@ -349,28 +349,34 @@
     def fold(first, center, cols, depth):
         own, a, b, *metas = iterate(first, center, cols)
         a, b = swaps((a, b), "col")
-        total, a, b = call(
-            functools.partial(fold_cols_kernel, depth),
-            (f32(2, EXT, TILE), f32(2, depth, TILE), f32(2, depth, TILE)),
+        sent = call(
+            functools.partial(fold_strips_kernel, depth),
+            (f32(2, depth, TILE), f32(2, depth, TILE)),
             [SMEM] + [VMEM] * 3,
         )(place, own, a, b)
-        return (total, metas) + swaps((a, b), "row")
-
-    total, metas, row_a, row_b = fold(True, center, (col_a, col_b), TILE)
+        came = swaps(sent, "row")
+        if first:
+            return sent, metas[0], came
+        total = call(fold_inner_kernel, f32(2, TILE, TILE), [SMEM] + [VMEM] * 3, bytes_accessed=4 << 20)(
+            place, own, a, b
+        )
+        return total, None, came
+
+    sent, metas, came = fold(True, center, (col_a, col_b), TILE)
     scale = call(
         light_kernel,
         f32(EXT, TILE),
         [SMEM, VMEM],
         [pltpu.VMEM((2, 4 * TILE + 8, LANES), jnp.float32), pltpu.VMEM((5, TILE, LANES), jnp.float32)],
         bytes_accessed=12 << 20,
-    )(metas[0], probe_field)
+    )(metas, probe_field)
     center, a, b = call(
-        update_wide_kernel, (f32(2, EXT, TILE), fold_strip, fold_strip), [SMEM] + [VMEM] * 5
-    )(place, center, total, row_a, row_b, scale)
-    total, _, row_a, row_b = fold(False, center, swaps((a, b), "col"), RIM)
+        update_wide_kernel, (f32(2, EXT, TILE), fold_strip, fold_strip), [SMEM] + [VMEM] * 6
+    )(place, center, *sent, *came, scale)
+    total, _, came = fold(False, center, swaps((a, b), "col"), RIM)
     return call(
         update_own_kernel, jax.ShapeDtypeStruct((2, TILE, TILE), jnp.float32), [SMEM] + [VMEM] * 5
-    )(place, center, total, row_a, row_b, scale)
+    )(place, center, total, *came, scale)
 
 
 def solution(mesh):

time: 145 us -> 145 us (level)
  no operation moved by 1% of the time
where the time goes in v5:
time: 145 us; the launch traced here: 144 us
  waiting for transfers between devices  69.7 us (48%)
  starting transfers between devices  44.3 us (31%)
  Pallas kernels  28.2 us (19%)
    ppermute x14, waiting for transfers between devices, swap(): return lax.ppermute(value, axis, pairs)  69.7 us
    ppermute x14, starting transfers between devices, swap(): return lax.ppermute(value, axis, pairs)  44.3 us
    pallas_call x2, Pallas kernels, iterate(): call(functools.partial(iterate_kernel, first), outs, [SMEM] * 3 + [VMEM]...  12.3 us
    pallas_call x1, Pallas kernels, per_device(): call(light_kernel, f32(EXT, TILE), [SMEM, VMEM], [pltpu.VMEM((2, 4 * TILE...  8.34 us
  transfers between devices with their start and end apart: 14, of which 10 were waited for; matrix products, arithmetic and copies ran while one was open for 0% of the time, Pallas kernels for 7%

profile of v5, /device:TPU:87, one launch (start us, length us, event | category | flops | bytes accessed | tf_op | source)
XLA Modules:
  0.0 144.5 jit_solution(7900188231867126202)
XLA Ops:
  0.9 1.0 copy-done
  2.0 0.6 shard_map.64
  2.6 1.7 %collective-permute-start = (f32[264,256]{1,0:T(8,128)S(1)}, f32[264,256]{1,0:T(8,128)S(1)}, u32[]{:S(2)}, u32[]{:S(2)}) collective-permute-start(f32[264,256]{1,0:T(8,128)S(1)} %get-tuple-element.23), channel_id=1, source_target_pairs={{0,32},{32,0},{64,96},{96,64},{128,160},{160,128},{192,224},{224,1... | collective-permute-start | bytes 811016 | tf_op jit(solution)/shard_map/ppermute | solution.py:40
  4.3 1.9 %collective-permute-start.1 = (f32[264,256]{1,0:T(8,128)S(1)}, f32[264,256]{1,0:T(8,128)S(1)}, u32[]{:S(2)}, u32[]{:S(2)}) collective-permute-start(f32[264,256]{1,0:T(8,128)S(1)} %get-tuple-element.24), channel_id=1, source_target_pairs={{32,64},{64,32},{96,128},{128,96},{160,192},{192,160},{33,65},{65,... | collective-permute-start | bytes 811016 | tf_op jit(solution)/shard_map/ppermute | solution.py:40
  6.2 4.2 %collective-permute-done.row_a = f32[264,256]{1,0:T(8,128)S(1)} collective-permute-done((f32[264,256]{1,0:T(8,128)S(1)}, f32[264,256]{1,0:T(8,128)S(1)}, u32[]{:S(2)}, u32[]{:S(2)}) %collective-permute-start) | collective-permute-done | bytes 270368 | tf_op jit(solution)/shard_map/ppermute | solution.py:40
  10.4 5.7 %collective-permute-done.1.row_b = f32[264,256]{1,0:T(8,128)S(1)} collective-permute-done((f32[264,256]{1,0:T(8,128)S(1)}, f32[264,256]{1,0:T(8,128)S(1)}, u32[]{:S(2)}, u32[]{:S(2)}) %collective-permute-start.1) | collective-permute-done | bytes 270368 | tf_op jit(solution)/shard_map/ppermute | solution.py:40
  16.1 1.5 %shard_map.66 = (f32[1032,128]{1,0:T(8,128)}, f32[8,128]{1,0:T(8,128)S(1)}) custom-call(s32[4]{0:T(128)S(1)} %pad_add_fusion.place, f32[2,256,256]{2,1,0:T(8,128)S(1)} %copy-done, f32[264,256]{1,0:T(8,128)S(1)} %collective-permute-done.row_a, f32[264,256]{1,0:T(8,128)S(1)} %collective-permute-done.1.row_b, s32[1,12]{1,0:T(1,128)S(1)} %reshape.12.offs, ...), custom_call_target="tpu_custom_call" | custom-call | bytes 1048576 | tf_op jit(solution)/shard_map/pallas_call | solution.py:320
  17.5 7.2 %collective-permute-start.3 = (f32[1032,128]{1,0:T(8,128)}, f32[1032,128]{1,0:T(8,128)S(1)}, u32[]{:S(2)}, u32[]{:S(2)}) collective-permute-start(f32[1032,128]{1,0:T(8,128)} %get-tuple-element.26), channel_id=1, source_target_pairs={{1,2},{2,1},{3,4},{4,3},{5,6},{6,5},{7,8},{8,7},{9,10},{10,9},{11,... | collective-permute-start | bytes 1585160 | tf_op jit(solution)/shard_map/ppermute | solution.py:40
  24.8 0.7 shard_map.67
  25.6 0.6 shard_map.65.center
  26.2 12.1 %collective-permute-done.3.col_b = f32[1032,128]{1,0:T(8,128)S(1)} collective-permute-done((f32[1032,128]{1,0:T(8,128)}, f32[1032,128]{1,0:T(8,128)S(1)}, u32[]{:S(2)}, u32[]{:S(2)}) %collective-permute-start.3) | collective-permute-done | bytes 528416 | tf_op jit(solution)/shard_map/ppermute | solution.py:40
  38.3 6.4 %shard_map.68 = (f32[2,512,256]{2,1,0:T(8,128)S(1)}, f32[1024,128]{1,0:T(8,128)S(1)}, f32[1024,128]{1,0:T(8,128)S(1)}, s32[24,128]{1,0:T(8,128)S(1)}) custom-call(s32[4]{0:T(128)S(1)} %pad_add_fusion.place, s32[12]{0:T(128)S(1)} %reshape.13.offs, s32[1]{0:T(128)} %bitcast.4.cnt, f32[8,128]{1,0:T(8,128)S(1)} %get-tuple-element.25.meta, ...), custom_call_target="tpu_custom_call" | custom-call | flops 3221225472 | bytes 6291456 | tf_op jit(solution)/shard_map/pallas_call | solution.py:339
  44.8 7.0 %collective-permute-start.5 = (f32[1024,128]{1,0:T(8,128)S(1)}, f32[1024,128]{1,0:T(8,128)S(1)}, u32[]{:S(2)}, u32[]{:S(2)}) collective-permute-start(f32[1024,128]{1,0:T(8,128)S(1)} %get-tuple-element.29), channel_id=1, source_target_pairs={{1,2},{2,1},{3,4},{4,3},{5,6},{6,5},{7,8},{8,7},{9,10},{10,9},{11,... | collective-permute-start | bytes 1572872 | tf_op jit(solution)/shard_map/ppermute | solution.py:40
  51.9 14.9 %collective-permute-done.5.col_b = f32[1024,128]{1,0:T(8,128)S(1)} collective-permute-done((f32[1024,128]{1,0:T(8,128)S(1)}, f32[1024,128]{1,0:T(8,128)S(1)}, u32[]{:S(2)}, u32[]{:S(2)}) %collective-permute-start.5) | collective-permute-done | bytes 524320 | tf_op jit(solution)/shard_map/ppermute | solution.py:40
  66.8 0.7 shard_map.69
  67.5 1.9 %collective-permute-start.7 = (f32[2,256,256]{2,1,0:T(8,128)S(1)}, f32[2,256,256]{2,1,0:T(8,128)S(1)}, u32[]{:S(2)}, u32[]{:S(2)}) collective-permute-start(f32[2,256,256]{2,1,0:T(8,128)S(1)} %get-tuple-element.31.sent_b), channel_id=1, source_target_pairs={{32,64},{64,32},{96,128},{128,96},{160,192},{192,160},{33,65},{65,... | collective-permute-start | bytes 1572872 | tf_op jit(solution)/shard_map/ppermute | solution.py:40
  69.4 8.3 %shard_map.70.scale = f32[512,256]{1,0:T(8,128)S(1)} custom-call(s32[24,128]{1,0:T(8,128)S(1)} %get-tuple-element.32.metas, f32[2,256,256]{2,1,0:T(8,128)S(1)} %copy-done.3), custom_call_target="tpu_custom_call" | custom-call | bytes 12582912 | tf_op jit(solution)/shard_map/pallas_call | solution.py:366
  77.8 1.1 collective-permute-done.6.row_a
  78.9 5.6 %collective-permute-done.7.row_b = f32[2,256,256]{2,1,0:T(8,128)S(1)} collective-permute-done((f32[2,256,256]{2,1,0:T(8,128)S(1)}, f32[2,256,256]{2,1,0:T(8,128)S(1)}, u32[]{:S(2)}, u32[]{:S(2)}) %collective-permute-start.7) | collective-permute-done | bytes 524320 | tf_op jit(solution)/shard_map/ppermute | solution.py:40
  84.5 0.8 shard_map.71
  85.4 5.8 %collective-permute-start.9 = (f32[1024,128]{1,0:T(8,128)S(1)}, f32[1024,128]{1,0:T(8,128)S(1)}, u32[]{:S(2)}, u32[]{:S(2)}) collective-permute-start(f32[1024,128]{1,0:T(8,128)S(1)} %get-tuple-element.35), channel_id=1, source_target_pairs={{1,2},{2,1},{3,4},{4,3},{5,6},{6,5},{7,8},{8,7},{9,10},{10,9},{11,... | collective-permute-start | bytes 1572872 | tf_op jit(solution)/shard_map/ppermute | solution.py:40
  91.3 9.0 %collective-permute-done.9.col_b = f32[1024,128]{1,0:T(8,128)S(1)} collective-permute-done((f32[1024,128]{1,0:T(8,128)S(1)}, f32[1024,128]{1,0:T(8,128)S(1)}, u32[]{:S(2)}, u32[]{:S(2)}) %collective-permute-start.9) | collective-permute-done | bytes 524320 | tf_op jit(solution)/shard_map/ppermute | solution.py:40
  100.3 5.9 %shard_map.72 = (f32[2,512,256]{2,1,0:T(8,128)S(1)}, f32[1024,128]{1,0:T(8,128)S(1)}, f32[1024,128]{1,0:T(8,128)S(1)}) custom-call(s32[4]{0:T(128)S(1)} %pad_add_fusion.place, s32[12]{0:T(128)S(1)} %reshape.13.offs, s32[1]{0:T(128)} %bitcast.5.cnt, f32[8,128]{1,0:T(8,128)S(1)} %get-tuple-element.25.meta, f32[2,512,256]{2,1,0:T(8,128)S(1)} %get-tuple-element.33.center, ...), custom_call_target="tpu_custom_call" | custom-call | flops 3221225472 | bytes 6291456 | tf_op jit(solution)/shard_map/pallas_call | solution.py:339
  106.2 6.1 %collective-permute-start.11 = (f32[1024,128]{1,0:T(8,128)S(1)}, f32[1024,128]{1,0:T(8,128)S(1)}, u32[]{:S(2)}, u32[]{:S(2)}) collective-permute-start(f32[1024,128]{1,0:T(8,128)S(1)} %get-tuple-element.38), channel_id=1, source_target_pairs={{1,2},{2,1},{3,4},{4,3},{5,6},{6,5},{7,8},{8,7},{9,10},{10,9},{11,... | collective-permute-start | bytes 1572872 | tf_op jit(solution)/shard_map/ppermute | solution.py:40
  112.3 11.7 %collective-permute-done.11.col_b = f32[1024,128]{1,0:T(8,128)S(1)} collective-permute-done((f32[1024,128]{1,0:T(8,128)S(1)}, f32[1024,128]{1,0:T(8,128)S(1)}, u32[]{:S(2)}, u32[]{:S(2)}) %collective-permute-start.11) | collective-permute-done | bytes 524320 | tf_op jit(solution)/shard_map/ppermute | solution.py:40
  124.0 0.6 shard_map.74
  124.7 10.3 %collective-permute-start.12 = (f32[2,128,256]{2,1,0:T(8,128)S(1)}, f32[2,128,256]{2,1,0:T(8,128)S(1)}, u32[]{:S(2)}, u32[]{:S(2)}) collective-permute-start(f32[2,128,256]{2,1,0:T(8,128)S(1)} %get-tuple-element.39), channel_id=1, source_target_pairs={{0,32},{32,0},{64,96},{96,64},{128,160},{160,128},{192,224},{224,1... | collective-permute-start | bytes 786440 | tf_op jit(solution)/shard_map/ppermute | solution.py:40
  135.0 1.9 %collective-permute-start.13 = (f32[2,128,256]{2,1,0:T(8,128)S(1)}, f32[2,128,256]{2,1,0:T(8,128)S(1)}, u32[]{:S(2)}, u32[]{:S(2)}) collective-permute-start(f32[2,128,256]{2,1,0:T(8,128)S(1)} %get-tuple-element.40), channel_id=1, source_target_pairs={{32,64},{64,32},{96,128},{128,96},{160,192},{192,160},{33,65},{65,... | collective-permute-start | bytes 786440 | tf_op jit(solution)/shard_map/ppermute | solution.py:40
  136.9 0.6 shard_map.73.total
  137.5 1.2 collective-permute-done.12.row_a
  138.7 4.2 %collective-permute-done.13.row_b = f32[2,128,256]{2,1,0:T(8,128)S(1)} collective-permute-done((f32[2,128,256]{2,1,0:T(8,128)S(1)}, f32[2,128,256]{2,1,0:T(8,128)S(1)}, u32[]{:S(2)}, u32[]{:S(2)}) %collective-permute-start.13) | collective-permute-done | bytes 262176 | tf_op jit(solution)/shard_map/ppermute | solution.py:40
  143.0 1.5 %shard_map.75 = f32[2,256,256]{2,1,0:T(8,128)} custom-call(s32[4]{0:T(128)S(1)} %pad_add_fusion.place, f32[2,512,256]{2,1,0:T(8,128)S(1)} %get-tuple-element.33.center, f32[2,256,256]{2,1,0:T(8,128)S(1)} %shard_map.73.total, f32[2,128,256]{2,1,0:T(8,128)S(1)} %collective-permute-done.12.row_a, f32[2,128,256]{2,1,0:T(8,128)S(1)} %collective-permute-done.13.row_b, ...), custom_call_target="tpu_custom_call" | custom-call | bytes 1048576 | tf_op jit(solution)/shard_map/pallas_call | solution.py:377
  (24 shorter events, 0.8 us)
Async XLA Ops:
  0.0 0.7 copy-start.5
  0.9 1.0 copy-start
  2.6 7.8 %collective-permute-start = (f32[264,256]{1,0:T(8,128)S(1)}, f32[264,256]{1,0:T(8,128)S(1)}, u32[]{:S(2)}, u32[]{:S(2)}) collective-permute-start(f32[264,256]{1,0:T(8,128)S(1)} %get-tuple-element.23), channel_id=1, source_target_pairs={{0,32},{32,0},{64,96},{96,64},{128,160},{160,128},{192,224},{224,1... | collective-permute-start | bytes 811016 | tf_op jit(solution)/shard_map/ppermute | solution.py:40
  4.3 11.8 %collective-permute-start.1 = (f32[264,256]{1,0:T(8,128)S(1)}, f32[264,256]{1,0:T(8,128)S(1)}, u32[]{:S(2)}, u32[]{:S(2)}) collective-permute-start(f32[264,256]{1,0:T(8,128)S(1)} %get-tuple-element.24), channel_id=1, source_target_pairs={{32,64},{64,32},{96,128},{128,96},{160,192},{192,160},{33,65},{65,... | collective-permute-start | bytes 811016 | tf_op jit(solution)/shard_map/ppermute | solution.py:40
  17.5 8.0 %copy-start.2 = (bf16[1024,512]{1,0:T(8,128)(2,1)S(1)}, bf16[1024,512]{1,0:T(8,128)(2,1)}, u32[]{:S(2)}) copy-start(bf16[1024,512]{1,0:T(8,128)(2,1)} %constant.15.clone.tables) | copy-start | bytes 3145732
  17.5 8.0 %copy-start.1 = (f32[2,256,256]{2,1,0:T(8,128)S(1)}, f32[2,256,256]{2,1,0:T(8,128)}, u32[]{:S(2)}) copy-start(f32[2,256,256]{2,1,0:T(8,128)} %obj.7) | copy-start | bytes 1572868
  17.5 20.8 %collective-permute-start.3 = (f32[1032,128]{1,0:T(8,128)}, f32[1032,128]{1,0:T(8,128)S(1)}, u32[]{:S(2)}, u32[]{:S(2)}) collective-permute-start(f32[1032,128]{1,0:T(8,128)} %get-tuple-element.26), channel_id=1, source_target_pairs={{1,2},{2,1},{3,4},{4,3},{5,6},{6,5},{7,8},{8,7},{9,10},{10,9},{11,... | collective-permute-start | bytes 1585160 | tf_op jit(solution)/shard_map/ppermute | solution.py:40
  25.4 12.9 %collective-permute-start.2 = (f32[1032,128]{1,0:T(8,128)S(1)}, f32[1032,128]{1,0:T(8,128)}, u32[]{:S(2)}, u32[]{:S(2)}) collective-permute-start(f32[1032,128]{1,0:T(8,128)S(1)} %shard_map.67), channel_id=1, source_target_pairs={{0,1},{1,0},{2,3},{3,2},{4,5},{5,4},{6,7},{7,6},{8,9},{9,8},{10,11... | collective-permute-start | bytes 1585160 | tf_op jit(solution)/shard_map/ppermute | solution.py:40
  25.6 12.8 %copy-start.3 = (f32[2,256,256]{2,1,0:T(8,128)S(1)}, f32[2,256,256]{2,1,0:T(8,128)}, u32[]{:S(2)}) copy-start(f32[2,256,256]{2,1,0:T(8,128)} %probe.5) | copy-start | bytes 1572868
  25.6 12.7 %copy-start.4 = (bf16[1,1,6,256,256]{4,3,2,1,0:T(8,128)(2,1)S(1)}, bf16[1,1,6,256,256]{4,3,2,1,0:T(8,128)(2,1)}, u32[]{:S(2)}) copy-start(bf16[1,1,6,256,256]{4,3,2,1,0:T(8,128)(2,1)} %param.8) | copy-start | bytes 2359300
  44.7 7.2 %collective-permute-start.4 = (f32[1024,128]{1,0:T(8,128)S(1)}, f32[1024,128]{1,0:T(8,128)S(1)}, u32[]{:S(2)}, u32[]{:S(2)}) collective-permute-start(f32[1024,128]{1,0:T(8,128)S(1)} %get-tuple-element.28), channel_id=1, source_target_pairs={{0,1},{1,0},{2,3},{3,2},{4,5},{5,4},{6,7},{7,6},{8,9},{9,8},{10,11... | collective-permute-start | bytes 1572872 | tf_op jit(solution)/shard_map/ppermute | solution.py:40
  44.8 21.9 %collective-permute-start.5 = (f32[1024,128]{1,0:T(8,128)S(1)}, f32[1024,128]{1,0:T(8,128)S(1)}, u32[]{:S(2)}, u32[]{:S(2)}) collective-permute-start(f32[1024,128]{1,0:T(8,128)S(1)} %get-tuple-element.29), channel_id=1, source_target_pairs={{1,2},{2,1},{3,4},{4,3},{5,6},{6,5},{7,8},{8,7},{9,10},{10,9},{11,... | collective-permute-start | bytes 1572872 | tf_op jit(solution)/shard_map/ppermute | solution.py:40
  67.4 11.5 %collective-permute-start.6 = (f32[2,256,256]{2,1,0:T(8,128)S(1)}, f32[2,256,256]{2,1,0:T(8,128)S(1)}, u32[]{:S(2)}, u32[]{:S(2)}) collective-permute-start(f32[2,256,256]{2,1,0:T(8,128)S(1)} %get-tuple-element.30.sent_a), channel_id=1, source_target_pairs={{0,32},{32,0},{64,96},{96,64},{128,160},{160,128},{192,224},{224,1... | collective-permute-start | bytes 1572872 | tf_op jit(solution)/shard_map/ppermute | solution.py:40
  67.5 17.0 %collective-permute-start.7 = (f32[2,256,256]{2,1,0:T(8,128)S(1)}, f32[2,256,256]{2,1,0:T(8,128)S(1)}, u32[]{:S(2)}, u32[]{:S(2)}) collective-permute-start(f32[2,256,256]{2,1,0:T(8,128)S(1)} %get-tuple-element.31.sent_b), channel_id=1, source_target_pairs={{32,64},{64,32},{96,128},{128,96},{160,192},{192,160},{33,65},{65,... | collective-permute-start | bytes 1572872 | tf_op jit(solution)/shard_map/ppermute | solution.py:40
  85.3 5.9 %collective-permute-start.8 = (f32[1024,128]{1,0:T(8,128)S(1)}, f32[1024,128]{1,0:T(8,128)S(1)}, u32[]{:S(2)}, u32[]{:S(2)}) collective-permute-start(f32[1024,128]{1,0:T(8,128)S(1)} %get-tuple-element.34), channel_id=1, source_target_pairs={{0,1},{1,0},{2,3},{3,2},{4,5},{5,4},{6,7},{7,6},{8,9},{9,8},{10,11... | collective-permute-start | bytes 1572872 | tf_op jit(solution)/shard_map/ppermute | solution.py:40
  85.4 14.8 %collective-permute-start.9 = (f32[1024,128]{1,0:T(8,128)S(1)}, f32[1024,128]{1,0:T(8,128)S(1)}, u32[]{:S(2)}, u32[]{:S(2)}) collective-permute-start(f32[1024,128]{1,0:T(8,128)S(1)} %get-tuple-element.35), channel_id=1, source_target_pairs={{1,2},{2,1},{3,4},{4,3},{5,6},{6,5},{7,8},{8,7},{9,10},{10,9},{11,... | collective-permute-start | bytes 1572872 | tf_op jit(solution)/shard_map/ppermute | solution.py:40
  106.1 6.2 %collective-permute-start.10 = (f32[1024,128]{1,0:T(8,128)S(1)}, f32[1024,128]{1,0:T(8,128)S(1)}, u32[]{:S(2)}, u32[]{:S(2)}) collective-permute-start(f32[1024,128]{1,0:T(8,128)S(1)} %get-tuple-element.37), channel_id=1, source_target_pairs={{0,1},{1,0},{2,3},{3,2},{4,5},{5,4},{6,7},{7,6},{8,9},{9,8},{10,11... | collective-permute-start | bytes 1572872 | tf_op jit(solution)/shard_map/ppermute | solution.py:40
  106.2 17.8 %collective-permute-start.11 = (f32[1024,128]{1,0:T(8,128)S(1)}, f32[1024,128]{1,0:T(8,128)S(1)}, u32[]{:S(2)}, u32[]{:S(2)}) collective-permute-start(f32[1024,128]{1,0:T(8,128)S(1)} %get-tuple-element.38), channel_id=1, source_target_pairs={{1,2},{2,1},{3,4},{4,3},{5,6},{6,5},{7,8},{8,7},{9,10},{10,9},{11,... | collective-permute-start | bytes 1572872 | tf_op jit(solution)/shard_map/ppermute | solution.py:40
  124.7 14.1 %collective-permute-start.12 = (f32[2,128,256]{2,1,0:T(8,128)S(1)}, f32[2,128,256]{2,1,0:T(8,128)S(1)}, u32[]{:S(2)}, u32[]{:S(2)}) collective-permute-start(f32[2,128,256]{2,1,0:T(8,128)S(1)} %get-tuple-element.39), channel_id=1, source_target_pairs={{0,32},{32,0},{64,96},{96,64},{128,160},{160,128},{192,224},{224,1... | collective-permute-start | bytes 786440 | tf_op jit(solution)/shard_map/ppermute | solution.py:40
  135.0 8.0 %collective-permute-start.13 = (f32[2,128,256]{2,1,0:T(8,128)S(1)}, f32[2,128,256]{2,1,0:T(8,128)S(1)}, u32[]{:S(2)}, u32[]{:S(2)}) collective-permute-start(f32[2,128,256]{2,1,0:T(8,128)S(1)} %get-tuple-element.40), channel_id=1, source_target_pairs={{32,64},{64,32},{96,128},{128,96},{160,192},{192,160},{33,65},{65,... | collective-permute-start | bytes 786440 | tf_op jit(solution)/shard_map/ppermute | solution.py:40

commit v6 on v5

--- a/solution.py
+++ b/solution.py
@@ -282,16 +282,22 @@
         b_out[p * EXT : (p + 1) * EXT, :] = jnp.where(even, low, high)
 
 
-def update_own_kernel(place, center, total, row_a, row_b, scale, out):
+def update_own_kernel(place, center, total, row_a, row_b, scale, out, fresh, left):
     odd = (place[0] & 1) == 1
+    copies = []
     for p in range(2):
         top = jnp.where(odd, row_a[p], row_b[p])
         bottom = jnp.where(odd, row_b[p], row_a[p])
         for half, came in ((0, top), (1, bottom)):
             at = slice(RIM + half * RIM, RIM + (half + 1) * RIM)
-            out[p, half * RIM : (half + 1) * RIM, :] = center[p, at, :] - scale[at, :] * (
-                total[p, half * RIM : (half + 1) * RIM, :] + came
+            rows = slice(half * RIM, (half + 1) * RIM)
+            fresh[p, rows, :] = center[p, at, :] - scale[at, :] * (total[p, rows, :] + came)
+            copies.append(
+                pltpu.make_async_copy(fresh.at[p, rows, :], out.at[p, rows, :], left.at[len(copies)])
             )
+            copies[-1].start()
+    for copy in copies:
+        copy.wait()
 
 
 def swaps(values, axis):
@@ -374,8 +380,13 @@
         update_wide_kernel, (f32(2, EXT, TILE), fold_strip, fold_strip), [SMEM] + [VMEM] * 6
     )(place, center, *sent, *came, scale)
     total, _, came = fold(False, center, swaps((a, b), "col"), RIM)
-    return call(
-        update_own_kernel, jax.ShapeDtypeStruct((2, TILE, TILE), jnp.float32), [SMEM] + [VMEM] * 5
+    return pl.pallas_call(
+        update_own_kernel,
+        out_shape=jax.ShapeDtypeStruct((2, TILE, TILE), jnp.float32),
+        in_specs=[SMEM] + [VMEM] * 5,
+        out_specs=pl.BlockSpec(memory_space=pl.ANY),
+        scratch_shapes=[pltpu.VMEM((2, TILE, TILE), jnp.float32), pltpu.SemaphoreType.DMA((4,))],
+        compiler_params=pltpu.CompilerParams(vmem_limit_bytes=6 << 20),
     )(place, center, total, *came, scale)
 
 

time: 145 us -> 145 us (level)
  no operation moved by 1% of the time
where the time goes in v6:
time: 145 us; the launch traced here: 144 us
  waiting for transfers between devices  69.8 us (48%)
  starting transfers between devices  43.9 us (30%)
  Pallas kernels  28.2 us (19%)
    ppermute x14, waiting for transfers between devices, swap(): return lax.ppermute(value, axis, pairs)  69.8 us
    ppermute x14, starting transfers between devices, swap(): return lax.ppermute(value, axis, pairs)  43.9 us
    pallas_call x2, Pallas kernels, iterate(): call(functools.partial(iterate_kernel, first), outs, [SMEM] * 3 + [VMEM]...  12.4 us
    pallas_call x1, Pallas kernels, per_device(): call(light_kernel, f32(EXT, TILE), [SMEM, VMEM], [pltpu.VMEM((2, 4 * TILE...  8.34 us
  transfers between devices with their start and end apart: 14, of which 10 were waited for; matrix products, arithmetic and copies ran while one was open for 0% of the time, Pallas kernels for 7%

profile of v6, /device:TPU:87, one launch (start us, length us, event | category | flops | bytes accessed | tf_op | source)
XLA Modules:
  0.0 144.3 jit_solution(14222578779746648379)
XLA Ops:
  0.9 1.0 copy-done
  2.0 0.6 shard_map.64
  2.6 1.7 %collective-permute-start = (f32[264,256]{1,0:T(8,128)S(1)}, f32[264,256]{1,0:T(8,128)S(1)}, u32[]{:S(2)}, u32[]{:S(2)}) collective-permute-start(f32[264,256]{1,0:T(8,128)S(1)} %get-tuple-element.23), channel_id=1, source_target_pairs={{0,32},{32,0},{64,96},{96,64},{128,160},{160,128},{192,224},{224,1... | collective-permute-start | bytes 811016 | tf_op jit(solution)/shard_map/ppermute | solution.py:40
  4.3 1.9 %collective-permute-start.1 = (f32[264,256]{1,0:T(8,128)S(1)}, f32[264,256]{1,0:T(8,128)S(1)}, u32[]{:S(2)}, u32[]{:S(2)}) collective-permute-start(f32[264,256]{1,0:T(8,128)S(1)} %get-tuple-element.24), channel_id=1, source_target_pairs={{32,64},{64,32},{96,128},{128,96},{160,192},{192,160},{33,65},{65,... | collective-permute-start | bytes 811016 | tf_op jit(solution)/shard_map/ppermute | solution.py:40
  6.2 4.2 %collective-permute-done.row_a = f32[264,256]{1,0:T(8,128)S(1)} collective-permute-done((f32[264,256]{1,0:T(8,128)S(1)}, f32[264,256]{1,0:T(8,128)S(1)}, u32[]{:S(2)}, u32[]{:S(2)}) %collective-permute-start) | collective-permute-done | bytes 270368 | tf_op jit(solution)/shard_map/ppermute | solution.py:40
  10.4 5.7 %collective-permute-done.1.row_b = f32[264,256]{1,0:T(8,128)S(1)} collective-permute-done((f32[264,256]{1,0:T(8,128)S(1)}, f32[264,256]{1,0:T(8,128)S(1)}, u32[]{:S(2)}, u32[]{:S(2)}) %collective-permute-start.1) | collective-permute-done | bytes 270368 | tf_op jit(solution)/shard_map/ppermute | solution.py:40
  16.1 1.5 %shard_map.66 = (f32[1032,128]{1,0:T(8,128)}, f32[8,128]{1,0:T(8,128)S(1)}) custom-call(s32[4]{0:T(128)S(1)} %pad_add_fusion.place, f32[2,256,256]{2,1,0:T(8,128)S(1)} %copy-done, f32[264,256]{1,0:T(8,128)S(1)} %collective-permute-done.row_a, f32[264,256]{1,0:T(8,128)S(1)} %collective-permute-done.1.row_b, s32[1,12]{1,0:T(1,128)S(1)} %reshape.12.offs, ...), custom_call_target="tpu_custom_call" | custom-call | bytes 1048576 | tf_op jit(solution)/shard_map/pallas_call | solution.py:326
  17.5 7.2 %collective-permute-start.3 = (f32[1032,128]{1,0:T(8,128)}, f32[1032,128]{1,0:T(8,128)S(1)}, u32[]{:S(2)}, u32[]{:S(2)}) collective-permute-start(f32[1032,128]{1,0:T(8,128)} %get-tuple-element.26), channel_id=1, source_target_pairs={{1,2},{2,1},{3,4},{4,3},{5,6},{6,5},{7,8},{8,7},{9,10},{10,9},{11,... | collective-permute-start | bytes 1585160 | tf_op jit(solution)/shard_map/ppermute | solution.py:40
  24.8 0.7 shard_map.67
  25.6 0.6 shard_map.65.center
  26.2 12.1 %collective-permute-done.3.col_b = f32[1032,128]{1,0:T(8,128)S(1)} collective-permute-done((f32[1032,128]{1,0:T(8,128)}, f32[1032,128]{1,0:T(8,128)S(1)}, u32[]{:S(2)}, u32[]{:S(2)}) %collective-permute-start.3) | collective-permute-done | bytes 528416 | tf_op jit(solution)/shard_map/ppermute | solution.py:40
  38.3 6.4 %shard_map.68 = (f32[2,512,256]{2,1,0:T(8,128)S(1)}, f32[1024,128]{1,0:T(8,128)S(1)}, f32[1024,128]{1,0:T(8,128)S(1)}, s32[24,128]{1,0:T(8,128)S(1)}) custom-call(s32[4]{0:T(128)S(1)} %pad_add_fusion.place, s32[12]{0:T(128)S(1)} %reshape.13.offs, s32[1]{0:T(128)} %bitcast.4.cnt, f32[8,128]{1,0:T(8,128)S(1)} %get-tuple-element.25.meta, ...), custom_call_target="tpu_custom_call" | custom-call | flops 3221225472 | bytes 6291456 | tf_op jit(solution)/shard_map/pallas_call | solution.py:345
  44.9 7.1 %collective-permute-start.5 = (f32[1024,128]{1,0:T(8,128)S(1)}, f32[1024,128]{1,0:T(8,128)S(1)}, u32[]{:S(2)}, u32[]{:S(2)}) collective-permute-start(f32[1024,128]{1,0:T(8,128)S(1)} %get-tuple-element.29), channel_id=1, source_target_pairs={{1,2},{2,1},{3,4},{4,3},{5,6},{6,5},{7,8},{8,7},{9,10},{10,9},{11,... | collective-permute-start | bytes 1572872 | tf_op jit(solution)/shard_map/ppermute | solution.py:40
  52.0 14.8 %collective-permute-done.5.col_b = f32[1024,128]{1,0:T(8,128)S(1)} collective-permute-done((f32[1024,128]{1,0:T(8,128)S(1)}, f32[1024,128]{1,0:T(8,128)S(1)}, u32[]{:S(2)}, u32[]{:S(2)}) %collective-permute-start.5) | collective-permute-done | bytes 524320 | tf_op jit(solution)/shard_map/ppermute | solution.py:40
  66.8 0.7 shard_map.69
  67.6 1.9 %collective-permute-start.7 = (f32[2,256,256]{2,1,0:T(8,128)S(1)}, f32[2,256,256]{2,1,0:T(8,128)S(1)}, u32[]{:S(2)}, u32[]{:S(2)}) collective-permute-start(f32[2,256,256]{2,1,0:T(8,128)S(1)} %get-tuple-element.31.sent_b), channel_id=1, source_target_pairs={{32,64},{64,32},{96,128},{128,96},{160,192},{192,160},{33,65},{65,... | collective-permute-start | bytes 1572872 | tf_op jit(solution)/shard_map/ppermute | solution.py:40
  69.5 8.3 %shard_map.70.scale = f32[512,256]{1,0:T(8,128)S(1)} custom-call(s32[24,128]{1,0:T(8,128)S(1)} %get-tuple-element.32.metas, f32[2,256,256]{2,1,0:T(8,128)S(1)} %copy-done.3), custom_call_target="tpu_custom_call" | custom-call | bytes 12582912 | tf_op jit(solution)/shard_map/pallas_call | solution.py:372
  77.8 1.1 collective-permute-done.6.row_a
  78.9 5.6 %collective-permute-done.7.row_b = f32[2,256,256]{2,1,0:T(8,128)S(1)} collective-permute-done((f32[2,256,256]{2,1,0:T(8,128)S(1)}, f32[2,256,256]{2,1,0:T(8,128)S(1)}, u32[]{:S(2)}, u32[]{:S(2)}) %collective-permute-start.7) | collective-permute-done | bytes 524320 | tf_op jit(solution)/shard_map/ppermute | solution.py:40
  84.6 0.8 shard_map.71
  85.5 5.7 %collective-permute-start.9 = (f32[1024,128]{1,0:T(8,128)S(1)}, f32[1024,128]{1,0:T(8,128)S(1)}, u32[]{:S(2)}, u32[]{:S(2)}) collective-permute-start(f32[1024,128]{1,0:T(8,128)S(1)} %get-tuple-element.35), channel_id=1, source_target_pairs={{1,2},{2,1},{3,4},{4,3},{5,6},{6,5},{7,8},{8,7},{9,10},{10,9},{11,... | collective-permute-start | bytes 1572872 | tf_op jit(solution)/shard_map/ppermute | solution.py:40
  91.2 9.1 %collective-permute-done.9.col_b = f32[1024,128]{1,0:T(8,128)S(1)} collective-permute-done((f32[1024,128]{1,0:T(8,128)S(1)}, f32[1024,128]{1,0:T(8,128)S(1)}, u32[]{:S(2)}, u32[]{:S(2)}) %collective-permute-start.9) | collective-permute-done | bytes 524320 | tf_op jit(solution)/shard_map/ppermute | solution.py:40
  100.3 5.9 %shard_map.72 = (f32[2,512,256]{2,1,0:T(8,128)S(1)}, f32[1024,128]{1,0:T(8,128)S(1)}, f32[1024,128]{1,0:T(8,128)S(1)}) custom-call(s32[4]{0:T(128)S(1)} %pad_add_fusion.place, s32[12]{0:T(128)S(1)} %reshape.13.offs, s32[1]{0:T(128)} %bitcast.5.cnt, f32[8,128]{1,0:T(8,128)S(1)} %get-tuple-element.25.meta, f32[2,512,256]{2,1,0:T(8,128)S(1)} %get-tuple-element.33.center, ...), custom_call_target="tpu_custom_call" | custom-call | flops 3221225472 | bytes 6291456 | tf_op jit(solution)/shard_map/pallas_call | solution.py:345
  106.3 6.1 %collective-permute-start.11 = (f32[1024,128]{1,0:T(8,128)S(1)}, f32[1024,128]{1,0:T(8,128)S(1)}, u32[]{:S(2)}, u32[]{:S(2)}) collective-permute-start(f32[1024,128]{1,0:T(8,128)S(1)} %get-tuple-element.38), channel_id=1, source_target_pairs={{1,2},{2,1},{3,4},{4,3},{5,6},{6,5},{7,8},{8,7},{9,10},{10,9},{11,... | collective-permute-start | bytes 1572872 | tf_op jit(solution)/shard_map/ppermute | solution.py:40
  112.4 11.8 %collective-permute-done.11.col_b = f32[1024,128]{1,0:T(8,128)S(1)} collective-permute-done((f32[1024,128]{1,0:T(8,128)S(1)}, f32[1024,128]{1,0:T(8,128)S(1)}, u32[]{:S(2)}, u32[]{:S(2)}) %collective-permute-start.11) | collective-permute-done | bytes 524320 | tf_op jit(solution)/shard_map/ppermute | solution.py:40
  124.2 0.6 shard_map.74
  124.8 10.0 %collective-permute-start.12 = (f32[2,128,256]{2,1,0:T(8,128)S(1)}, f32[2,128,256]{2,1,0:T(8,128)S(1)}, u32[]{:S(2)}, u32[]{:S(2)}) collective-permute-start(f32[2,128,256]{2,1,0:T(8,128)S(1)} %get-tuple-element.39), channel_id=1, source_target_pairs={{0,32},{32,0},{64,96},{96,64},{128,160},{160,128},{192,224},{224,1... | collective-permute-start | bytes 786440 | tf_op jit(solution)/shard_map/ppermute | solution.py:40
  134.8 1.9 %collective-permute-start.13 = (f32[2,128,256]{2,1,0:T(8,128)S(1)}, f32[2,128,256]{2,1,0:T(8,128)S(1)}, u32[]{:S(2)}, u32[]{:S(2)}) collective-permute-start(f32[2,128,256]{2,1,0:T(8,128)S(1)} %get-tuple-element.40), channel_id=1, source_target_pairs={{32,64},{64,32},{96,128},{128,96},{160,192},{192,160},{33,65},{65,... | collective-permute-start | bytes 786440 | tf_op jit(solution)/shard_map/ppermute | solution.py:40
  136.7 0.6 shard_map.73.total
  137.3 1.2 collective-permute-done.12.row_a
  138.5 4.2 %collective-permute-done.13.row_b = f32[2,128,256]{2,1,0:T(8,128)S(1)} collective-permute-done((f32[2,128,256]{2,1,0:T(8,128)S(1)}, f32[2,128,256]{2,1,0:T(8,128)S(1)}, u32[]{:S(2)}, u32[]{:S(2)}) %collective-permute-start.13) | collective-permute-done | bytes 262176 | tf_op jit(solution)/shard_map/ppermute | solution.py:40
  142.8 1.4 shard_map.75
  (24 shorter events, 0.8 us)
Async XLA Ops:
  0.0 0.7 copy-start.5
  0.9 1.0 copy-start
  2.6 7.8 %collective-permute-start = (f32[264,256]{1,0:T(8,128)S(1)}, f32[264,256]{1,0:T(8,128)S(1)}, u32[]{:S(2)}, u32[]{:S(2)}) collective-permute-start(f32[264,256]{1,0:T(8,128)S(1)} %get-tuple-element.23), channel_id=1, source_target_pairs={{0,32},{32,0},{64,96},{96,64},{128,160},{160,128},{192,224},{224,1... | collective-permute-start | bytes 811016 | tf_op jit(solution)/shard_map/ppermute | solution.py:40
  4.3 11.8 %collective-permute-start.1 = (f32[264,256]{1,0:T(8,128)S(1)}, f32[264,256]{1,0:T(8,128)S(1)}, u32[]{:S(2)}, u32[]{:S(2)}) collective-permute-start(f32[264,256]{1,0:T(8,128)S(1)} %get-tuple-element.24), channel_id=1, source_target_pairs={{32,64},{64,32},{96,128},{128,96},{160,192},{192,160},{33,65},{65,... | collective-permute-start | bytes 811016 | tf_op jit(solution)/shard_map/ppermute | solution.py:40
  17.5 8.0 %copy-start.2 = (bf16[1024,512]{1,0:T(8,128)(2,1)S(1)}, bf16[1024,512]{1,0:T(8,128)(2,1)}, u32[]{:S(2)}) copy-start(bf16[1024,512]{1,0:T(8,128)(2,1)} %constant.15.clone.tables) | copy-start | bytes 3145732
  17.5 8.0 %copy-start.1 = (f32[2,256,256]{2,1,0:T(8,128)S(1)}, f32[2,256,256]{2,1,0:T(8,128)}, u32[]{:S(2)}) copy-start(f32[2,256,256]{2,1,0:T(8,128)} %obj.7) | copy-start | bytes 1572868
  17.5 20.8 %collective-permute-start.3 = (f32[1032,128]{1,0:T(8,128)}, f32[1032,128]{1,0:T(8,128)S(1)}, u32[]{:S(2)}, u32[]{:S(2)}) collective-permute-start(f32[1032,128]{1,0:T(8,128)} %get-tuple-element.26), channel_id=1, source_target_pairs={{1,2},{2,1},{3,4},{4,3},{5,6},{6,5},{7,8},{8,7},{9,10},{10,9},{11,... | collective-permute-start | bytes 1585160 | tf_op jit(solution)/shard_map/ppermute | solution.py:40
  25.4 12.9 %collective-permute-start.2 = (f32[1032,128]{1,0:T(8,128)S(1)}, f32[1032,128]{1,0:T(8,128)}, u32[]{:S(2)}, u32[]{:S(2)}) collective-permute-start(f32[1032,128]{1,0:T(8,128)S(1)} %shard_map.67), channel_id=1, source_target_pairs={{0,1},{1,0},{2,3},{3,2},{4,5},{5,4},{6,7},{7,6},{8,9},{9,8},{10,11... | collective-permute-start | bytes 1585160 | tf_op jit(solution)/shard_map/ppermute | solution.py:40
  25.6 12.8 %copy-start.3 = (f32[2,256,256]{2,1,0:T(8,128)S(1)}, f32[2,256,256]{2,1,0:T(8,128)}, u32[]{:S(2)}) copy-start(f32[2,256,256]{2,1,0:T(8,128)} %probe.5) | copy-start | bytes 1572868
  25.6 12.7 %copy-start.4 = (bf16[1,1,6,256,256]{4,3,2,1,0:T(8,128)(2,1)S(1)}, bf16[1,1,6,256,256]{4,3,2,1,0:T(8,128)(2,1)}, u32[]{:S(2)}) copy-start(bf16[1,1,6,256,256]{4,3,2,1,0:T(8,128)(2,1)} %param.8) | copy-start | bytes 2359300
  44.8 7.3 %collective-permute-start.4 = (f32[1024,128]{1,0:T(8,128)S(1)}, f32[1024,128]{1,0:T(8,128)S(1)}, u32[]{:S(2)}, u32[]{:S(2)}) collective-permute-start(f32[1024,128]{1,0:T(8,128)S(1)} %get-tuple-element.28), channel_id=1, source_target_pairs={{0,1},{1,0},{2,3},{3,2},{4,5},{5,4},{6,7},{7,6},{8,9},{9,8},{10,11... | collective-permute-start | bytes 1572872 | tf_op jit(solution)/shard_map/ppermute | solution.py:40
  44.9 21.9 %collective-permute-start.5 = (f32[1024,128]{1,0:T(8,128)S(1)}, f32[1024,128]{1,0:T(8,128)S(1)}, u32[]{:S(2)}, u32[]{:S(2)}) collective-permute-start(f32[1024,128]{1,0:T(8,128)S(1)} %get-tuple-element.29), channel_id=1, source_target_pairs={{1,2},{2,1},{3,4},{4,3},{5,6},{6,5},{7,8},{8,7},{9,10},{10,9},{11,... | collective-permute-start | bytes 1572872 | tf_op jit(solution)/shard_map/ppermute | solution.py:40
  67.5 11.5 %collective-permute-start.6 = (f32[2,256,256]{2,1,0:T(8,128)S(1)}, f32[2,256,256]{2,1,0:T(8,128)S(1)}, u32[]{:S(2)}, u32[]{:S(2)}) collective-permute-start(f32[2,256,256]{2,1,0:T(8,128)S(1)} %get-tuple-element.30.sent_a), channel_id=1, source_target_pairs={{0,32},{32,0},{64,96},{96,64},{128,160},{160,128},{192,224},{224,1... | collective-permute-start | bytes 1572872 | tf_op jit(solution)/shard_map/ppermute | solution.py:40
  67.6 17.0 %collective-permute-start.7 = (f32[2,256,256]{2,1,0:T(8,128)S(1)}, f32[2,256,256]{2,1,0:T(8,128)S(1)}, u32[]{:S(2)}, u32[]{:S(2)}) collective-permute-start(f32[2,256,256]{2,1,0:T(8,128)S(1)} %get-tuple-element.31.sent_b), channel_id=1, source_target_pairs={{32,64},{64,32},{96,128},{128,96},{160,192},{192,160},{33,65},{65,... | collective-permute-start | bytes 1572872 | tf_op jit(solution)/shard_map/ppermute | solution.py:40
  85.4 5.8 %collective-permute-start.8 = (f32[1024,128]{1,0:T(8,128)S(1)}, f32[1024,128]{1,0:T(8,128)S(1)}, u32[]{:S(2)}, u32[]{:S(2)}) collective-permute-start(f32[1024,128]{1,0:T(8,128)S(1)} %get-tuple-element.34), channel_id=1, source_target_pairs={{0,1},{1,0},{2,3},{3,2},{4,5},{5,4},{6,7},{7,6},{8,9},{9,8},{10,11... | collective-permute-start | bytes 1572872 | tf_op jit(solution)/shard_map/ppermute | solution.py:40
  85.5 14.8 %collective-permute-start.9 = (f32[1024,128]{1,0:T(8,128)S(1)}, f32[1024,128]{1,0:T(8,128)S(1)}, u32[]{:S(2)}, u32[]{:S(2)}) collective-permute-start(f32[1024,128]{1,0:T(8,128)S(1)} %get-tuple-element.35), channel_id=1, source_target_pairs={{1,2},{2,1},{3,4},{4,3},{5,6},{6,5},{7,8},{8,7},{9,10},{10,9},{11,... | collective-permute-start | bytes 1572872 | tf_op jit(solution)/shard_map/ppermute | solution.py:40
  106.2 6.2 %collective-permute-start.10 = (f32[1024,128]{1,0:T(8,128)S(1)}, f32[1024,128]{1,0:T(8,128)S(1)}, u32[]{:S(2)}, u32[]{:S(2)}) collective-permute-start(f32[1024,128]{1,0:T(8,128)S(1)} %get-tuple-element.37), channel_id=1, source_target_pairs={{0,1},{1,0},{2,3},{3,2},{4,5},{5,4},{6,7},{7,6},{8,9},{9,8},{10,11... | collective-permute-start | bytes 1572872 | tf_op jit(solution)/shard_map/ppermute | solution.py:40
  106.3 17.8 %collective-permute-start.11 = (f32[1024,128]{1,0:T(8,128)S(1)}, f32[1024,128]{1,0:T(8,128)S(1)}, u32[]{:S(2)}, u32[]{:S(2)}) collective-permute-start(f32[1024,128]{1,0:T(8,128)S(1)} %get-tuple-element.38), channel_id=1, source_target_pairs={{1,2},{2,1},{3,4},{4,3},{5,6},{6,5},{7,8},{8,7},{9,10},{10,9},{11,... | collective-permute-start | bytes 1572872 | tf_op jit(solution)/shard_map/ppermute | solution.py:40
  124.8 13.7 %collective-permute-start.12 = (f32[2,128,256]{2,1,0:T(8,128)S(1)}, f32[2,128,256]{2,1,0:T(8,128)S(1)}, u32[]{:S(2)}, u32[]{:S(2)}) collective-permute-start(f32[2,128,256]{2,1,0:T(8,128)S(1)} %get-tuple-element.39), channel_id=1, source_target_pairs={{0,32},{32,0},{64,96},{96,64},{128,160},{160,128},{192,224},{224,1... | collective-permute-start | bytes 786440 | tf_op jit(solution)/shard_map/ppermute | solution.py:40
  134.8 8.0 %collective-permute-start.13 = (f32[2,128,256]{2,1,0:T(8,128)S(1)}, f32[2,128,256]{2,1,0:T(8,128)S(1)}, u32[]{:S(2)}, u32[]{:S(2)}) collective-permute-start(f32[2,128,256]{2,1,0:T(8,128)S(1)} %get-tuple-element.40), channel_id=1, source_target_pairs={{32,64},{64,32},{96,128},{128,96},{160,192},{192,160},{33,65},{65,... | collective-permute-start | bytes 786440 | tf_op jit(solution)/shard_map/ppermute | solution.py:40
